TPU v7x, 32 devices: a whole 2x2x4 slice. The times are simulated.
32 devices in a mesh: grp: 2 (over x), leaf: 8 (over z, y), sub: 2 (over core).
Axes of the slice: x: 2, y: 2, z: 4, core: 2. Of those that a mesh axis runs over, the one named last changes fastest.
Arguments:
- right_side: float32 [512, 2048], P(('grp', 'leaf', 'sub')), parts along dimension 0, may hold values from -24 to 24, as said below
- first_guess: float32 [512, 2048], P(('grp', 'leaf', 'sub')), parts along dimension 0, may hold values from -3 to 3
- couple: bfloat16 [512, 64, 384], P(('grp', 'leaf', 'sub')), parts along dimension 0, may hold values from -0.75 to 0.75
- send_lists: int32 [32, 2, 4], P(('grp', 'leaf', 'sub')), parts along dimension 0, may hold values from -1 to 15, as said below
- neighbours: int32 [512, 6], P(('grp', 'leaf', 'sub')), parts along dimension 0, may hold values from -1 to 23, as said below
Outputs:
- solution: float32 [512, 2048], P(('grp', 'leaf', 'sub')), parts along dimension 0
- residual: float32 [512, 2048], P(('grp', 'leaf', 'sub')), parts along dimension 0
There are 2 independent parts, one for each index of `grp`. A program takes and returns all parts, laid end to end along the dimension named above; each array names one. Nothing has to cross between parts.
Inputs may be any that keep to these rules, and one draw needn't show every extreme that they name: `right_side`: rows rise in scale along the element order. `send_lists`: for device d of a part and direction 0 (toward device d + 1) or 1 (toward device d - 1): distinct local element indices in the live slots, which come first, and -1 after them. The first device sends nothing in direction 1, the last nothing in direction 0; some device fills all 4 slots in direction 0 and the device after it all 4 in direction 1. `neighbours`: positions below 16 are the device's own elements, 16 + s the live slot s received from the previous device, 20 + s the live slot s received from the next device; -1 marks a face on the band's boundary.
All inputs are finite; a program needn't handle non-finite values.
Results may differ from a plain program's by a relative error of at most 0.034.
Values may be sent and summed in bfloat16 or wider, within the bound.
No kernel may reach another device: no remote copies, remote signals or barrier semaphores. Data moves between devices by JAX's collectives and lax.ppermute only.
A program may use at most 64 MiB of HBM per device.

v0:
```python
import jax
import jax.numpy as jnp
from jax import lax
from jax.experimental import pallas as pl
from jax.experimental.pallas import tpu as pltpu
from jax.sharding import PartitionSpec as P

DOF = 64
FACES = 6
RHS = 32
SSTEP = 3
CYCLES = 4
MERGED = 2
POWERS = SSTEP * MERGED
GROWTH = 8.0
PACK = 4
TRUST_PIVOT = 1e3
TRUST_RESIDUAL = 5e4
TRUST_ROUNDING = 64.0
META = 16
LANES = 128
AXES = ("leaf", "sub")
F32 = jnp.float32
BF16 = jnp.bfloat16

VMEM = pl.BlockSpec(memory_space=pltpu.VMEM)
ANY = pl.BlockSpec(memory_space=pl.ANY)
PARAMS = pltpu.CompilerParams(vmem_limit_bytes=16 * 1024 * 1024)


def pack(message, blocks):
    for g in range(len(blocks) // PACK):
        message[g] = jnp.concatenate(blocks[PACK * g : PACK * g + PACK], axis=1).astype(BF16)


def unpack(ext, start, message):
    for g in range(message.shape[0]):
        row = message[g]
        for j in range(PACK):
            ext[start + PACK * g + j] = row[:, RHS * j : RHS * j + RHS]


def coupled(table, e, rows, ext):
    gathered = jnp.concatenate([ext[table[e, f]] for f in range(FACES)], axis=0)
    return jnp.dot(rows, gathered, preferred_element_type=F32)


def split(value):
    high = value.astype(BF16)
    return high, (value - high.astype(F32)).astype(BF16)


def listed(lists, side, ext):
    slots = lists.shape[1] // 2
    return [ext[lists[0, side * slots + s]].astype(F32) for s in range(slots)]


def start_kernel(lists, x, to_chip, to_link, ext):
    count = x.shape[0]
    ext[:count] = x[...].astype(BF16)
    ext[count] = jnp.zeros(ext.shape[1:], BF16)
    pack(to_chip, listed(lists, 0, ext))
    pack(to_link, listed(lists, 1, ext))


def rows_kernel(lists, codes, couple, after, to_chip, to_link, kept):
    kept[...] = couple[...]
    count, slots = couple.shape[0], to_chip.shape[0]
    lanes = lax.broadcasted_iota(jnp.int32, (1, LANES), 1)
    for side, message in ((0, to_chip), (1, to_link)):
        for s in range(slots):
            place = lists[0, side * slots + s]
            e = jnp.minimum(place, count - 1)
            message[s, :DOF] = couple[e]
            meta = jnp.where(place < count, codes[pl.ds(e, 1), :], count + 2 * slots)
            meta = jnp.where(lanes == FACES, place, meta).astype(F32)
            message[s, DOF:] = jnp.zeros((META, couple.shape[2]), BF16)
            message[s, DOF:, :LANES] = jnp.broadcast_to(meta, (META, LANES)).astype(BF16)


def tables_kernel(lists, codes, chip_rows, link_rows, chip_table, link_table):
    count, slots = codes.shape[0], chip_rows.shape[0]
    reach = count + slots
    chip_base, link_base, empty = count, count + slots, 2 * reach
    sides = ((0, chip_table, chip_rows, link_base, chip_base), (1, link_table, link_rows, chip_base, link_base))
    for side, table, rows, known_base, far_base in sides:
        meta = [rows[s, DOF:, :LANES].astype(F32)[:1].astype(jnp.int32) for s in range(slots)]
        far = [value[:, FACES : FACES + 1] for value in meta]
        near = [lists[:, side * slots + s : side * slots + s + 1] for s in range(slots)]

        def place(at, own, known, listed_at, listed_own):
            found = jnp.where((at >= known_base) & (at < known_base + slots), at - known_base + known, empty)
            for s in range(slots):
                target = jnp.where(listed_at[s] < count, listed_at[s] + listed_own, empty)
                found = jnp.where(at == far_base + s, target, found)
            return jnp.where(at < count, at + own, found)

        table[:count] = place(codes[...], 0, count, far, reach)
        for s in range(slots):
            table[count + s : count + s + 1] = place(meta[s], reach, reach + count, near, 0)


def residual_kernel(lists, positions, couple, from_chip, from_link, b, x, r, own, to_chip, ext):
    count = x.shape[0]
    ext[:count] = x[...].astype(BF16)
    unpack(ext, count, from_chip)
    unpack(ext, count + PACK * from_chip.shape[0], from_link)
    ext[ext.shape[0] - 1] = jnp.zeros(ext.shape[1:], BF16)
    for e in range(count):
        r[e] = b[e] - x[e] + coupled(positions, e, couple[e], ext)
    pack(own, [r[e] for e in range(count)])
    ext[:count] = r[...].astype(BF16)
    ext[count] = jnp.zeros(ext.shape[1:], BF16)
    pack(to_chip, listed(lists, 0, ext))


def extend(ext, mine, theirs):
    unpack(ext, 0, mine)
    unpack(ext, PACK * mine.shape[0], theirs)
    ext[ext.shape[0] - 1] = jnp.zeros(ext.shape[1:], BF16)


def power_kernel(table, couple, extra, mine, theirs, power, message, ext):
    count, slots = couple.shape[0], extra.shape[0]
    extend(ext, mine, theirs)
    values = []
    for e in range(count + slots):
        rows = couple[e] if e < count else extra[e - count, :DOF]
        values.append(coupled(table, e, rows, ext) * (1.0 / GROWTH))
        if e < count:
            power[e] = values[e]
    pack(message, values)


def inner_products(columns):
    stacked = jnp.concatenate(columns, axis=1)
    high, low = split(stacked)
    width = stacked.shape[1]
    sums = lax.dot_general(
        high, jnp.concatenate([high, low], axis=1), (((0,), (0,)), ((), ())), preferred_element_type=F32
    )
    cross = sums[:, width:]
    return sums[:, :width] + cross + cross.T


def gram_kernel(table, couple, mine, theirs, *refs):
    fields, (last, left, right, ext) = refs[:POWERS], refs[POWERS:]
    count = couple.shape[0]
    rows = count * DOF
    extend(ext, mine, theirs)
    for e in range(count):
        last[e] = coupled(table, e, couple[e], ext) * (1.0 / GROWTH)
    fields = [field[...].reshape(rows, RHS) for field in (*fields, last)]
    empty = jnp.zeros((rows, RHS), F32)
    gram = inner_products([fields[k] - GROWTH * fields[k + 1] for k in range(POWERS)] + [fields[0], empty])
    norms = jnp.concatenate(
        [jnp.sum(field * field, axis=0, keepdims=True) for field in fields] + [jnp.zeros((1, RHS), F32)], axis=0
    )
    half = gram.shape[0] // 2
    below = jnp.concatenate([jnp.zeros((RHS, half), F32), gram[half:, half:][: half - RHS]], axis=0)
    left[...] = jnp.where(block_of(half, 0) > block_of(half, 1), below, gram[:half, :half])
    right[...] = gram[:half, half:]
    right[: POWERS + 2, half - RHS :] = norms


def block_of(size, dimension):
    return lax.broadcasted_iota(jnp.int32, (size, size), dimension) // RHS


def unpack_gram(left, right):
    half = left.shape[0]
    low_left, right = left[...], right[...]
    row, column = block_of(half, 0), block_of(half, 1)
    by_lane = right[: POWERS + 2].T
    norms = jnp.concatenate([by_lane[half - RHS :, j : j + 1] for j in range(POWERS + 2)], axis=0)
    right = jnp.where(column < 3, right, 0.0)
    first = jnp.where(row <= column, low_left, low_left.T)
    moved = jnp.concatenate([low_left[RHS:], jnp.zeros((RHS, half), F32)], axis=0)
    last = jnp.where(row >= column, moved, moved.T)
    last = jnp.where((row < 3) & (column < 3), last, 0.0)
    gram = jnp.concatenate(
        [jnp.concatenate([first, right], axis=1), jnp.concatenate([right.T, last], axis=1)], axis=0
    )
    return gram, norms


def eliminate(gram):
    count = SSTEP * RHS // 8
    groups = [gram[8 * g : 8 * g + 8, :] for g in range(count)]
    shape = groups[0].shape
    row_ids = lax.broadcasted_iota(jnp.int32, shape, 0)
    lane_ids = lax.broadcasted_iota(jnp.int32, (1, shape[1]), 1)
    pivots = jnp.zeros((1, shape[1]), F32)
    for home in range(count):
        columns = [
            [jnp.broadcast_to(group[:, 8 * home + m : 8 * home + m + 1], shape) for m in range(8)]
            for group in groups
        ]
        own = list(columns[home])
        panel = groups[home]
        for m in range(8):
            pivot = own[m][m : m + 1, :]
            pivots = jnp.where(lane_ids == 8 * home + m, pivot, pivots)
            inverse = 1.0 / pivot
            scaled = panel[m : m + 1, :] * inverse
            panel = jnp.where(row_ids == m, scaled, panel - own[m] * scaled)
            for k in range(m + 1, 8):
                scaled = own[k][m : m + 1, :] * inverse
                own[k] = jnp.where(row_ids == m, scaled, own[k] - own[m] * scaled)
        for g in range(count):
            if g == home:
                groups[g] = panel
                continue
            for m in range(8):
                groups[g] = groups[g] - columns[g][m] * panel[m : m + 1, :]
    return jnp.concatenate(groups, axis=0)[:, SSTEP * RHS :], pivots


def exact(a, b, contract=(1, 0)):
    return lax.dot_general(
        a,
        b,
        (((contract[0],), (contract[1],)), ((), ())),
        precision=lax.Precision.HIGHEST,
        preferred_element_type=F32,
    )


def below(value, size, blocks):
    parts = [jnp.zeros((RHS * blocks, value.shape[1]), F32)] if blocks else []
    rest = size - RHS * blocks - value.shape[0]
    parts.append(value)
    if rest:
        parts.append(jnp.zeros((rest, value.shape[1]), F32))
    return jnp.concatenate(parts, axis=0)


def mixing(left, right):
    gram, norms = unpack_gram(left, right)
    size = gram.shape[0]
    right = RHS * POWERS
    square = SSTEP * RHS
    eye = (
        lax.broadcasted_iota(jnp.int32, (RHS, RHS), 0) == lax.broadcasted_iota(jnp.int32, (RHS, RHS), 1)
    ).astype(F32)

    first, _ = eliminate(jnp.concatenate([gram[:square, :square], gram[:square, right : right + RHS]], axis=1))
    first_left = GROWTH * below(first, square + RHS, 1) - below(first, square + RHS, 0) + below(eye, square + RHS, 0)
    moved = jnp.concatenate([below(first_left, size, k) for k in range(SSTEP)], axis=1)
    images = jnp.concatenate([moved, below(eye, size, POWERS) - below(first, size, 0)], axis=1)
    projected = exact(images, exact(gram, images), (0, 0))
    second, pivots = eliminate(projected)
    change = exact(moved, second)
    sol = below(first, size, 0) + change
    res = below(first_left, size, 0) - change + GROWTH * below(change[: size - RHS], size, 1)
    is_diagonal = lax.broadcasted_iota(jnp.int32, gram.shape, 0) == lax.broadcasted_iota(jnp.int32, gram.shape, 1)
    scale = jnp.sqrt(jnp.sum(jnp.where(is_diagonal, gram, 0.0), axis=1, keepdims=True))
    reach = jnp.sum(jnp.abs(images) * scale, axis=0, keepdims=True)
    reach = reach * reach
    corner = jnp.where(eye > 0, projected[square:, square:], 0.0)
    left_over = jnp.sum(corner, axis=0, keepdims=True) - jnp.sum(
        projected[:square, square:] * second, axis=0, keepdims=True
    )
    power = (lax.broadcasted_iota(jnp.int32, (size, 1), 0) // RHS).astype(F32)
    rounding = jnp.sum(res * res * (norms * power), axis=0, keepdims=True)
    doubts = [
        jnp.where(reach[:, :square] <= TRUST_PIVOT * pivots[:, :square], 0.0, 1.0),
        jnp.where(reach[:, square:] <= TRUST_RESIDUAL * left_over, 0.0, 1.0),
        jnp.where(jnp.sum(rounding, axis=1, keepdims=True) <= TRUST_ROUNDING * jnp.sum(left_over, axis=1, keepdims=True), 0.0, 1.0),
    ]
    doubt = sum(jnp.sum(value, axis=1, keepdims=True) for value in doubts)
    return jnp.concatenate([sol, res], axis=1), doubt


def combined(mix, fields):
    rows = fields[0].shape[0] * DOF
    stacked = jnp.concatenate([field[...].reshape(rows, RHS) for field in fields], axis=1)
    rest = mix.shape[0] - stacked.shape[1]
    if rest:
        stacked = jnp.concatenate([stacked, jnp.zeros((rows, rest), F32)], axis=1)
    mix_high, mix_low = split(mix)
    high, low = split(stacked)
    out = jnp.dot(high, mix_high, preferred_element_type=F32)
    out += jnp.dot(high, mix_low, preferred_element_type=F32)
    out += jnp.dot(low, mix_high, preferred_element_type=F32)
    shape = fields[0].shape
    return out[:, :RHS].reshape(shape), out[:, RHS:].reshape(shape)


def update_kernel(lists, left, right, *refs):
    fields, (x, new_x, r, own, to_chip, doubt, ext) = refs[: POWERS + 1], refs[POWERS + 1 :]
    count = x.shape[0]
    mix, found = mixing(left, right)
    doubt[...] = jnp.broadcast_to(found, doubt.shape)
    step, r[...] = combined(mix, fields)
    new_x[...] = x[...] + step
    pack(own, [r[e] for e in range(count)])
    ext[:count] = r[...].astype(BF16)
    ext[count] = jnp.zeros(ext.shape[1:], BF16)
    pack(to_chip, listed(lists, 0, ext))


def finish_kernel(left, right, *refs):
    fields, (x, earlier, first_r, first_x, new_x, r, doubt) = refs[: POWERS + 1], refs[POWERS + 1 :]
    mix, found = mixing(left, right)
    found = found + earlier[:1, :1]
    doubt[...] = jnp.broadcast_to(found, doubt.shape)
    step, last = combined(mix, fields)
    trusted = (found == 0).reshape(1, 1, 1)
    new_x[...] = jnp.where(trusted, x[...] + step, first_x[...]).reshape(new_x.shape)
    r[...] = jnp.where(trusted, last, first_r[...]).reshape(r.shape)


def single_power_kernel(codes, couple, value, from_chip, from_link, power, ext):
    count = value.shape[0]
    ext[:count] = value[...].astype(BF16)
    unpack(ext, count, from_chip)
    unpack(ext, count + PACK * from_chip.shape[0], from_link)
    ext[ext.shape[0] - 1] = jnp.zeros(ext.shape[1:], BF16)
    for e in range(count):
        power[e] = coupled(codes, e, couple[e], ext)


def single_gram_kernel(*refs):
    fields, gram = refs[:-1], refs[-1]
    fields = [field[...].reshape(-1, RHS) for field in fields]
    gram[...] = inner_products([fields[k] - fields[k + 1] for k in range(SSTEP)] + [fields[0]])


def single_update_kernel(gram, *refs):
    fields, (x, new_x, r) = refs[: SSTEP + 1], refs[SSTEP + 1 :]
    first, _ = eliminate(gram)
    size = gram.shape[0]
    eye = (
        lax.broadcasted_iota(jnp.int32, (RHS, RHS), 0) == lax.broadcasted_iota(jnp.int32, (RHS, RHS), 1)
    ).astype(F32)
    res = below(eye, size, 0) - below(first, size, 0) + below(first, size, 1)
    step, r[...] = combined(jnp.concatenate([below(first, size, 0), res], axis=1), fields)
    new_x[...] = x[...] + step


def shards(right_side, first_guess, couple, send_lists, neighbours):
    count = right_side.shape[0]
    slots = send_lists.shape[2]
    devices = lax.axis_size(AXES)
    assert lax.axis_size("sub") == 2 and slots % PACK == 0 and count % PACK == 0
    second = lax.axis_index("sub") == 1

    def shape(dtype, *sizes):
        return jax.ShapeDtypeStruct(sizes, dtype)

    field = shape(F32, count, DOF, RHS)
    slot_message = shape(BF16, slots // PACK, DOF, PACK * RHS)
    own_message = shape(BF16, count // PACK, DOF, PACK * RHS)
    message = shape(BF16, (count + slots) // PACK, DOF, PACK * RHS)
    rows_shape = shape(BF16, count, DOF, FACES * DOF)
    row_message = shape(BF16, slots, DOF + META, FACES * DOF)
    half_gram = shape(F32, (POWERS + 2) * RHS // 2, (POWERS + 2) * RHS // 2)
    doubt_shape = shape(F32, 8, LANES)
    table_shape = shape(jnp.int32, count + slots, LANES)

    def call(kernel, outs, specs, name, blocks=0):
        return pl.pallas_call(
            kernel,
            out_shape=outs,
            in_specs=specs,
            out_specs=[VMEM] * len(outs),
            scratch_shapes=[pltpu.VMEM((blocks, DOF, RHS), BF16)] if blocks else [],
            compiler_params=PARAMS,
            name=name,
        )

    nowhere = count + 2 * slots
    own_lists = jnp.where(send_lists[0] < 0, count, send_lists[0]).astype(jnp.int32)
    lists = jnp.where(second, own_lists[::-1], own_lists).reshape(1, 2 * slots)
    swapped = jnp.where(neighbours < count + slots, neighbours + slots, neighbours - slots)
    codes = jnp.where(second | (neighbours < count), neighbours, swapped)
    codes = jnp.where(neighbours < 0, nowhere, codes).astype(jnp.int32)
    codes = jnp.pad(codes, ((0, 0), (0, LANES - FACES)))

    chip_pairs = [(d, d ^ 1) for d in range(devices)]
    link_pairs = [(d, d + 1 if d % 2 else d - 1) for d in range(devices)]
    link_pairs = [(s, t) for s, t in link_pairs if 0 <= t < devices]

    def chip(value):
        return lax.ppermute(value, AXES, chip_pairs)

    def link(value):
        return lax.ppermute(value, AXES, link_pairs)

    def total(left, right):
        value = jnp.where(second, right, left) + chip(jnp.where(second, left, right))
        step = 2
        while step < devices:
            value = value + lax.ppermute(value, AXES, [(d, d ^ step) for d in range(devices)])
            step *= 2
        other = chip(value)
        return jnp.where(second, other, value), jnp.where(second, value, other)

    start = call(start_kernel, [slot_message] * 2, [VMEM, VMEM], "start", count + 1)
    send_rows = call(rows_kernel, [row_message, row_message, rows_shape], [VMEM, VMEM, VMEM, ANY], "rows")
    tables = call(tables_kernel, [table_shape] * 2, [VMEM] * 4, "tables")
    first = call(
        residual_kernel,
        [field, own_message, slot_message],
        [VMEM] * 7,
        "first_residual",
        nowhere + 1,
    )
    reach = 2 * (count + slots) + 1
    power = call(power_kernel, [field, message], [VMEM] * 5, "power", reach)
    gram = call(
        gram_kernel, [field, half_gram, half_gram], [VMEM] * (4 + POWERS), "power_and_gram", reach
    )
    update = call(
        update_kernel,
        [field, field, own_message, slot_message, doubt_shape],
        [VMEM] * (POWERS + 5),
        "solve_update",
        count + 1,
    )
    flat = shape(F32, *right_side.shape)
    finish = call(finish_kernel, [flat, flat, doubt_shape], [VMEM] * (POWERS + 7), "solve_finish")

    b = right_side.reshape(count, DOF, RHS)
    x = first_x = first_guess.reshape(count, DOF, RHS)
    assert CYCLES == 2 * MERGED
    to_chip, to_link = start(lists, x)
    from_link = link(to_link)
    from_chip = chip(to_chip)
    chip_rows, link_rows, kept = send_rows(lists, codes, couple, from_chip)
    link_rows = link(link_rows)
    chip_rows = chip(chip_rows)
    r, own, to_chip = first(lists, codes, kept, from_chip, from_link, b, x)
    chip_table, link_table = tables(lists, codes, chip_rows, link_rows)
    for group in range(CYCLES // MERGED):
        mine = jnp.concatenate([own, chip(to_chip)], axis=0)
        fields = [r]
        for k in range(POWERS - 1):
            if k % 2 == 0:
                value, mine = power(link_table, kept, link_rows, mine, link(mine))
            else:
                value, mine = power(chip_table, kept, chip_rows, mine, chip(mine))
            fields.append(value)
        value, left, right = gram(chip_table, kept, mine, chip(mine), *fields)
        fields.append(value)
        sums = total(left, right)
        if group == 0:
            first_r = r
        if group + 1 < CYCLES // MERGED:
            x, r, own, to_chip, doubt = update(lists, *sums, *fields, x)
        else:
            x, r, doubt = finish(*sums, *fields, x, doubt, first_r, first_x)

    single_power = call(single_power_kernel, [field], [VMEM] * 5, "single_power", nowhere + 1)
    single_gram = call(single_gram_kernel, [shape(F32, LANES, LANES)], [VMEM] * (SSTEP + 1), "single_gram")
    single_update = call(single_update_kernel, [field, field], [VMEM] * (SSTEP + 3), "single_update")

    def slots_of(value):
        to_chip, to_link = start(lists, value)
        return chip(to_chip), link(to_link)

    def one_cycle(_, state):
        x, r = (value.reshape(count, DOF, RHS) for value in state)
        fields = [r]
        for _ in range(SSTEP):
            fields += single_power(codes, couple, fields[-1], *slots_of(fields[-1]))
        (value,) = single_gram(*fields)
        step = 1
        while step < devices:
            value = value + lax.ppermute(value, AXES, [(d, d ^ step) for d in range(devices)])
            step *= 2
        x, r = single_update(value, *fields, x)
        return x.reshape(right_side.shape), r.reshape(right_side.shape)

    return lax.fori_loop(0, jnp.where(doubt[0, 0] == 0, 0, CYCLES), one_cycle, (x, r))


def solution(mesh):
    rows = ("grp", "leaf", "sub")
    placed = (P(rows, None), P(rows, None), P(rows, None, None), P(rows, None, None), P(rows, None))
    return jax.shard_map(
        shards,
        mesh=mesh,
        in_specs=placed,
        out_specs=(P(rows, None), P(rows, None)),
        check_vma=False,
    )
```

profile of v0, /device:TPU:0, one launch (start us, length us, event | category | flops | bytes accessed | tf_op | source)
XLA Modules:
  0.0 131.3 jit_solution(6495592449924725704)
XLA Ops:
  4.2 1.4 %rows.1 = (bf16[4,80,384]{2,1,0:T(8,128)(2,1)S(1)}, bf16[4,80,384]{2,1,0:T(8,128)(2,1)S(1)}, bf16[16,64,384]{2,1,0:T(8,128)(2,1)S(1)}) custom-call(s32[1,8]{1,0:T(1,128)S(1)} %reshape.30.lists, s32[16,128]{1,0:T(8,128)S(1)} %pad.4.codes.positions, bf16[16,64,384]{2,1,0:T(8,128)(2,1)} %couple.1, bf16[1,64,128]{2,1,0:T(8,128)(2,1)S(1)} %collective-permute-done.10.after.from_chip), custom_call_target="tpu_custom_call" | custom-call | tf_op jit(solution)/shard_map/rows/pallas_call | solution.py:431
  6.3 4.0 %collective-permute-start.14 = (bf16[1,64,128]{2,1,0:T(8,128)(2,1)S(1)}, bf16[1,64,128]{2,1,0:T(8,128)(2,1)S(1)}, u32[]{:S(2)}, u32[]{:S(2)}) collective-permute-start(bf16[1,64,128]{2,1,0:T(8,128)(2,1)S(1)} %get-tuple-element.101), channel_id=1, source_target_pairs={{0,1},{1,0},{2,3},{3,2},{4,5},{5,4},{6,7},{7,6},{8,9},{9,8},{10,11... | collective-permute-start | bytes 49160 | tf_op jit(solution)/shard_map/ppermute | solution.py:386
  12.8 10.7 %collective-permute-start.16 = (bf16[5,64,128]{2,1,0:T(8,128)(2,1)S(1)}, bf16[5,64,128]{2,1,0:T(8,128)(2,1)S(1)}, u32[]{:S(2)}, u32[]{:S(2)}) collective-permute-start(bf16[5,64,128]{2,1,0:T(8,128)(2,1)S(1)} %get-tuple-element.102.mine), channel_id=1, source_target_pairs={{0,1},{1,0},{2,3},{3,2},{4,5},{5,4},{6,7},{7,6},{8,9},{9,8},{10,11... | collective-permute-start | bytes 245768 | tf_op jit(solution)/shard_map/ppermute | solution.py:386
  27.0 6.2 %collective-permute-start.18 = (bf16[5,64,128]{2,1,0:T(8,128)(2,1)S(1)}, bf16[5,64,128]{2,1,0:T(8,128)(2,1)S(1)}, u32[]{:S(2)}, u32[]{:S(2)}) collective-permute-start(bf16[5,64,128]{2,1,0:T(8,128)(2,1)S(1)} %get-tuple-element.104.mine), channel_id=1, source_target_pairs={{0,1},{1,0},{2,3},{3,2},{4,5},{5,4},{6,7},{7,6},{8,9},{9,8},{10,11... | collective-permute-start | bytes 245768 | tf_op jit(solution)/shard_map/ppermute | solution.py:386
  36.9 6.0 %collective-permute-start.20 = (bf16[5,64,128]{2,1,0:T(8,128)(2,1)S(1)}, bf16[5,64,128]{2,1,0:T(8,128)(2,1)S(1)}, u32[]{:S(2)}, u32[]{:S(2)}) collective-permute-start(bf16[5,64,128]{2,1,0:T(8,128)(2,1)S(1)} %get-tuple-element.106.mine), channel_id=1, source_target_pairs={{0,1},{1,0},{2,3},{3,2},{4,5},{5,4},{6,7},{7,6},{8,9},{9,8},{10,11... | collective-permute-start | bytes 245768 | tf_op jit(solution)/shard_map/ppermute | solution.py:386
  43.8 2.0 %power_and_gram.2 = (f32[16,64,32]{2,1,0:T(8,128)S(1)}, f32[128,128]{1,0:T(8,128)S(1)}, f32[128,128]{1,0:T(8,128)S(1)}) custom-call(s32[20,128]{1,0:T(8,128)S(1)} %get-tuple-element.96.table, bf16[16,64,384]{2,1,0:T(8,128)(2,1)S(1)} %get-tuple-element.97.couple, bf16[5,64,128]{2,1,0:T(8,128)(2,1)S(1)} %get-tuple-element.106.mine, ...), custom_call_target="tpu_custom_call" | custom-call | tf_op jit(solution)/shard_map/power_and_gram/pallas_call | solution.py:445
  47.1 2.9 %collective-permute-start.22 = (f32[128,128]{1,0:T(8,128)S(1)}, f32[128,128]{1,0:T(8,128)S(1)}, u32[]{:S(2)}, u32[]{:S(2)}) collective-permute-start(f32[128,128]{1,0:T(8,128)S(1)} %select_add_fusion.1), channel_id=1, source_target_pairs={{0,2},{1,3},{2,0},{3,1},{4,6},{5,7},{6,4},{7,5},{8,10},{9,11},{10,... | collective-permute-start | bytes 196616 | tf_op jit(solution)/shard_map/ppermute | solution.py:395
  50.1 2.6 %collective-permute-done.22 = f32[128,128]{1,0:T(8,128)S(1)} collective-permute-done((f32[128,128]{1,0:T(8,128)S(1)}, f32[128,128]{1,0:T(8,128)S(1)}, u32[]{:S(2)}, u32[]{:S(2)}) %collective-permute-start.22) | collective-permute-done | bytes 65568 | tf_op jit(solution)/shard_map/ppermute | solution.py:395
  52.7 1.9 %collective-permute-start.23 = (f32[128,128]{1,0:T(8,128)S(1)}, f32[128,128]{1,0:T(8,128)S(1)}, u32[]{:S(2)}, u32[]{:S(2)}) collective-permute-start(f32[128,128]{1,0:T(8,128)S(1)} %add.47), channel_id=1, source_target_pairs={{0,4},{1,5},{2,6},{3,7},{4,0},{5,1},{6,2},{7,3},{8,12},{9,13},{10,... | collective-permute-start | bytes 196616 | tf_op jit(solution)/shard_map/ppermute | solution.py:395
  54.5 2.5 %collective-permute-done.23 = f32[128,128]{1,0:T(8,128)S(1)} collective-permute-done((f32[128,128]{1,0:T(8,128)S(1)}, f32[128,128]{1,0:T(8,128)S(1)}, u32[]{:S(2)}, u32[]{:S(2)}) %collective-permute-start.23) | collective-permute-done | bytes 65568 | tf_op jit(solution)/shard_map/ppermute | solution.py:395
  57.0 2.9 %collective-permute-start.24 = (f32[128,128]{1,0:T(8,128)S(1)}, f32[128,128]{1,0:T(8,128)S(1)}, u32[]{:S(2)}, u32[]{:S(2)}) collective-permute-start(f32[128,128]{1,0:T(8,128)S(1)} %add.48), channel_id=1, source_target_pairs={{0,8},{1,9},{2,10},{3,11},{4,12},{5,13},{6,14},{7,15},{8,0},{9,1},... | collective-permute-start | bytes 196616 | tf_op jit(solution)/shard_map/ppermute | solution.py:395
  59.9 2.4 %collective-permute-done.24 = f32[128,128]{1,0:T(8,128)S(1)} collective-permute-done((f32[128,128]{1,0:T(8,128)S(1)}, f32[128,128]{1,0:T(8,128)S(1)}, u32[]{:S(2)}, u32[]{:S(2)}) %collective-permute-start.24) | collective-permute-done | bytes 65568 | tf_op jit(solution)/shard_map/ppermute | solution.py:395
  63.6 8.4 %solve_update.1 = (f32[16,64,32]{2,1,0:T(8,128)S(1)}, f32[16,64,32]{2,1,0:T(8,128)S(1)}, bf16[4,64,128]{2,1,0:T(8,128)(2,1)S(1)}, bf16[1,64,128]{2,1,0:T(8,128)(2,1)S(1)}, f32[8,128]{1,0:T(8,128)S(1)}) custom-call(s32[1,8]{1,0:T(1,128)S(1)} %reshape.30.lists, f32[128,128]{1,0:T(8,128)S(1)} %get-tuple-element.156.left, ...), custom_call_target="tpu_custom_call" | custom-call | tf_op jit(solution)/shard_map/solve_update/pallas_call | solution.py:451
  74.8 5.3 %collective-permute-start.28 = (bf16[5,64,128]{2,1,0:T(8,128)(2,1)S(1)}, bf16[5,64,128]{2,1,0:T(8,128)(2,1)S(1)}, u32[]{:S(2)}, u32[]{:S(2)}) collective-permute-start(bf16[5,64,128]{2,1,0:T(8,128)(2,1)S(1)} %get-tuple-element.118.mine), channel_id=1, source_target_pairs={{0,1},{1,0},{2,3},{3,2},{4,5},{5,4},{6,7},{7,6},{8,9},{9,8},{10,11... | collective-permute-start | bytes 245768 | tf_op jit(solution)/shard_map/ppermute | solution.py:386
  83.8 5.9 %collective-permute-start.30 = (bf16[5,64,128]{2,1,0:T(8,128)(2,1)S(1)}, bf16[5,64,128]{2,1,0:T(8,128)(2,1)S(1)}, u32[]{:S(2)}, u32[]{:S(2)}) collective-permute-start(bf16[5,64,128]{2,1,0:T(8,128)(2,1)S(1)} %get-tuple-element.120.mine), channel_id=1, source_target_pairs={{0,1},{1,0},{2,3},{3,2},{4,5},{5,4},{6,7},{7,6},{8,9},{9,8},{10,11... | collective-permute-start | bytes 245768 | tf_op jit(solution)/shard_map/ppermute | solution.py:386
  93.1 6.4 %collective-permute-start.32 = (bf16[5,64,128]{2,1,0:T(8,128)(2,1)S(1)}, bf16[5,64,128]{2,1,0:T(8,128)(2,1)S(1)}, u32[]{:S(2)}, u32[]{:S(2)}) collective-permute-start(bf16[5,64,128]{2,1,0:T(8,128)(2,1)S(1)} %get-tuple-element.122.mine), channel_id=1, source_target_pairs={{0,1},{1,0},{2,3},{3,2},{4,5},{5,4},{6,7},{7,6},{8,9},{9,8},{10,11... | collective-permute-start | bytes 245768 | tf_op jit(solution)/shard_map/ppermute | solution.py:386
  100.4 2.0 %power_and_gram.3 = (f32[16,64,32]{2,1,0:T(8,128)S(1)}, f32[128,128]{1,0:T(8,128)S(1)}, f32[128,128]{1,0:T(8,128)S(1)}) custom-call(s32[20,128]{1,0:T(8,128)S(1)} %get-tuple-element.96.table, bf16[16,64,384]{2,1,0:T(8,128)(2,1)S(1)} %get-tuple-element.97.couple, bf16[5,64,128]{2,1,0:T(8,128)(2,1)S(1)} %get-tuple-element.122.mine, ...), custom_call_target="tpu_custom_call" | custom-call | tf_op jit(solution)/shard_map/power_and_gram/pallas_call | solution.py:445
  103.8 2.9 %collective-permute-start.34 = (f32[128,128]{1,0:T(8,128)S(1)}, f32[128,128]{1,0:T(8,128)S(1)}, u32[]{:S(2)}, u32[]{:S(2)}) collective-permute-start(f32[128,128]{1,0:T(8,128)S(1)} %select_add_fusion), channel_id=1, source_target_pairs={{0,2},{1,3},{2,0},{3,1},{4,6},{5,7},{6,4},{7,5},{8,10},{9,11},{10,... | collective-permute-start | bytes 196616 | tf_op jit(solution)/shard_map/ppermute | solution.py:395
  106.7 2.6 %collective-permute-done.34 = f32[128,128]{1,0:T(8,128)S(1)} collective-permute-done((f32[128,128]{1,0:T(8,128)S(1)}, f32[128,128]{1,0:T(8,128)S(1)}, u32[]{:S(2)}, u32[]{:S(2)}) %collective-permute-start.34) | collective-permute-done | bytes 65568 | tf_op jit(solution)/shard_map/ppermute | solution.py:395
  109.3 2.3 %collective-permute-start.35 = (f32[128,128]{1,0:T(8,128)S(1)}, f32[128,128]{1,0:T(8,128)S(1)}, u32[]{:S(2)}, u32[]{:S(2)}) collective-permute-start(f32[128,128]{1,0:T(8,128)S(1)} %add.51), channel_id=1, source_target_pairs={{0,4},{1,5},{2,6},{3,7},{4,0},{5,1},{6,2},{7,3},{8,12},{9,13},{10,... | collective-permute-start | bytes 196616 | tf_op jit(solution)/shard_map/ppermute | solution.py:395
  111.6 2.2 %collective-permute-done.35 = f32[128,128]{1,0:T(8,128)S(1)} collective-permute-done((f32[128,128]{1,0:T(8,128)S(1)}, f32[128,128]{1,0:T(8,128)S(1)}, u32[]{:S(2)}, u32[]{:S(2)}) %collective-permute-start.35) | collective-permute-done | bytes 65568 | tf_op jit(solution)/shard_map/ppermute | solution.py:395
  113.9 3.2 %collective-permute-start.36 = (f32[128,128]{1,0:T(8,128)S(1)}, f32[128,128]{1,0:T(8,128)S(1)}, u32[]{:S(2)}, u32[]{:S(2)}) collective-permute-start(f32[128,128]{1,0:T(8,128)S(1)} %add.52), channel_id=1, source_target_pairs={{0,8},{1,9},{2,10},{3,11},{4,12},{5,13},{6,14},{7,15},{8,0},{9,1},... | collective-permute-start | bytes 196616 | tf_op jit(solution)/shard_map/ppermute | solution.py:395
  117.1 2.2 %collective-permute-done.36 = f32[128,128]{1,0:T(8,128)S(1)} collective-permute-done((f32[128,128]{1,0:T(8,128)S(1)}, f32[128,128]{1,0:T(8,128)S(1)}, u32[]{:S(2)}, u32[]{:S(2)}) %collective-permute-start.36) | collective-permute-done | bytes 65568 | tf_op jit(solution)/shard_map/ppermute | solution.py:395
  120.7 8.5 %solve_finish.1 = (f32[16,2048]{1,0:T(8,128)S(1)}, f32[16,2048]{1,0:T(8,128)S(1)}, f32[8,128]{1,0:T(8,128)S(1)}) custom-call(f32[128,128]{1,0:T(8,128)S(1)} %get-tuple-element.154.left, f32[128,128]{1,0:T(8,128)S(1)} %get-tuple-element.153.right, f32[16,64,32]{2,1,0:T(8,128)S(1)} %get-tuple-element.123.refs_0_, ...), custom_call_target="tpu_custom_call" | custom-call | tf_op jit(solution)/shard_map/solve_finish/pallas_call | solution.py:453
  (87 shorter events, 32.3 us)
Async XLA Ops:
  2.7 1.5 %collective-permute-start.10 = (bf16[1,64,128]{2,1,0:T(8,128)(2,1)S(1)}, bf16[1,64,128]{2,1,0:T(8,128)(2,1)S(1)}, u32[]{:S(2)}, u32[]{:S(2)}) collective-permute-start(bf16[1,64,128]{2,1,0:T(8,128)(2,1)S(1)} %get-tuple-element.93), channel_id=1, source_target_pairs={{0,1},{1,0},{2,3},{3,2},{4,5},{5,4},{6,7},{7,6},{8,9},{9,8},{10,11... | collective-permute-start | bytes 49160 | tf_op jit(solution)/shard_map/ppermute | solution.py:386
  3.3 2.3 %collective-permute-start.13 = (bf16[1,64,128]{2,1,0:T(8,128)(2,1)S(1)}, bf16[1,64,128]{2,1,0:T(8,128)(2,1)S(1)}, u32[]{:S(2)}, u32[]{:S(2)}) collective-permute-start(bf16[1,64,128]{2,1,0:T(8,128)(2,1)S(1)} %get-tuple-element.99), channel_id=1, source_target_pairs={{1,2},{2,1},{3,4},{4,3},{5,6},{6,5},{7,8},{8,7},{9,10},{10,9},{11,... | collective-permute-start | bytes 49160 | tf_op jit(solution)/shard_map/ppermute | solution.py:389
  6.3 4.8 %collective-permute-start.14 = (bf16[1,64,128]{2,1,0:T(8,128)(2,1)S(1)}, bf16[1,64,128]{2,1,0:T(8,128)(2,1)S(1)}, u32[]{:S(2)}, u32[]{:S(2)}) collective-permute-start(bf16[1,64,128]{2,1,0:T(8,128)(2,1)S(1)} %get-tuple-element.101), channel_id=1, source_target_pairs={{0,1},{1,0},{2,3},{3,2},{4,5},{5,4},{6,7},{7,6},{8,9},{9,8},{10,11... | collective-permute-start | bytes 49160 | tf_op jit(solution)/shard_map/ppermute | solution.py:386
  10.3 1.5 %collective-permute-start.11 = (bf16[4,80,384]{2,1,0:T(8,128)(2,1)S(1)}, bf16[4,80,384]{2,1,0:T(8,128)(2,1)S(1)}, u32[]{:S(2)}, u32[]{:S(2)}) collective-permute-start(bf16[4,80,384]{2,1,0:T(8,128)(2,1)S(1)} %get-tuple-element.94), channel_id=1, source_target_pairs={{0,1},{1,0},{2,3},{3,2},{4,5},{5,4},{6,7},{7,6},{8,9},{9,8},{10,11... | collective-permute-start | bytes 737288 | tf_op jit(solution)/shard_map/ppermute | solution.py:386
  10.4 1.4 %collective-permute-start.12 = (bf16[4,80,384]{2,1,0:T(8,128)(2,1)S(1)}, bf16[4,80,384]{2,1,0:T(8,128)(2,1)S(1)}, u32[]{:S(2)}, u32[]{:S(2)}) collective-permute-start(bf16[4,80,384]{2,1,0:T(8,128)(2,1)S(1)} %get-tuple-element.95), channel_id=1, source_target_pairs={{1,2},{2,1},{3,4},{4,3},{5,6},{6,5},{7,8},{8,7},{9,10},{10,9},{11,... | collective-permute-start | bytes 737288 | tf_op jit(solution)/shard_map/ppermute | solution.py:389
  12.8 11.7 %collective-permute-start.16 = (bf16[5,64,128]{2,1,0:T(8,128)(2,1)S(1)}, bf16[5,64,128]{2,1,0:T(8,128)(2,1)S(1)}, u32[]{:S(2)}, u32[]{:S(2)}) collective-permute-start(bf16[5,64,128]{2,1,0:T(8,128)(2,1)S(1)} %get-tuple-element.102.mine), channel_id=1, source_target_pairs={{0,1},{1,0},{2,3},{3,2},{4,5},{5,4},{6,7},{7,6},{8,9},{9,8},{10,11... | collective-permute-start | bytes 245768 | tf_op jit(solution)/shard_map/ppermute | solution.py:386
  27.0 7.2 %collective-permute-start.18 = (bf16[5,64,128]{2,1,0:T(8,128)(2,1)S(1)}, bf16[5,64,128]{2,1,0:T(8,128)(2,1)S(1)}, u32[]{:S(2)}, u32[]{:S(2)}) collective-permute-start(bf16[5,64,128]{2,1,0:T(8,128)(2,1)S(1)} %get-tuple-element.104.mine), channel_id=1, source_target_pairs={{0,1},{1,0},{2,3},{3,2},{4,5},{5,4},{6,7},{7,6},{8,9},{9,8},{10,11... | collective-permute-start | bytes 245768 | tf_op jit(solution)/shard_map/ppermute | solution.py:386
  35.1 0.9 collective-permute-start.19
  36.9 6.9 %collective-permute-start.20 = (bf16[5,64,128]{2,1,0:T(8,128)(2,1)S(1)}, bf16[5,64,128]{2,1,0:T(8,128)(2,1)S(1)}, u32[]{:S(2)}, u32[]{:S(2)}) collective-permute-start(bf16[5,64,128]{2,1,0:T(8,128)(2,1)S(1)} %get-tuple-element.106.mine), channel_id=1, source_target_pairs={{0,1},{1,0},{2,3},{3,2},{4,5},{5,4},{6,7},{7,6},{8,9},{9,8},{10,11... | collective-permute-start | bytes 245768 | tf_op jit(solution)/shard_map/ppermute | solution.py:386
  45.8 1.3 %collective-permute-start.21 = (f32[128,128]{1,0:T(8,128)S(1)}, f32[128,128]{1,0:T(8,128)S(1)}, u32[]{:S(2)}, u32[]{:S(2)}) collective-permute-start(f32[128,128]{1,0:T(8,128)S(1)} %broadcast_select_fusion.5), channel_id=1, source_target_pairs={{0,1},{1,0},{2,3},{3,2},{4,5},{5,4},{6,7},{7,6},{8,9},{9,8},{10,11... | collective-permute-start | bytes 196616 | tf_op jit(solution)/shard_map/ppermute | solution.py:386
  47.1 5.5 %collective-permute-start.22 = (f32[128,128]{1,0:T(8,128)S(1)}, f32[128,128]{1,0:T(8,128)S(1)}, u32[]{:S(2)}, u32[]{:S(2)}) collective-permute-start(f32[128,128]{1,0:T(8,128)S(1)} %select_add_fusion.1), channel_id=1, source_target_pairs={{0,2},{1,3},{2,0},{3,1},{4,6},{5,7},{6,4},{7,5},{8,10},{9,11},{10,... | collective-permute-start | bytes 196616 | tf_op jit(solution)/shard_map/ppermute | solution.py:395
  52.7 4.3 %collective-permute-start.23 = (f32[128,128]{1,0:T(8,128)S(1)}, f32[128,128]{1,0:T(8,128)S(1)}, u32[]{:S(2)}, u32[]{:S(2)}) collective-permute-start(f32[128,128]{1,0:T(8,128)S(1)} %add.47), channel_id=1, source_target_pairs={{0,4},{1,5},{2,6},{3,7},{4,0},{5,1},{6,2},{7,3},{8,12},{9,13},{10,... | collective-permute-start | bytes 196616 | tf_op jit(solution)/shard_map/ppermute | solution.py:395
  57.0 5.2 %collective-permute-start.24 = (f32[128,128]{1,0:T(8,128)S(1)}, f32[128,128]{1,0:T(8,128)S(1)}, u32[]{:S(2)}, u32[]{:S(2)}) collective-permute-start(f32[128,128]{1,0:T(8,128)S(1)} %add.48), channel_id=1, source_target_pairs={{0,8},{1,9},{2,10},{3,11},{4,12},{5,13},{6,14},{7,15},{8,0},{9,1},... | collective-permute-start | bytes 196616 | tf_op jit(solution)/shard_map/ppermute | solution.py:395
  62.3 1.3 %collective-permute-start.25 = (f32[128,128]{1,0:T(8,128)S(1)}, f32[128,128]{1,0:T(8,128)S(1)}, u32[]{:S(2)}, u32[]{:S(2)}) collective-permute-start(f32[128,128]{1,0:T(8,128)S(1)} %add.49), channel_id=1, source_target_pairs={{0,1},{1,0},{2,3},{3,2},{4,5},{5,4},{6,7},{7,6},{8,9},{9,8},{10,11... | collective-permute-start | bytes 196616 | tf_op jit(solution)/shard_map/ppermute | solution.py:386
  72.0 1.2 collective-permute-start.26
  74.8 6.2 %collective-permute-start.28 = (bf16[5,64,128]{2,1,0:T(8,128)(2,1)S(1)}, bf16[5,64,128]{2,1,0:T(8,128)(2,1)S(1)}, u32[]{:S(2)}, u32[]{:S(2)}) collective-permute-start(bf16[5,64,128]{2,1,0:T(8,128)(2,1)S(1)} %get-tuple-element.118.mine), channel_id=1, source_target_pairs={{0,1},{1,0},{2,3},{3,2},{4,5},{5,4},{6,7},{7,6},{8,9},{9,8},{10,11... | collective-permute-start | bytes 245768 | tf_op jit(solution)/shard_map/ppermute | solution.py:386
  82.0 0.9 collective-permute-start.29
  83.8 6.9 %collective-permute-start.30 = (bf16[5,64,128]{2,1,0:T(8,128)(2,1)S(1)}, bf16[5,64,128]{2,1,0:T(8,128)(2,1)S(1)}, u32[]{:S(2)}, u32[]{:S(2)}) collective-permute-start(bf16[5,64,128]{2,1,0:T(8,128)(2,1)S(1)} %get-tuple-element.120.mine), channel_id=1, source_target_pairs={{0,1},{1,0},{2,3},{3,2},{4,5},{5,4},{6,7},{7,6},{8,9},{9,8},{10,11... | collective-permute-start | bytes 245768 | tf_op jit(solution)/shard_map/ppermute | solution.py:386
  93.1 7.3 %collective-permute-start.32 = (bf16[5,64,128]{2,1,0:T(8,128)(2,1)S(1)}, bf16[5,64,128]{2,1,0:T(8,128)(2,1)S(1)}, u32[]{:S(2)}, u32[]{:S(2)}) collective-permute-start(bf16[5,64,128]{2,1,0:T(8,128)(2,1)S(1)} %get-tuple-element.122.mine), channel_id=1, source_target_pairs={{0,1},{1,0},{2,3},{3,2},{4,5},{5,4},{6,7},{7,6},{8,9},{9,8},{10,11... | collective-permute-start | bytes 245768 | tf_op jit(solution)/shard_map/ppermute | solution.py:386
  102.4 1.3 %collective-permute-start.33 = (f32[128,128]{1,0:T(8,128)S(1)}, f32[128,128]{1,0:T(8,128)S(1)}, u32[]{:S(2)}, u32[]{:S(2)}) collective-permute-start(f32[128,128]{1,0:T(8,128)S(1)} %broadcast_select_fusion.2), channel_id=1, source_target_pairs={{0,1},{1,0},{2,3},{3,2},{4,5},{5,4},{6,7},{7,6},{8,9},{9,8},{10,11... | collective-permute-start | bytes 196616 | tf_op jit(solution)/shard_map/ppermute | solution.py:386
  103.8 5.5 %collective-permute-start.34 = (f32[128,128]{1,0:T(8,128)S(1)}, f32[128,128]{1,0:T(8,128)S(1)}, u32[]{:S(2)}, u32[]{:S(2)}) collective-permute-start(f32[128,128]{1,0:T(8,128)S(1)} %select_add_fusion), channel_id=1, source_target_pairs={{0,2},{1,3},{2,0},{3,1},{4,6},{5,7},{6,4},{7,5},{8,10},{9,11},{10,... | collective-permute-start | bytes 196616 | tf_op jit(solution)/shard_map/ppermute | solution.py:395
  109.3 4.5 %collective-permute-start.35 = (f32[128,128]{1,0:T(8,128)S(1)}, f32[128,128]{1,0:T(8,128)S(1)}, u32[]{:S(2)}, u32[]{:S(2)}) collective-permute-start(f32[128,128]{1,0:T(8,128)S(1)} %add.51), channel_id=1, source_target_pairs={{0,4},{1,5},{2,6},{3,7},{4,0},{5,1},{6,2},{7,3},{8,12},{9,13},{10,... | collective-permute-start | bytes 196616 | tf_op jit(solution)/shard_map/ppermute | solution.py:395
  113.9 5.5 %collective-permute-start.36 = (f32[128,128]{1,0:T(8,128)S(1)}, f32[128,128]{1,0:T(8,128)S(1)}, u32[]{:S(2)}, u32[]{:S(2)}) collective-permute-start(f32[128,128]{1,0:T(8,128)S(1)} %add.52), channel_id=1, source_target_pairs={{0,8},{1,9},{2,10},{3,11},{4,12},{5,13},{6,14},{7,15},{8,0},{9,1},... | collective-permute-start | bytes 196616 | tf_op jit(solution)/shard_map/ppermute | solution.py:395
  119.4 1.3 %collective-permute-start.37 = (f32[128,128]{1,0:T(8,128)S(1)}, f32[128,128]{1,0:T(8,128)S(1)}, u32[]{:S(2)}, u32[]{:S(2)}) collective-permute-start(f32[128,128]{1,0:T(8,128)S(1)} %add.53), channel_id=1, source_target_pairs={{0,1},{1,0},{2,3},{3,2},{4,5},{5,4},{6,7},{7,6},{8,9},{9,8},{10,11... | collective-permute-start | bytes 196616 | tf_op jit(solution)/shard_map/ppermute | solution.py:386
  (9 other events, 7.8 us)
where the time goes:
time: 132 us; the launch traced here: 131 us
  starting transfers between devices  68.2 us (52%)
  Pallas kernels  32.2 us (24%)
  waiting for transfers between devices  25.5 us (19%)
  local copies, waits for them, and re-layouts  3.35 us (3%)
  between operations  1.66 us (1%)
    ppermute x14, starting transfers between devices, chip(): return lax.ppermute(value, AXES, chip_pairs)  46.4 us
    ppermute x6, starting transfers between devices, total(): lax.ppermute(value, AXES, [(d, d ^ step) for d in range(devices)])  16.1 us
    ppermute x6, waiting for transfers between devices, total(): lax.ppermute(value, AXES, [(d, d ^ step) for d in range(devices)])  14.5 us
    ppermute x14, waiting for transfers between devices, chip(): return lax.ppermute(value, AXES, chip_pairs)  10.9 us
    pallas_call x1, Pallas kernels, shards(): x, r, doubt = finish(*sums, *fields, x, doubt, first_r, first_x)  8.46 us
    pallas_call x1, Pallas kernels, shards(): x, r, own, to_chip, doubt = update(lists, *sums, *fields, x)  8.37 us
    ppermute x8, starting transfers between devices, link(): return lax.ppermute(value, AXES, link_pairs)  5.68 us
    pallas_call x6, Pallas kernels, shards(): value, mine = power(link_table, kept, link_rows, mine, link(mine))  5.45 us
  transfers between devices with their start and end apart: 28, of which 18 were waited for; matrix products, arithmetic and copies ran while one was open for 0% of the time, Pallas kernels for 1%

commit v1 on v0

--- a/solution.py
+++ b/solution.py
@@ -24,6 +24,7 @@
 BF16 = jnp.bfloat16
 
 VMEM = pl.BlockSpec(memory_space=pltpu.VMEM)
+SMEM = pl.BlockSpec(memory_space=pltpu.SMEM)
 ANY = pl.BlockSpec(memory_space=pl.ANY)
 PARAMS = pltpu.CompilerParams(vmem_limit_bytes=16 * 1024 * 1024)
 
@@ -53,6 +54,11 @@
 def listed(lists, side, ext):
     slots = lists.shape[1] // 2
     return [ext[lists[0, side * slots + s]].astype(F32) for s in range(slots)]
+
+
+def first_kernel(lists, flat, x, to_chip, to_link, ext):
+    x[...] = flat[...].reshape(x.shape)
+    start_kernel(lists, x, to_chip, to_link, ext)
 
 
 def start_kernel(lists, x, to_chip, to_link, ext):
@@ -171,8 +177,7 @@
     half = left.shape[0]
     low_left, right = left[...], right[...]
     row, column = block_of(half, 0), block_of(half, 1)
-    by_lane = right[: POWERS + 2].T
-    norms = jnp.concatenate([by_lane[half - RHS :, j : j + 1] for j in range(POWERS + 2)], axis=0)
+    norms = jnp.concatenate([right[j : j + 1, half - RHS :] for j in range(POWERS + 2)], axis=1)
     right = jnp.where(column < 3, right, 0.0)
     first = jnp.where(row <= column, low_left, low_left.T)
     moved = jnp.concatenate([low_left[RHS:], jnp.zeros((RHS, half), F32)], axis=0)
@@ -235,6 +240,10 @@
     return jnp.concatenate(parts, axis=0)
 
 
+def weighted(weights, rows):
+    return jnp.dot(weights.astype(BF16), rows.astype(BF16), preferred_element_type=F32)
+
+
 def mixing(left, right):
     gram, norms = unpack_gram(left, right)
     size = gram.shape[0]
@@ -253,16 +262,23 @@
     change = exact(moved, second)
     sol = below(first, size, 0) + change
     res = below(first_left, size, 0) - change + GROWTH * below(change[: size - RHS], size, 1)
-    is_diagonal = lax.broadcasted_iota(jnp.int32, gram.shape, 0) == lax.broadcasted_iota(jnp.int32, gram.shape, 1)
-    scale = jnp.sqrt(jnp.sum(jnp.where(is_diagonal, gram, 0.0), axis=1, keepdims=True))
-    reach = jnp.sum(jnp.abs(images) * scale, axis=0, keepdims=True)
+    half = size // 2
+    is_diagonal = lax.broadcasted_iota(jnp.int32, (half, half), 0) == lax.broadcasted_iota(jnp.int32, (half, half), 1)
+    diagonal = jnp.concatenate(
+        [
+            jnp.sum(jnp.where(is_diagonal, block, 0.0), axis=0, keepdims=True)
+            for block in (gram[:half, :half], gram[half:, half:])
+        ],
+        axis=1,
+    )
+    reach = weighted(jnp.sqrt(diagonal), jnp.abs(images))
     reach = reach * reach
     corner = jnp.where(eye > 0, projected[square:, square:], 0.0)
     left_over = jnp.sum(corner, axis=0, keepdims=True) - jnp.sum(
         projected[:square, square:] * second, axis=0, keepdims=True
     )
-    power = (lax.broadcasted_iota(jnp.int32, (size, 1), 0) // RHS).astype(F32)
-    rounding = jnp.sum(res * res * (norms * power), axis=0, keepdims=True)
+    power = (lax.broadcasted_iota(jnp.int32, (1, size), 1) // RHS).astype(F32)
+    rounding = weighted(norms * power, res * res)
     doubts = [
         jnp.where(reach[:, :square] <= TRUST_PIVOT * pivots[:, :square], 0.0, 1.0),
         jnp.where(reach[:, square:] <= TRUST_RESIDUAL * left_over, 0.0, 1.0),
@@ -272,27 +288,29 @@
     return jnp.concatenate([sol, res], axis=1), doubt
 
 
-def combined(mix, fields):
+def stack_kernel(*refs):
+    fields, (high, low) = refs[:-2], refs[-2:]
     rows = fields[0].shape[0] * DOF
-    stacked = jnp.concatenate([field[...].reshape(rows, RHS) for field in fields], axis=1)
-    rest = mix.shape[0] - stacked.shape[1]
+    columns = [field[...].reshape(rows, RHS) for field in fields]
+    rest = high.shape[1] - RHS * len(fields)
     if rest:
-        stacked = jnp.concatenate([stacked, jnp.zeros((rows, rest), F32)], axis=1)
+        columns.append(jnp.zeros((rows, rest), F32))
+    high[...], low[...] = split(jnp.concatenate(columns, axis=1))
+
+
+def combined(mix, high, low, shape):
     mix_high, mix_low = split(mix)
-    high, low = split(stacked)
-    out = jnp.dot(high, mix_high, preferred_element_type=F32)
-    out += jnp.dot(high, mix_low, preferred_element_type=F32)
-    out += jnp.dot(low, mix_high, preferred_element_type=F32)
-    shape = fields[0].shape
+    width = mix.shape[1]
+    out = jnp.dot(high[...], jnp.concatenate([mix_high, mix_low], axis=1), preferred_element_type=F32)
+    out = out[:, :width] + out[:, width:] + jnp.dot(low[...], mix_high, preferred_element_type=F32)
     return out[:, :RHS].reshape(shape), out[:, RHS:].reshape(shape)
 
 
-def update_kernel(lists, left, right, *refs):
-    fields, (x, new_x, r, own, to_chip, doubt, ext) = refs[: POWERS + 1], refs[POWERS + 1 :]
+def update_kernel(lists, left, right, high, low, x, new_x, r, own, to_chip, doubt, ext):
     count = x.shape[0]
     mix, found = mixing(left, right)
     doubt[...] = jnp.broadcast_to(found, doubt.shape)
-    step, r[...] = combined(mix, fields)
+    step, r[...] = combined(mix, high, low, x.shape)
     new_x[...] = x[...] + step
     pack(own, [r[e] for e in range(count)])
     ext[:count] = r[...].astype(BF16)
@@ -300,12 +318,11 @@
     pack(to_chip, listed(lists, 0, ext))
 
 
-def finish_kernel(left, right, *refs):
-    fields, (x, earlier, first_r, first_x, new_x, r, doubt) = refs[: POWERS + 1], refs[POWERS + 1 :]
+def finish_kernel(left, right, high, low, x, earlier, first_r, first_x, new_x, r, repeats):
     mix, found = mixing(left, right)
     found = found + earlier[:1, :1]
-    doubt[...] = jnp.broadcast_to(found, doubt.shape)
-    step, last = combined(mix, fields)
+    repeats[0] = jnp.where(found[0, 0] == 0, 0, CYCLES)
+    step, last = combined(mix, high, low, x.shape)
     trusted = (found == 0).reshape(1, 1, 1)
     new_x[...] = jnp.where(trusted, x[...] + step, first_x[...]).reshape(new_x.shape)
     r[...] = jnp.where(trusted, last, first_r[...]).reshape(r.shape)
@@ -327,15 +344,14 @@
     gram[...] = inner_products([fields[k] - fields[k + 1] for k in range(SSTEP)] + [fields[0]])
 
 
-def single_update_kernel(gram, *refs):
-    fields, (x, new_x, r) = refs[: SSTEP + 1], refs[SSTEP + 1 :]
+def single_update_kernel(gram, high, low, x, new_x, r):
     first, _ = eliminate(gram)
     size = gram.shape[0]
     eye = (
         lax.broadcasted_iota(jnp.int32, (RHS, RHS), 0) == lax.broadcasted_iota(jnp.int32, (RHS, RHS), 1)
     ).astype(F32)
     res = below(eye, size, 0) - below(first, size, 0) + below(first, size, 1)
-    step, r[...] = combined(jnp.concatenate([below(first, size, 0), res], axis=1), fields)
+    step, r[...] = combined(jnp.concatenate([below(first, size, 0), res], axis=1), high, low, x.shape)
     new_x[...] = x[...] + step
 
 
@@ -359,12 +375,12 @@
     doubt_shape = shape(F32, 8, LANES)
     table_shape = shape(jnp.int32, count + slots, LANES)
 
-    def call(kernel, outs, specs, name, blocks=0):
+    def call(kernel, outs, specs, name, blocks=0, last=VMEM):
         return pl.pallas_call(
             kernel,
             out_shape=outs,
             in_specs=specs,
-            out_specs=[VMEM] * len(outs),
+            out_specs=[VMEM] * (len(outs) - 1) + [last],
             scratch_shapes=[pltpu.VMEM((blocks, DOF, RHS), BF16)] if blocks else [],
             compiler_params=PARAMS,
             name=name,
@@ -390,14 +406,15 @@
 
     def total(left, right):
         value = jnp.where(second, right, left) + chip(jnp.where(second, left, right))
-        step = 2
-        while step < devices:
-            value = value + lax.ppermute(value, AXES, [(d, d ^ step) for d in range(devices)])
-            step *= 2
+        steps = [1 << k for k in range(1, devices.bit_length() - 1)]
+        for first_step, second_step in zip(steps, steps[1:] + steps[:1]):
+            pairs = [(d, d ^ (second_step if d % 2 else first_step)) for d in range(devices)]
+            value = value + lax.ppermute(value, AXES, pairs)
         other = chip(value)
         return jnp.where(second, other, value), jnp.where(second, value, other)
 
     start = call(start_kernel, [slot_message] * 2, [VMEM, VMEM], "start", count + 1)
+    prepare = call(first_kernel, [field] + [slot_message] * 2, [VMEM, VMEM], "prepare", count + 1)
     send_rows = call(rows_kernel, [row_message, row_message, rows_shape], [VMEM, VMEM, VMEM, ANY], "rows")
     tables = call(tables_kernel, [table_shape] * 2, [VMEM] * 4, "tables")
     first = call(
@@ -412,20 +429,25 @@
     gram = call(
         gram_kernel, [field, half_gram, half_gram], [VMEM] * (4 + POWERS), "power_and_gram", reach
     )
+    def stacked(fields):
+        width = -(-len(fields) * RHS // LANES) * LANES
+        parts = [shape(BF16, count * DOF, width)] * 2
+        return call(stack_kernel, parts, [VMEM] * len(fields), "stack")(*fields)
+
     update = call(
         update_kernel,
         [field, field, own_message, slot_message, doubt_shape],
-        [VMEM] * (POWERS + 5),
+        [VMEM] * 6,
         "solve_update",
         count + 1,
     )
     flat = shape(F32, *right_side.shape)
-    finish = call(finish_kernel, [flat, flat, doubt_shape], [VMEM] * (POWERS + 7), "solve_finish")
+    finish = call(finish_kernel, [flat, flat, shape(jnp.int32, 1)], [VMEM] * 8, "solve_finish", last=SMEM)
 
     b = right_side.reshape(count, DOF, RHS)
-    x = first_x = first_guess.reshape(count, DOF, RHS)
     assert CYCLES == 2 * MERGED
-    to_chip, to_link = start(lists, x)
+    first_x, to_chip, to_link = prepare(lists, first_guess)
+    x = first_x
     from_link = link(to_link)
     from_chip = chip(to_chip)
     chip_rows, link_rows, kept = send_rows(lists, codes, couple, from_chip)
@@ -448,13 +470,13 @@
         if group == 0:
             first_r = r
         if group + 1 < CYCLES // MERGED:
-            x, r, own, to_chip, doubt = update(lists, *sums, *fields, x)
+            x, r, own, to_chip, doubt = update(lists, *sums, *stacked(fields), x)
         else:
-            x, r, doubt = finish(*sums, *fields, x, doubt, first_r, first_x)
+            x, r, repeats = finish(*sums, *stacked(fields), x, doubt, first_r, first_x)
 
     single_power = call(single_power_kernel, [field], [VMEM] * 5, "single_power", nowhere + 1)
     single_gram = call(single_gram_kernel, [shape(F32, LANES, LANES)], [VMEM] * (SSTEP + 1), "single_gram")
-    single_update = call(single_update_kernel, [field, field], [VMEM] * (SSTEP + 3), "single_update")
+    single_update = call(single_update_kernel, [field, field], [VMEM] * 4, "single_update")
 
     def slots_of(value):
         to_chip, to_link = start(lists, value)
@@ -470,10 +492,10 @@
         while step < devices:
             value = value + lax.ppermute(value, AXES, [(d, d ^ step) for d in range(devices)])
             step *= 2
-        x, r = single_update(value, *fields, x)
+        x, r = single_update(value, *stacked(fields), x)
         return x.reshape(right_side.shape), r.reshape(right_side.shape)
 
-    return lax.fori_loop(0, jnp.where(doubt[0, 0] == 0, 0, CYCLES), one_cycle, (x, r))
+    return lax.fori_loop(0, repeats[0], one_cycle, (x, r))
 
 
 def solution(mesh):

time: 132 us -> 130 us (0.985)
  waiting for transfers between devices: 25.5 us -> 24.1 us
    ppermute x14, waiting for transfers between devices: 10.9 us -> 9.19 us  [chip(): return lax.ppermute(value, AXES, chip_pairs)]
    pallas_call x3 -> x5, Pallas kernels: 17 us -> 17.5 us  [the longest x1 8.23 us: shards(): x, r, repeats = finish(*sums, *stacked(fields), x, doubt, first_r, first_x)]
  transfers between devices with their start and end apart: 28 -> 28, of which waited for: 18 -> 18; matrix products, arithmetic and copies ran while one was open for 0% -> 1% of each run, Pallas kernels for 1% -> 2%
where the time goes in v1:
time: 130 us
  starting transfers between devices  68.5 us (53%)
  Pallas kernels  31.4 us (24%)
  waiting for transfers between devices  24.1 us (19%)
  local copies, waits for them, and re-layouts  3.54 us (3%)
    ppermute x14, starting transfers between devices, chip(): return lax.ppermute(value, AXES, chip_pairs)  46.7 us
    ppermute x6, starting transfers between devices, total(): value = value + lax.ppermute(value, AXES, pairs)  16.1 us
    ppermute x6, waiting for transfers between devices, total(): value = value + lax.ppermute(value, AXES, pairs)  14.9 us
    ppermute x14, waiting for transfers between devices, chip(): return lax.ppermute(value, AXES, chip_pairs)  9.19 us
    pallas_call x1, Pallas kernels, shards(): x, r, repeats = finish(*sums, *stacked(fields), x, doubt, first_r, first_x)  8.23 us
    pallas_call x1, Pallas kernels, shards(): x, r, own, to_chip, doubt = update(lists, *sums, *stacked(fields), x)  7.17 us
    ppermute x8, starting transfers between devices, link(): return lax.ppermute(value, AXES, link_pairs)  5.68 us
    pallas_call x6, Pallas kernels, shards(): value, mine = power(link_table, kept, link_rows, mine, link(mine))  5.46 us
  transfers between devices with their start and end apart: 28, of which 18 were waited for; matrix products, arithmetic and copies ran while one was open for 1% of the time, Pallas kernels for 2%

profile of v1, /device:TPU:0, one launch (start us, length us, event | category | flops | bytes accessed | tf_op | source)
XLA Modules:
  0.0 129.7 jit_solution(17036667308545739116)
XLA Ops:
  4.0 1.1 reshape.23.b
  6.0 4.0 %collective-permute-start.14 = (bf16[1,64,128]{2,1,0:T(8,128)(2,1)S(1)}, bf16[1,64,128]{2,1,0:T(8,128)(2,1)S(1)}, u32[]{:S(2)}, u32[]{:S(2)}) collective-permute-start(bf16[1,64,128]{2,1,0:T(8,128)(2,1)S(1)} %get-tuple-element.109), channel_id=1, source_target_pairs={{0,1},{1,0},{2,3},{3,2},{4,5},{5,4},{6,7},{7,6},{8,9},{9,8},{10,11... | collective-permute-start | bytes 49160 | tf_op jit(solution)/shard_map/ppermute | solution.py:402
  12.6 11.0 %collective-permute-start.16 = (bf16[5,64,128]{2,1,0:T(8,128)(2,1)S(1)}, bf16[5,64,128]{2,1,0:T(8,128)(2,1)S(1)}, u32[]{:S(2)}, u32[]{:S(2)}) collective-permute-start(bf16[5,64,128]{2,1,0:T(8,128)(2,1)S(1)} %get-tuple-element.110.mine), channel_id=1, source_target_pairs={{0,1},{1,0},{2,3},{3,2},{4,5},{5,4},{6,7},{7,6},{8,9},{9,8},{10,11... | collective-permute-start | bytes 245768 | tf_op jit(solution)/shard_map/ppermute | solution.py:402
  27.0 6.2 %collective-permute-start.18 = (bf16[5,64,128]{2,1,0:T(8,128)(2,1)S(1)}, bf16[5,64,128]{2,1,0:T(8,128)(2,1)S(1)}, u32[]{:S(2)}, u32[]{:S(2)}) collective-permute-start(bf16[5,64,128]{2,1,0:T(8,128)(2,1)S(1)} %get-tuple-element.112.mine), channel_id=1, source_target_pairs={{0,1},{1,0},{2,3},{3,2},{4,5},{5,4},{6,7},{7,6},{8,9},{9,8},{10,11... | collective-permute-start | bytes 245768 | tf_op jit(solution)/shard_map/ppermute | solution.py:402
  36.8 6.0 %collective-permute-start.20 = (bf16[5,64,128]{2,1,0:T(8,128)(2,1)S(1)}, bf16[5,64,128]{2,1,0:T(8,128)(2,1)S(1)}, u32[]{:S(2)}, u32[]{:S(2)}) collective-permute-start(bf16[5,64,128]{2,1,0:T(8,128)(2,1)S(1)} %get-tuple-element.114.mine), channel_id=1, source_target_pairs={{0,1},{1,0},{2,3},{3,2},{4,5},{5,4},{6,7},{7,6},{8,9},{9,8},{10,11... | collective-permute-start | bytes 245768 | tf_op jit(solution)/shard_map/ppermute | solution.py:402
  43.8 2.0 %power_and_gram.2 = (f32[16,64,32]{2,1,0:T(8,128)S(1)}, f32[128,128]{1,0:T(8,128)S(1)}, f32[128,128]{1,0:T(8,128)S(1)}) custom-call(s32[20,128]{1,0:T(8,128)S(1)} %get-tuple-element.103.table, bf16[16,64,384]{2,1,0:T(8,128)(2,1)S(1)} %get-tuple-element.104.couple, bf16[5,64,128]{2,1,0:T(8,128)(2,1)S(1)} %get-tuple-element.114.mine, ...), custom_call_target="tpu_custom_call" | custom-call | tf_op jit(solution)/shard_map/power_and_gram/pallas_call | solution.py:467
  47.1 2.9 %collective-permute-start.22 = (f32[128,128]{1,0:T(8,128)S(1)}, f32[128,128]{1,0:T(8,128)S(1)}, u32[]{:S(2)}, u32[]{:S(2)}) collective-permute-start(f32[128,128]{1,0:T(8,128)S(1)} %select_add_fusion.1), channel_id=1, source_target_pairs={{0,2},{1,5},{2,0},{3,7},{4,6},{5,1},{6,4},{7,3},{8,10},{9,13},{10,... | collective-permute-start | bytes 196616 | tf_op jit(solution)/shard_map/ppermute | solution.py:412
  50.0 2.2 %collective-permute-done.22 = f32[128,128]{1,0:T(8,128)S(1)} collective-permute-done((f32[128,128]{1,0:T(8,128)S(1)}, f32[128,128]{1,0:T(8,128)S(1)}, u32[]{:S(2)}, u32[]{:S(2)}) %collective-permute-start.22) | collective-permute-done | bytes 65568 | tf_op jit(solution)/shard_map/ppermute | solution.py:412
  52.3 2.2 %collective-permute-start.23 = (f32[128,128]{1,0:T(8,128)S(1)}, f32[128,128]{1,0:T(8,128)S(1)}, u32[]{:S(2)}, u32[]{:S(2)}) collective-permute-start(f32[128,128]{1,0:T(8,128)S(1)} %add.47), channel_id=1, source_target_pairs={{0,4},{1,9},{2,6},{3,11},{4,0},{5,13},{6,2},{7,15},{8,12},{9,1},{1... | collective-permute-start | bytes 196616 | tf_op jit(solution)/shard_map/ppermute | solution.py:412
  54.5 2.5 %collective-permute-done.23 = f32[128,128]{1,0:T(8,128)S(1)} collective-permute-done((f32[128,128]{1,0:T(8,128)S(1)}, f32[128,128]{1,0:T(8,128)S(1)}, u32[]{:S(2)}, u32[]{:S(2)}) %collective-permute-start.23) | collective-permute-done | bytes 65568 | tf_op jit(solution)/shard_map/ppermute | solution.py:412
  57.0 2.9 %collective-permute-start.24 = (f32[128,128]{1,0:T(8,128)S(1)}, f32[128,128]{1,0:T(8,128)S(1)}, u32[]{:S(2)}, u32[]{:S(2)}) collective-permute-start(f32[128,128]{1,0:T(8,128)S(1)} %add.48), channel_id=1, source_target_pairs={{0,8},{1,3},{2,10},{3,1},{4,12},{5,7},{6,14},{7,5},{8,0},{9,11},{1... | collective-permute-start | bytes 196616 | tf_op jit(solution)/shard_map/ppermute | solution.py:412
  59.8 2.3 %collective-permute-done.24 = f32[128,128]{1,0:T(8,128)S(1)} collective-permute-done((f32[128,128]{1,0:T(8,128)S(1)}, f32[128,128]{1,0:T(8,128)S(1)}, u32[]{:S(2)}, u32[]{:S(2)}) %collective-permute-start.24) | collective-permute-done | bytes 65568 | tf_op jit(solution)/shard_map/ppermute | solution.py:412
  63.5 7.2 %solve_update.1 = (f32[16,64,32]{2,1,0:T(8,128)S(1)}, f32[16,64,32]{2,1,0:T(8,128)S(1)}, bf16[4,64,128]{2,1,0:T(8,128)(2,1)S(1)}, bf16[1,64,128]{2,1,0:T(8,128)(2,1)S(1)}, f32[8,128]{1,0:T(8,128)S(1)}) custom-call(s32[1,8]{1,0:T(1,128)S(1)} %reshape.22.lists, f32[128,128]{1,0:T(8,128)S(1)} %get-tuple-element.168.left, ...), custom_call_target="tpu_custom_call" | custom-call | tf_op jit(solution)/shard_map/solve_update/pallas_call | solution.py:473
  73.6 5.3 %collective-permute-start.28 = (bf16[5,64,128]{2,1,0:T(8,128)(2,1)S(1)}, bf16[5,64,128]{2,1,0:T(8,128)(2,1)S(1)}, u32[]{:S(2)}, u32[]{:S(2)}) collective-permute-start(bf16[5,64,128]{2,1,0:T(8,128)(2,1)S(1)} %get-tuple-element.128.mine), channel_id=1, source_target_pairs={{0,1},{1,0},{2,3},{3,2},{4,5},{5,4},{6,7},{7,6},{8,9},{9,8},{10,11... | collective-permute-start | bytes 245768 | tf_op jit(solution)/shard_map/ppermute | solution.py:402
  82.5 6.0 %collective-permute-start.30 = (bf16[5,64,128]{2,1,0:T(8,128)(2,1)S(1)}, bf16[5,64,128]{2,1,0:T(8,128)(2,1)S(1)}, u32[]{:S(2)}, u32[]{:S(2)}) collective-permute-start(bf16[5,64,128]{2,1,0:T(8,128)(2,1)S(1)} %get-tuple-element.130.mine), channel_id=1, source_target_pairs={{0,1},{1,0},{2,3},{3,2},{4,5},{5,4},{6,7},{7,6},{8,9},{9,8},{10,11... | collective-permute-start | bytes 245768 | tf_op jit(solution)/shard_map/ppermute | solution.py:402
  91.9 6.4 %collective-permute-start.32 = (bf16[5,64,128]{2,1,0:T(8,128)(2,1)S(1)}, bf16[5,64,128]{2,1,0:T(8,128)(2,1)S(1)}, u32[]{:S(2)}, u32[]{:S(2)}) collective-permute-start(bf16[5,64,128]{2,1,0:T(8,128)(2,1)S(1)} %get-tuple-element.132.mine), channel_id=1, source_target_pairs={{0,1},{1,0},{2,3},{3,2},{4,5},{5,4},{6,7},{7,6},{8,9},{9,8},{10,11... | collective-permute-start | bytes 245768 | tf_op jit(solution)/shard_map/ppermute | solution.py:402
  99.2 1.9 %power_and_gram.3 = (f32[16,64,32]{2,1,0:T(8,128)S(1)}, f32[128,128]{1,0:T(8,128)S(1)}, f32[128,128]{1,0:T(8,128)S(1)}) custom-call(s32[20,128]{1,0:T(8,128)S(1)} %get-tuple-element.103.table, bf16[16,64,384]{2,1,0:T(8,128)(2,1)S(1)} %get-tuple-element.104.couple, bf16[5,64,128]{2,1,0:T(8,128)(2,1)S(1)} %get-tuple-element.132.mine, ...), custom_call_target="tpu_custom_call" | custom-call | tf_op jit(solution)/shard_map/power_and_gram/pallas_call | solution.py:467
  102.5 2.9 %collective-permute-start.34 = (f32[128,128]{1,0:T(8,128)S(1)}, f32[128,128]{1,0:T(8,128)S(1)}, u32[]{:S(2)}, u32[]{:S(2)}) collective-permute-start(f32[128,128]{1,0:T(8,128)S(1)} %select_add_fusion), channel_id=1, source_target_pairs={{0,2},{1,5},{2,0},{3,7},{4,6},{5,1},{6,4},{7,3},{8,10},{9,13},{10,... | collective-permute-start | bytes 196616 | tf_op jit(solution)/shard_map/ppermute | solution.py:412
  105.5 2.2 %collective-permute-done.34 = f32[128,128]{1,0:T(8,128)S(1)} collective-permute-done((f32[128,128]{1,0:T(8,128)S(1)}, f32[128,128]{1,0:T(8,128)S(1)}, u32[]{:S(2)}, u32[]{:S(2)}) %collective-permute-start.34) | collective-permute-done | bytes 65568 | tf_op jit(solution)/shard_map/ppermute | solution.py:412
  107.7 2.6 %collective-permute-start.35 = (f32[128,128]{1,0:T(8,128)S(1)}, f32[128,128]{1,0:T(8,128)S(1)}, u32[]{:S(2)}, u32[]{:S(2)}) collective-permute-start(f32[128,128]{1,0:T(8,128)S(1)} %add.51), channel_id=1, source_target_pairs={{0,4},{1,9},{2,6},{3,11},{4,0},{5,13},{6,2},{7,15},{8,12},{9,1},{1... | collective-permute-start | bytes 196616 | tf_op jit(solution)/shard_map/ppermute | solution.py:412
  110.3 2.9 %collective-permute-done.35 = f32[128,128]{1,0:T(8,128)S(1)} collective-permute-done((f32[128,128]{1,0:T(8,128)S(1)}, f32[128,128]{1,0:T(8,128)S(1)}, u32[]{:S(2)}, u32[]{:S(2)}) %collective-permute-start.35) | collective-permute-done | bytes 65568 | tf_op jit(solution)/shard_map/ppermute | solution.py:412
  113.3 2.6 %collective-permute-start.36 = (f32[128,128]{1,0:T(8,128)S(1)}, f32[128,128]{1,0:T(8,128)S(1)}, u32[]{:S(2)}, u32[]{:S(2)}) collective-permute-start(f32[128,128]{1,0:T(8,128)S(1)} %add.52), channel_id=1, source_target_pairs={{0,8},{1,3},{2,10},{3,1},{4,12},{5,7},{6,14},{7,5},{8,0},{9,11},{1... | collective-permute-start | bytes 196616 | tf_op jit(solution)/shard_map/ppermute | solution.py:412
  115.8 2.7 %collective-permute-done.36 = f32[128,128]{1,0:T(8,128)S(1)} collective-permute-done((f32[128,128]{1,0:T(8,128)S(1)}, f32[128,128]{1,0:T(8,128)S(1)}, u32[]{:S(2)}, u32[]{:S(2)}) %collective-permute-start.36) | collective-permute-done | bytes 65568 | tf_op jit(solution)/shard_map/ppermute | solution.py:412
  119.9 8.2 %solve_finish.1 = (f32[16,2048]{1,0:T(8,128)}, f32[16,2048]{1,0:T(8,128)S(1)}, s32[1]{0:T(128)}) custom-call(f32[128,128]{1,0:T(8,128)S(1)} %get-tuple-element.166.left, f32[128,128]{1,0:T(8,128)S(1)} %get-tuple-element.165.right, bf16[1024,256]{1,0:T(8,128)(2,1)S(1)} %get-tuple-element.142.high, bf16[1024,256]{1,0:T(8,128)(2,1)S(1)} %get-tuple-element.143.low, ...), custom_call_target="tpu_custom_call" | custom-call | tf_op jit(solution)/shard_map/solve_finish/pallas_call | solution.py:475
  (87 shorter events, 32.3 us)
Async XLA Ops:
  2.7 2.4 %collective-permute-start.10 = (bf16[1,64,128]{2,1,0:T(8,128)(2,1)S(1)}, bf16[1,64,128]{2,1,0:T(8,128)(2,1)S(1)}, u32[]{:S(2)}, u32[]{:S(2)}) collective-permute-start(bf16[1,64,128]{2,1,0:T(8,128)(2,1)S(1)} %get-tuple-element.100), channel_id=1, source_target_pairs={{0,1},{1,0},{2,3},{3,2},{4,5},{5,4},{6,7},{7,6},{8,9},{9,8},{10,11... | collective-permute-start | bytes 49160 | tf_op jit(solution)/shard_map/ppermute | solution.py:402
  3.2 2.1 %collective-permute-start.13 = (bf16[1,64,128]{2,1,0:T(8,128)(2,1)S(1)}, bf16[1,64,128]{2,1,0:T(8,128)(2,1)S(1)}, u32[]{:S(2)}, u32[]{:S(2)}) collective-permute-start(bf16[1,64,128]{2,1,0:T(8,128)(2,1)S(1)} %get-tuple-element.106), channel_id=1, source_target_pairs={{1,2},{2,1},{3,4},{4,3},{5,6},{6,5},{7,8},{8,7},{9,10},{10,9},{11,... | collective-permute-start | bytes 49160 | tf_op jit(solution)/shard_map/ppermute | solution.py:405
  6.0 4.8 %collective-permute-start.14 = (bf16[1,64,128]{2,1,0:T(8,128)(2,1)S(1)}, bf16[1,64,128]{2,1,0:T(8,128)(2,1)S(1)}, u32[]{:S(2)}, u32[]{:S(2)}) collective-permute-start(bf16[1,64,128]{2,1,0:T(8,128)(2,1)S(1)} %get-tuple-element.109), channel_id=1, source_target_pairs={{0,1},{1,0},{2,3},{3,2},{4,5},{5,4},{6,7},{7,6},{8,9},{9,8},{10,11... | collective-permute-start | bytes 49160 | tf_op jit(solution)/shard_map/ppermute | solution.py:402
  10.0 1.5 %collective-permute-start.11 = (bf16[4,80,384]{2,1,0:T(8,128)(2,1)S(1)}, bf16[4,80,384]{2,1,0:T(8,128)(2,1)S(1)}, u32[]{:S(2)}, u32[]{:S(2)}) collective-permute-start(bf16[4,80,384]{2,1,0:T(8,128)(2,1)S(1)} %get-tuple-element.101), channel_id=1, source_target_pairs={{0,1},{1,0},{2,3},{3,2},{4,5},{5,4},{6,7},{7,6},{8,9},{9,8},{10,11... | collective-permute-start | bytes 737288 | tf_op jit(solution)/shard_map/ppermute | solution.py:402
  10.1 1.4 %collective-permute-start.12 = (bf16[4,80,384]{2,1,0:T(8,128)(2,1)S(1)}, bf16[4,80,384]{2,1,0:T(8,128)(2,1)S(1)}, u32[]{:S(2)}, u32[]{:S(2)}) collective-permute-start(bf16[4,80,384]{2,1,0:T(8,128)(2,1)S(1)} %get-tuple-element.102), channel_id=1, source_target_pairs={{1,2},{2,1},{3,4},{4,3},{5,6},{6,5},{7,8},{8,7},{9,10},{10,9},{11,... | collective-permute-start | bytes 737288 | tf_op jit(solution)/shard_map/ppermute | solution.py:405
  12.6 11.9 %collective-permute-start.16 = (bf16[5,64,128]{2,1,0:T(8,128)(2,1)S(1)}, bf16[5,64,128]{2,1,0:T(8,128)(2,1)S(1)}, u32[]{:S(2)}, u32[]{:S(2)}) collective-permute-start(bf16[5,64,128]{2,1,0:T(8,128)(2,1)S(1)} %get-tuple-element.110.mine), channel_id=1, source_target_pairs={{0,1},{1,0},{2,3},{3,2},{4,5},{5,4},{6,7},{7,6},{8,9},{9,8},{10,11... | collective-permute-start | bytes 245768 | tf_op jit(solution)/shard_map/ppermute | solution.py:402
  27.0 7.2 %collective-permute-start.18 = (bf16[5,64,128]{2,1,0:T(8,128)(2,1)S(1)}, bf16[5,64,128]{2,1,0:T(8,128)(2,1)S(1)}, u32[]{:S(2)}, u32[]{:S(2)}) collective-permute-start(bf16[5,64,128]{2,1,0:T(8,128)(2,1)S(1)} %get-tuple-element.112.mine), channel_id=1, source_target_pairs={{0,1},{1,0},{2,3},{3,2},{4,5},{5,4},{6,7},{7,6},{8,9},{9,8},{10,11... | collective-permute-start | bytes 245768 | tf_op jit(solution)/shard_map/ppermute | solution.py:402
  35.0 0.9 collective-permute-start.19
  36.8 6.9 %collective-permute-start.20 = (bf16[5,64,128]{2,1,0:T(8,128)(2,1)S(1)}, bf16[5,64,128]{2,1,0:T(8,128)(2,1)S(1)}, u32[]{:S(2)}, u32[]{:S(2)}) collective-permute-start(bf16[5,64,128]{2,1,0:T(8,128)(2,1)S(1)} %get-tuple-element.114.mine), channel_id=1, source_target_pairs={{0,1},{1,0},{2,3},{3,2},{4,5},{5,4},{6,7},{7,6},{8,9},{9,8},{10,11... | collective-permute-start | bytes 245768 | tf_op jit(solution)/shard_map/ppermute | solution.py:402
  45.7 1.3 %collective-permute-start.21 = (f32[128,128]{1,0:T(8,128)S(1)}, f32[128,128]{1,0:T(8,128)S(1)}, u32[]{:S(2)}, u32[]{:S(2)}) collective-permute-start(f32[128,128]{1,0:T(8,128)S(1)} %broadcast_select_fusion.5), channel_id=1, source_target_pairs={{0,1},{1,0},{2,3},{3,2},{4,5},{5,4},{6,7},{7,6},{8,9},{9,8},{10,11... | collective-permute-start | bytes 196616 | tf_op jit(solution)/shard_map/ppermute | solution.py:402
  47.1 5.2 %collective-permute-start.22 = (f32[128,128]{1,0:T(8,128)S(1)}, f32[128,128]{1,0:T(8,128)S(1)}, u32[]{:S(2)}, u32[]{:S(2)}) collective-permute-start(f32[128,128]{1,0:T(8,128)S(1)} %select_add_fusion.1), channel_id=1, source_target_pairs={{0,2},{1,5},{2,0},{3,7},{4,6},{5,1},{6,4},{7,3},{8,10},{9,13},{10,... | collective-permute-start | bytes 196616 | tf_op jit(solution)/shard_map/ppermute | solution.py:412
  52.3 4.7 %collective-permute-start.23 = (f32[128,128]{1,0:T(8,128)S(1)}, f32[128,128]{1,0:T(8,128)S(1)}, u32[]{:S(2)}, u32[]{:S(2)}) collective-permute-start(f32[128,128]{1,0:T(8,128)S(1)} %add.47), channel_id=1, source_target_pairs={{0,4},{1,9},{2,6},{3,11},{4,0},{5,13},{6,2},{7,15},{8,12},{9,1},{1... | collective-permute-start | bytes 196616 | tf_op jit(solution)/shard_map/ppermute | solution.py:412
  57.0 5.2 %collective-permute-start.24 = (f32[128,128]{1,0:T(8,128)S(1)}, f32[128,128]{1,0:T(8,128)S(1)}, u32[]{:S(2)}, u32[]{:S(2)}) collective-permute-start(f32[128,128]{1,0:T(8,128)S(1)} %add.48), channel_id=1, source_target_pairs={{0,8},{1,3},{2,10},{3,1},{4,12},{5,7},{6,14},{7,5},{8,0},{9,11},{1... | collective-permute-start | bytes 196616 | tf_op jit(solution)/shard_map/ppermute | solution.py:412
  62.2 1.3 %collective-permute-start.25 = (f32[128,128]{1,0:T(8,128)S(1)}, f32[128,128]{1,0:T(8,128)S(1)}, u32[]{:S(2)}, u32[]{:S(2)}) collective-permute-start(f32[128,128]{1,0:T(8,128)S(1)} %add.49), channel_id=1, source_target_pairs={{0,1},{1,0},{2,3},{3,2},{4,5},{5,4},{6,7},{7,6},{8,9},{9,8},{10,11... | collective-permute-start | bytes 196616 | tf_op jit(solution)/shard_map/ppermute | solution.py:402
  70.7 1.2 collective-permute-start.26
  73.6 6.2 %collective-permute-start.28 = (bf16[5,64,128]{2,1,0:T(8,128)(2,1)S(1)}, bf16[5,64,128]{2,1,0:T(8,128)(2,1)S(1)}, u32[]{:S(2)}, u32[]{:S(2)}) collective-permute-start(bf16[5,64,128]{2,1,0:T(8,128)(2,1)S(1)} %get-tuple-element.128.mine), channel_id=1, source_target_pairs={{0,1},{1,0},{2,3},{3,2},{4,5},{5,4},{6,7},{7,6},{8,9},{9,8},{10,11... | collective-permute-start | bytes 245768 | tf_op jit(solution)/shard_map/ppermute | solution.py:402
  80.7 0.9 collective-permute-start.29
  82.5 6.9 %collective-permute-start.30 = (bf16[5,64,128]{2,1,0:T(8,128)(2,1)S(1)}, bf16[5,64,128]{2,1,0:T(8,128)(2,1)S(1)}, u32[]{:S(2)}, u32[]{:S(2)}) collective-permute-start(bf16[5,64,128]{2,1,0:T(8,128)(2,1)S(1)} %get-tuple-element.130.mine), channel_id=1, source_target_pairs={{0,1},{1,0},{2,3},{3,2},{4,5},{5,4},{6,7},{7,6},{8,9},{9,8},{10,11... | collective-permute-start | bytes 245768 | tf_op jit(solution)/shard_map/ppermute | solution.py:402
  91.9 7.3 %collective-permute-start.32 = (bf16[5,64,128]{2,1,0:T(8,128)(2,1)S(1)}, bf16[5,64,128]{2,1,0:T(8,128)(2,1)S(1)}, u32[]{:S(2)}, u32[]{:S(2)}) collective-permute-start(bf16[5,64,128]{2,1,0:T(8,128)(2,1)S(1)} %get-tuple-element.132.mine), channel_id=1, source_target_pairs={{0,1},{1,0},{2,3},{3,2},{4,5},{5,4},{6,7},{7,6},{8,9},{9,8},{10,11... | collective-permute-start | bytes 245768 | tf_op jit(solution)/shard_map/ppermute | solution.py:402
  101.2 1.3 %collective-permute-start.33 = (f32[128,128]{1,0:T(8,128)S(1)}, f32[128,128]{1,0:T(8,128)S(1)}, u32[]{:S(2)}, u32[]{:S(2)}) collective-permute-start(f32[128,128]{1,0:T(8,128)S(1)} %broadcast_select_fusion.2), channel_id=1, source_target_pairs={{0,1},{1,0},{2,3},{3,2},{4,5},{5,4},{6,7},{7,6},{8,9},{9,8},{10,11... | collective-permute-start | bytes 196616 | tf_op jit(solution)/shard_map/ppermute | solution.py:402
  102.5 5.2 %collective-permute-start.34 = (f32[128,128]{1,0:T(8,128)S(1)}, f32[128,128]{1,0:T(8,128)S(1)}, u32[]{:S(2)}, u32[]{:S(2)}) collective-permute-start(f32[128,128]{1,0:T(8,128)S(1)} %select_add_fusion), channel_id=1, source_target_pairs={{0,2},{1,5},{2,0},{3,7},{4,6},{5,1},{6,4},{7,3},{8,10},{9,13},{10,... | collective-permute-start | bytes 196616 | tf_op jit(solution)/shard_map/ppermute | solution.py:412
  107.7 5.5 %collective-permute-start.35 = (f32[128,128]{1,0:T(8,128)S(1)}, f32[128,128]{1,0:T(8,128)S(1)}, u32[]{:S(2)}, u32[]{:S(2)}) collective-permute-start(f32[128,128]{1,0:T(8,128)S(1)} %add.51), channel_id=1, source_target_pairs={{0,4},{1,9},{2,6},{3,11},{4,0},{5,13},{6,2},{7,15},{8,12},{9,1},{1... | collective-permute-start | bytes 196616 | tf_op jit(solution)/shard_map/ppermute | solution.py:412
  113.3 5.2 %collective-permute-start.36 = (f32[128,128]{1,0:T(8,128)S(1)}, f32[128,128]{1,0:T(8,128)S(1)}, u32[]{:S(2)}, u32[]{:S(2)}) collective-permute-start(f32[128,128]{1,0:T(8,128)S(1)} %add.52), channel_id=1, source_target_pairs={{0,8},{1,3},{2,10},{3,1},{4,12},{5,7},{6,14},{7,5},{8,0},{9,11},{1... | collective-permute-start | bytes 196616 | tf_op jit(solution)/shard_map/ppermute | solution.py:412
  118.5 1.3 %collective-permute-start.37 = (f32[128,128]{1,0:T(8,128)S(1)}, f32[128,128]{1,0:T(8,128)S(1)}, u32[]{:S(2)}, u32[]{:S(2)}) collective-permute-start(f32[128,128]{1,0:T(8,128)S(1)} %add.53), channel_id=1, source_target_pairs={{0,1},{1,0},{2,3},{3,2},{4,5},{5,4},{6,7},{7,6},{8,9},{9,8},{10,11... | collective-permute-start | bytes 196616 | tf_op jit(solution)/shard_map/ppermute | solution.py:402
  (9 other events, 10.4 us)

commit v2 on v1

--- a/solution.py
+++ b/solution.py
@@ -56,9 +56,23 @@
     return [ext[lists[0, side * slots + s]].astype(F32) for s in range(slots)]
 
 
-def first_kernel(lists, flat, x, to_chip, to_link, ext):
+def first_kernel(send_lists, guess, couple, x, kept, forward, backward, lists, flat, ext, sems):
+    copies = [
+        pltpu.make_async_copy(source, target, sems.at[k])
+        for k, (source, target) in enumerate(((send_lists, lists), (guess, flat), (couple, kept)))
+    ]
+    for copy in copies:
+        copy.start()
+    count = x.shape[0]
+    ext[count] = jnp.zeros(ext.shape[1:], BF16)
+    copies[1].wait()
     x[...] = flat[...].reshape(x.shape)
-    start_kernel(lists, x, to_chip, to_link, ext)
+    ext[:count] = x[...].astype(BF16)
+    copies[0].wait()
+    for side, message in ((0, forward), (1, backward)):
+        places = [lists[0, side, s] for s in range(lists.shape[2])]
+        pack(message, [ext[jnp.where(place < 0, count, place)].astype(F32) for place in places])
+    copies[2].wait()
 
 
 def start_kernel(lists, x, to_chip, to_link, ext):
@@ -69,8 +83,7 @@
     pack(to_link, listed(lists, 1, ext))
 
 
-def rows_kernel(lists, codes, couple, after, to_chip, to_link, kept):
-    kept[...] = couple[...]
+def rows_kernel(lists, codes, couple, to_chip, to_link):
     count, slots = couple.shape[0], to_chip.shape[0]
     lanes = lax.broadcasted_iota(jnp.int32, (1, LANES), 1)
     for side, message in ((0, to_chip), (1, to_link)):
@@ -375,13 +388,13 @@
     doubt_shape = shape(F32, 8, LANES)
     table_shape = shape(jnp.int32, count + slots, LANES)
 
-    def call(kernel, outs, specs, name, blocks=0, last=VMEM):
+    def call(kernel, outs, specs, name, blocks=0, last=VMEM, scratch=()):
         return pl.pallas_call(
             kernel,
             out_shape=outs,
             in_specs=specs,
             out_specs=[VMEM] * (len(outs) - 1) + [last],
-            scratch_shapes=[pltpu.VMEM((blocks, DOF, RHS), BF16)] if blocks else [],
+            scratch_shapes=list(scratch) + ([pltpu.VMEM((blocks, DOF, RHS), BF16)] if blocks else []),
             compiler_params=PARAMS,
             name=name,
         )
@@ -414,8 +427,19 @@
         return jnp.where(second, other, value), jnp.where(second, value, other)
 
     start = call(start_kernel, [slot_message] * 2, [VMEM, VMEM], "start", count + 1)
-    prepare = call(first_kernel, [field] + [slot_message] * 2, [VMEM, VMEM], "prepare", count + 1)
-    send_rows = call(rows_kernel, [row_message, row_message, rows_shape], [VMEM, VMEM, VMEM, ANY], "rows")
+    prepare = call(
+        first_kernel,
+        [field, rows_shape, slot_message, slot_message],
+        [ANY] * 3,
+        "prepare",
+        scratch=[
+            pltpu.VMEM(send_lists.shape, jnp.int32),
+            pltpu.VMEM(first_guess.shape, F32),
+            pltpu.VMEM((count + 1, DOF, RHS), BF16),
+            pltpu.SemaphoreType.DMA((3,)),
+        ],
+    )
+    send_rows = call(rows_kernel, [row_message] * 2, [VMEM] * 3, "rows")
     tables = call(tables_kernel, [table_shape] * 2, [VMEM] * 4, "tables")
     first = call(
         residual_kernel,
@@ -446,11 +470,15 @@
 
     b = right_side.reshape(count, DOF, RHS)
     assert CYCLES == 2 * MERGED
-    first_x, to_chip, to_link = prepare(lists, first_guess)
+    first_x, kept, forward, backward = prepare(
+        *(pltpu.with_memory_space_constraint(value, pltpu.HBM) for value in (send_lists, first_guess, couple))
+    )
+    to_chip = jnp.where(second, backward, forward)
+    to_link = jnp.where(second, forward, backward)
     x = first_x
     from_link = link(to_link)
     from_chip = chip(to_chip)
-    chip_rows, link_rows, kept = send_rows(lists, codes, couple, from_chip)
+    chip_rows, link_rows = send_rows(lists, codes, kept)
     link_rows = link(link_rows)
     chip_rows = chip(chip_rows)
     r, own, to_chip = first(lists, codes, kept, from_chip, from_link, b, x)

time: 130 us -> 127 us (0.977)
  local copies, waits for them, and re-layouts: 3.54 us -> 1.07 us
  starting transfers between devices: 68.5 us -> 66.2 us
    ppermute x14, starting transfers between devices: 46.7 us -> 43.4 us  [chip(): return lax.ppermute(value, AXES, chip_pairs)]
    unnamed x13, local copies, waits for them, and re-layouts: 2.33 us -> 0.77 us
  transfers between devices with their start and end apart: 28 -> 28, of which waited for: 18 -> 18; matrix products, arithmetic and copies ran while one was open for 1% -> 0% of each run, Pallas kernels for 2% -> 2%
where the time goes in v2:
time: 127 us; the launch traced here: 126 us
  starting transfers between devices  66.2 us (52%)
  Pallas kernels  32.4 us (26%)
  waiting for transfers between devices  24.8 us (20%)
    ppermute x14, starting transfers between devices, chip(): return lax.ppermute(value, AXES, chip_pairs)  43.4 us
    ppermute x6, starting transfers between devices, total(): value = value + lax.ppermute(value, AXES, pairs)  17.1 us
    ppermute x6, waiting for transfers between devices, total(): value = value + lax.ppermute(value, AXES, pairs)  14.8 us
    ppermute x14, waiting for transfers between devices, chip(): return lax.ppermute(value, AXES, chip_pairs)  9.95 us
    pallas_call x1, Pallas kernels, shards(): x, r, repeats = finish(*sums, *stacked(fields), x, doubt, first_r, first_x)  8.23 us
    pallas_call x1, Pallas kernels, shards(): x, r, own, to_chip, doubt = update(lists, *sums, *stacked(fields), x)  7.17 us
    ppermute x8, starting transfers between devices, link(): return lax.ppermute(value, AXES, link_pairs)  5.69 us
    pallas_call x6, Pallas kernels, shards(): value, mine = power(link_table, kept, link_rows, mine, link(mine))  5.44 us
  transfers between devices with their start and end apart: 28, of which 18 were waited for; matrix products, arithmetic and copies ran while one was open for 0% of the time, Pallas kernels for 2%

profile of v2, /device:TPU:0, one launch (start us, length us, event | category | flops | bytes accessed | tf_op | source)
XLA Modules:
  0.0 126.5 jit_solution(7808704321518407918)
XLA Ops:
  2.8 4.4 %collective-permute-start.12 = (bf16[1,64,128]{2,1,0:T(8,128)(2,1)S(1)}, bf16[1,64,128]{2,1,0:T(8,128)(2,1)S(1)}, u32[]{:S(2)}, u32[]{:S(2)}) collective-permute-start(bf16[1,64,128]{2,1,0:T(8,128)(2,1)S(1)} %get-tuple-element.170), channel_id=1, source_target_pairs={{0,1},{1,0},{2,3},{3,2},{4,5},{5,4},{6,7},{7,6},{8,9},{9,8},{10,11... | collective-permute-start | bytes 49160 | tf_op jit(solution)/shard_map/ppermute | solution.py:415
  9.2 2.9 %collective-permute-start.14 = (bf16[1,64,128]{2,1,0:T(8,128)(2,1)S(1)}, bf16[1,64,128]{2,1,0:T(8,128)(2,1)S(1)}, u32[]{:S(2)}, u32[]{:S(2)}) collective-permute-start(bf16[1,64,128]{2,1,0:T(8,128)(2,1)S(1)} %get-tuple-element.109), channel_id=1, source_target_pairs={{0,1},{1,0},{2,3},{3,2},{4,5},{5,4},{6,7},{7,6},{8,9},{9,8},{10,11... | collective-permute-start | bytes 49160 | tf_op jit(solution)/shard_map/ppermute | solution.py:415
  14.7 5.3 %collective-permute-start.16 = (bf16[5,64,128]{2,1,0:T(8,128)(2,1)S(1)}, bf16[5,64,128]{2,1,0:T(8,128)(2,1)S(1)}, u32[]{:S(2)}, u32[]{:S(2)}) collective-permute-start(bf16[5,64,128]{2,1,0:T(8,128)(2,1)S(1)} %get-tuple-element.110.mine), channel_id=1, source_target_pairs={{0,1},{1,0},{2,3},{3,2},{4,5},{5,4},{6,7},{7,6},{8,9},{9,8},{10,11... | collective-permute-start | bytes 245768 | tf_op jit(solution)/shard_map/ppermute | solution.py:415
  23.5 5.9 %collective-permute-start.18 = (bf16[5,64,128]{2,1,0:T(8,128)(2,1)S(1)}, bf16[5,64,128]{2,1,0:T(8,128)(2,1)S(1)}, u32[]{:S(2)}, u32[]{:S(2)}) collective-permute-start(bf16[5,64,128]{2,1,0:T(8,128)(2,1)S(1)} %get-tuple-element.112.mine), channel_id=1, source_target_pairs={{0,1},{1,0},{2,3},{3,2},{4,5},{5,4},{6,7},{7,6},{8,9},{9,8},{10,11... | collective-permute-start | bytes 245768 | tf_op jit(solution)/shard_map/ppermute | solution.py:415
  33.0 6.2 %collective-permute-start.20 = (bf16[5,64,128]{2,1,0:T(8,128)(2,1)S(1)}, bf16[5,64,128]{2,1,0:T(8,128)(2,1)S(1)}, u32[]{:S(2)}, u32[]{:S(2)}) collective-permute-start(bf16[5,64,128]{2,1,0:T(8,128)(2,1)S(1)} %get-tuple-element.114.mine), channel_id=1, source_target_pairs={{0,1},{1,0},{2,3},{3,2},{4,5},{5,4},{6,7},{7,6},{8,9},{9,8},{10,11... | collective-permute-start | bytes 245768 | tf_op jit(solution)/shard_map/ppermute | solution.py:415
  40.1 1.9 %power_and_gram.2 = (f32[16,64,32]{2,1,0:T(8,128)S(1)}, f32[128,128]{1,0:T(8,128)S(1)}, f32[128,128]{1,0:T(8,128)S(1)}) custom-call(s32[20,128]{1,0:T(8,128)S(1)} %get-tuple-element.103.table, bf16[16,64,384]{2,1,0:T(8,128)(2,1)S(1)} %get-tuple-element.100.couple, bf16[5,64,128]{2,1,0:T(8,128)(2,1)S(1)} %get-tuple-element.114.mine, ...), custom_call_target="tpu_custom_call" | custom-call | tf_op jit(solution)/shard_map/power_and_gram/pallas_call | solution.py:495
  43.5 2.9 %collective-permute-start.22 = (f32[128,128]{1,0:T(8,128)S(1)}, f32[128,128]{1,0:T(8,128)S(1)}, u32[]{:S(2)}, u32[]{:S(2)}) collective-permute-start(f32[128,128]{1,0:T(8,128)S(1)} %select_add_fusion.1), channel_id=1, source_target_pairs={{0,2},{1,5},{2,0},{3,7},{4,6},{5,1},{6,4},{7,3},{8,10},{9,13},{10,... | collective-permute-start | bytes 196616 | tf_op jit(solution)/shard_map/ppermute | solution.py:425
  46.4 2.2 %collective-permute-done.22 = f32[128,128]{1,0:T(8,128)S(1)} collective-permute-done((f32[128,128]{1,0:T(8,128)S(1)}, f32[128,128]{1,0:T(8,128)S(1)}, u32[]{:S(2)}, u32[]{:S(2)}) %collective-permute-start.22) | collective-permute-done | bytes 65568 | tf_op jit(solution)/shard_map/ppermute | solution.py:425
  48.7 2.7 %collective-permute-start.23 = (f32[128,128]{1,0:T(8,128)S(1)}, f32[128,128]{1,0:T(8,128)S(1)}, u32[]{:S(2)}, u32[]{:S(2)}) collective-permute-start(f32[128,128]{1,0:T(8,128)S(1)} %add.47), channel_id=1, source_target_pairs={{0,4},{1,9},{2,6},{3,11},{4,0},{5,13},{6,2},{7,15},{8,12},{9,1},{1... | collective-permute-start | bytes 196616 | tf_op jit(solution)/shard_map/ppermute | solution.py:425
  51.3 2.4 %collective-permute-done.23 = f32[128,128]{1,0:T(8,128)S(1)} collective-permute-done((f32[128,128]{1,0:T(8,128)S(1)}, f32[128,128]{1,0:T(8,128)S(1)}, u32[]{:S(2)}, u32[]{:S(2)}) %collective-permute-start.23) | collective-permute-done | bytes 65568 | tf_op jit(solution)/shard_map/ppermute | solution.py:425
  53.7 2.9 %collective-permute-start.24 = (f32[128,128]{1,0:T(8,128)S(1)}, f32[128,128]{1,0:T(8,128)S(1)}, u32[]{:S(2)}, u32[]{:S(2)}) collective-permute-start(f32[128,128]{1,0:T(8,128)S(1)} %add.48), channel_id=1, source_target_pairs={{0,8},{1,3},{2,10},{3,1},{4,12},{5,7},{6,14},{7,5},{8,0},{9,11},{1... | collective-permute-start | bytes 196616 | tf_op jit(solution)/shard_map/ppermute | solution.py:425
  56.7 2.3 %collective-permute-done.24 = f32[128,128]{1,0:T(8,128)S(1)} collective-permute-done((f32[128,128]{1,0:T(8,128)S(1)}, f32[128,128]{1,0:T(8,128)S(1)}, u32[]{:S(2)}, u32[]{:S(2)}) %collective-permute-start.24) | collective-permute-done | bytes 65568 | tf_op jit(solution)/shard_map/ppermute | solution.py:425
  60.3 7.2 %solve_update.1 = (f32[16,64,32]{2,1,0:T(8,128)S(1)}, f32[16,64,32]{2,1,0:T(8,128)S(1)}, bf16[4,64,128]{2,1,0:T(8,128)(2,1)S(1)}, bf16[1,64,128]{2,1,0:T(8,128)(2,1)S(1)}, f32[8,128]{1,0:T(8,128)S(1)}) custom-call(s32[1,8]{1,0:T(1,128)S(1)} %reshape.22.lists, f32[128,128]{1,0:T(8,128)S(1)} %get-tuple-element.168.left, ...), custom_call_target="tpu_custom_call" | custom-call | tf_op jit(solution)/shard_map/solve_update/pallas_call | solution.py:501
  70.3 5.3 %collective-permute-start.28 = (bf16[5,64,128]{2,1,0:T(8,128)(2,1)S(1)}, bf16[5,64,128]{2,1,0:T(8,128)(2,1)S(1)}, u32[]{:S(2)}, u32[]{:S(2)}) collective-permute-start(bf16[5,64,128]{2,1,0:T(8,128)(2,1)S(1)} %get-tuple-element.128.mine), channel_id=1, source_target_pairs={{0,1},{1,0},{2,3},{3,2},{4,5},{5,4},{6,7},{7,6},{8,9},{9,8},{10,11... | collective-permute-start | bytes 245768 | tf_op jit(solution)/shard_map/ppermute | solution.py:415
  79.3 5.6 %collective-permute-start.30 = (bf16[5,64,128]{2,1,0:T(8,128)(2,1)S(1)}, bf16[5,64,128]{2,1,0:T(8,128)(2,1)S(1)}, u32[]{:S(2)}, u32[]{:S(2)}) collective-permute-start(bf16[5,64,128]{2,1,0:T(8,128)(2,1)S(1)} %get-tuple-element.130.mine), channel_id=1, source_target_pairs={{0,1},{1,0},{2,3},{3,2},{4,5},{5,4},{6,7},{7,6},{8,9},{9,8},{10,11... | collective-permute-start | bytes 245768 | tf_op jit(solution)/shard_map/ppermute | solution.py:415
  88.3 6.4 %collective-permute-start.32 = (bf16[5,64,128]{2,1,0:T(8,128)(2,1)S(1)}, bf16[5,64,128]{2,1,0:T(8,128)(2,1)S(1)}, u32[]{:S(2)}, u32[]{:S(2)}) collective-permute-start(bf16[5,64,128]{2,1,0:T(8,128)(2,1)S(1)} %get-tuple-element.132.mine), channel_id=1, source_target_pairs={{0,1},{1,0},{2,3},{3,2},{4,5},{5,4},{6,7},{7,6},{8,9},{9,8},{10,11... | collective-permute-start | bytes 245768 | tf_op jit(solution)/shard_map/ppermute | solution.py:415
  95.6 1.9 %power_and_gram.3 = (f32[16,64,32]{2,1,0:T(8,128)S(1)}, f32[128,128]{1,0:T(8,128)S(1)}, f32[128,128]{1,0:T(8,128)S(1)}) custom-call(s32[20,128]{1,0:T(8,128)S(1)} %get-tuple-element.103.table, bf16[16,64,384]{2,1,0:T(8,128)(2,1)S(1)} %get-tuple-element.100.couple, bf16[5,64,128]{2,1,0:T(8,128)(2,1)S(1)} %get-tuple-element.132.mine, ...), custom_call_target="tpu_custom_call" | custom-call | tf_op jit(solution)/shard_map/power_and_gram/pallas_call | solution.py:495
  98.9 2.9 %collective-permute-start.34 = (f32[128,128]{1,0:T(8,128)S(1)}, f32[128,128]{1,0:T(8,128)S(1)}, u32[]{:S(2)}, u32[]{:S(2)}) collective-permute-start(f32[128,128]{1,0:T(8,128)S(1)} %select_add_fusion), channel_id=1, source_target_pairs={{0,2},{1,5},{2,0},{3,7},{4,6},{5,1},{6,4},{7,3},{8,10},{9,13},{10,... | collective-permute-start | bytes 196616 | tf_op jit(solution)/shard_map/ppermute | solution.py:425
  101.8 2.2 %collective-permute-done.34 = f32[128,128]{1,0:T(8,128)S(1)} collective-permute-done((f32[128,128]{1,0:T(8,128)S(1)}, f32[128,128]{1,0:T(8,128)S(1)}, u32[]{:S(2)}, u32[]{:S(2)}) %collective-permute-start.34) | collective-permute-done | bytes 65568 | tf_op jit(solution)/shard_map/ppermute | solution.py:425
  104.1 3.1 %collective-permute-start.35 = (f32[128,128]{1,0:T(8,128)S(1)}, f32[128,128]{1,0:T(8,128)S(1)}, u32[]{:S(2)}, u32[]{:S(2)}) collective-permute-start(f32[128,128]{1,0:T(8,128)S(1)} %add.51), channel_id=1, source_target_pairs={{0,4},{1,9},{2,6},{3,11},{4,0},{5,13},{6,2},{7,15},{8,12},{9,1},{1... | collective-permute-start | bytes 196616 | tf_op jit(solution)/shard_map/ppermute | solution.py:425
  107.1 2.9 %collective-permute-done.35 = f32[128,128]{1,0:T(8,128)S(1)} collective-permute-done((f32[128,128]{1,0:T(8,128)S(1)}, f32[128,128]{1,0:T(8,128)S(1)}, u32[]{:S(2)}, u32[]{:S(2)}) %collective-permute-start.35) | collective-permute-done | bytes 65568 | tf_op jit(solution)/shard_map/ppermute | solution.py:425
  110.1 2.5 %collective-permute-start.36 = (f32[128,128]{1,0:T(8,128)S(1)}, f32[128,128]{1,0:T(8,128)S(1)}, u32[]{:S(2)}, u32[]{:S(2)}) collective-permute-start(f32[128,128]{1,0:T(8,128)S(1)} %add.52), channel_id=1, source_target_pairs={{0,8},{1,3},{2,10},{3,1},{4,12},{5,7},{6,14},{7,5},{8,0},{9,11},{1... | collective-permute-start | bytes 196616 | tf_op jit(solution)/shard_map/ppermute | solution.py:425
  112.6 2.7 %collective-permute-done.36 = f32[128,128]{1,0:T(8,128)S(1)} collective-permute-done((f32[128,128]{1,0:T(8,128)S(1)}, f32[128,128]{1,0:T(8,128)S(1)}, u32[]{:S(2)}, u32[]{:S(2)}) %collective-permute-start.36) | collective-permute-done | bytes 65568 | tf_op jit(solution)/shard_map/ppermute | solution.py:425
  116.7 8.2 %solve_finish.1 = (f32[16,2048]{1,0:T(8,128)}, f32[16,2048]{1,0:T(8,128)S(1)}, s32[1]{0:T(128)}) custom-call(f32[128,128]{1,0:T(8,128)S(1)} %get-tuple-element.166.left, f32[128,128]{1,0:T(8,128)S(1)} %get-tuple-element.165.right, bf16[1024,256]{1,0:T(8,128)(2,1)S(1)} %get-tuple-element.142.high, bf16[1024,256]{1,0:T(8,128)(2,1)S(1)} %get-tuple-element.143.low, ...), custom_call_target="tpu_custom_call" | custom-call | tf_op jit(solution)/shard_map/solve_finish/pallas_call | solution.py:503
  (88 shorter events, 32.2 us)
Async XLA Ops:
  2.1 6.4 %collective-permute-start.13 = (bf16[1,64,128]{2,1,0:T(8,128)(2,1)S(1)}, bf16[1,64,128]{2,1,0:T(8,128)(2,1)S(1)}, u32[]{:S(2)}, u32[]{:S(2)}) collective-permute-start(bf16[1,64,128]{2,1,0:T(8,128)(2,1)S(1)} %get-tuple-element.169), channel_id=1, source_target_pairs={{1,2},{2,1},{3,4},{4,3},{5,6},{6,5},{7,8},{8,7},{9,10},{10,9},{11,... | collective-permute-start | bytes 49160 | tf_op jit(solution)/shard_map/ppermute | solution.py:418
  2.8 5.7 %collective-permute-start.12 = (bf16[1,64,128]{2,1,0:T(8,128)(2,1)S(1)}, bf16[1,64,128]{2,1,0:T(8,128)(2,1)S(1)}, u32[]{:S(2)}, u32[]{:S(2)}) collective-permute-start(bf16[1,64,128]{2,1,0:T(8,128)(2,1)S(1)} %get-tuple-element.170), channel_id=1, source_target_pairs={{0,1},{1,0},{2,3},{3,2},{4,5},{5,4},{6,7},{7,6},{8,9},{9,8},{10,11... | collective-permute-start | bytes 49160 | tf_op jit(solution)/shard_map/ppermute | solution.py:415
  7.6 6.1 %collective-permute-start.10 = (bf16[4,80,384]{2,1,0:T(8,128)(2,1)S(1)}, bf16[4,80,384]{2,1,0:T(8,128)(2,1)S(1)}, u32[]{:S(2)}, u32[]{:S(2)}) collective-permute-start(bf16[4,80,384]{2,1,0:T(8,128)(2,1)S(1)} %get-tuple-element.101), channel_id=1, source_target_pairs={{0,1},{1,0},{2,3},{3,2},{4,5},{5,4},{6,7},{7,6},{8,9},{9,8},{10,11... | collective-permute-start | bytes 737288 | tf_op jit(solution)/shard_map/ppermute | solution.py:415
  7.6 6.0 %collective-permute-start.11 = (bf16[4,80,384]{2,1,0:T(8,128)(2,1)S(1)}, bf16[4,80,384]{2,1,0:T(8,128)(2,1)S(1)}, u32[]{:S(2)}, u32[]{:S(2)}) collective-permute-start(bf16[4,80,384]{2,1,0:T(8,128)(2,1)S(1)} %get-tuple-element.102), channel_id=1, source_target_pairs={{1,2},{2,1},{3,4},{4,3},{5,6},{6,5},{7,8},{8,7},{9,10},{10,9},{11,... | collective-permute-start | bytes 737288 | tf_op jit(solution)/shard_map/ppermute | solution.py:418
  9.2 3.8 %collective-permute-start.14 = (bf16[1,64,128]{2,1,0:T(8,128)(2,1)S(1)}, bf16[1,64,128]{2,1,0:T(8,128)(2,1)S(1)}, u32[]{:S(2)}, u32[]{:S(2)}) collective-permute-start(bf16[1,64,128]{2,1,0:T(8,128)(2,1)S(1)} %get-tuple-element.109), channel_id=1, source_target_pairs={{0,1},{1,0},{2,3},{3,2},{4,5},{5,4},{6,7},{7,6},{8,9},{9,8},{10,11... | collective-permute-start | bytes 49160 | tf_op jit(solution)/shard_map/ppermute | solution.py:415
  14.7 6.3 %collective-permute-start.16 = (bf16[5,64,128]{2,1,0:T(8,128)(2,1)S(1)}, bf16[5,64,128]{2,1,0:T(8,128)(2,1)S(1)}, u32[]{:S(2)}, u32[]{:S(2)}) collective-permute-start(bf16[5,64,128]{2,1,0:T(8,128)(2,1)S(1)} %get-tuple-element.110.mine), channel_id=1, source_target_pairs={{0,1},{1,0},{2,3},{3,2},{4,5},{5,4},{6,7},{7,6},{8,9},{9,8},{10,11... | collective-permute-start | bytes 245768 | tf_op jit(solution)/shard_map/ppermute | solution.py:415
  23.5 6.9 %collective-permute-start.18 = (bf16[5,64,128]{2,1,0:T(8,128)(2,1)S(1)}, bf16[5,64,128]{2,1,0:T(8,128)(2,1)S(1)}, u32[]{:S(2)}, u32[]{:S(2)}) collective-permute-start(bf16[5,64,128]{2,1,0:T(8,128)(2,1)S(1)} %get-tuple-element.112.mine), channel_id=1, source_target_pairs={{0,1},{1,0},{2,3},{3,2},{4,5},{5,4},{6,7},{7,6},{8,9},{9,8},{10,11... | collective-permute-start | bytes 245768 | tf_op jit(solution)/shard_map/ppermute | solution.py:415
  31.2 0.9 collective-permute-start.19
  33.0 7.1 %collective-permute-start.20 = (bf16[5,64,128]{2,1,0:T(8,128)(2,1)S(1)}, bf16[5,64,128]{2,1,0:T(8,128)(2,1)S(1)}, u32[]{:S(2)}, u32[]{:S(2)}) collective-permute-start(bf16[5,64,128]{2,1,0:T(8,128)(2,1)S(1)} %get-tuple-element.114.mine), channel_id=1, source_target_pairs={{0,1},{1,0},{2,3},{3,2},{4,5},{5,4},{6,7},{7,6},{8,9},{9,8},{10,11... | collective-permute-start | bytes 245768 | tf_op jit(solution)/shard_map/ppermute | solution.py:415
  42.1 1.3 %collective-permute-start.21 = (f32[128,128]{1,0:T(8,128)S(1)}, f32[128,128]{1,0:T(8,128)S(1)}, u32[]{:S(2)}, u32[]{:S(2)}) collective-permute-start(f32[128,128]{1,0:T(8,128)S(1)} %broadcast_select_fusion.5), channel_id=1, source_target_pairs={{0,1},{1,0},{2,3},{3,2},{4,5},{5,4},{6,7},{7,6},{8,9},{9,8},{10,11... | collective-permute-start | bytes 196616 | tf_op jit(solution)/shard_map/ppermute | solution.py:415
  43.5 5.2 %collective-permute-start.22 = (f32[128,128]{1,0:T(8,128)S(1)}, f32[128,128]{1,0:T(8,128)S(1)}, u32[]{:S(2)}, u32[]{:S(2)}) collective-permute-start(f32[128,128]{1,0:T(8,128)S(1)} %select_add_fusion.1), channel_id=1, source_target_pairs={{0,2},{1,5},{2,0},{3,7},{4,6},{5,1},{6,4},{7,3},{8,10},{9,13},{10,... | collective-permute-start | bytes 196616 | tf_op jit(solution)/shard_map/ppermute | solution.py:425
  48.7 5.1 %collective-permute-start.23 = (f32[128,128]{1,0:T(8,128)S(1)}, f32[128,128]{1,0:T(8,128)S(1)}, u32[]{:S(2)}, u32[]{:S(2)}) collective-permute-start(f32[128,128]{1,0:T(8,128)S(1)} %add.47), channel_id=1, source_target_pairs={{0,4},{1,9},{2,6},{3,11},{4,0},{5,13},{6,2},{7,15},{8,12},{9,1},{1... | collective-permute-start | bytes 196616 | tf_op jit(solution)/shard_map/ppermute | solution.py:425
  53.7 5.2 %collective-permute-start.24 = (f32[128,128]{1,0:T(8,128)S(1)}, f32[128,128]{1,0:T(8,128)S(1)}, u32[]{:S(2)}, u32[]{:S(2)}) collective-permute-start(f32[128,128]{1,0:T(8,128)S(1)} %add.48), channel_id=1, source_target_pairs={{0,8},{1,3},{2,10},{3,1},{4,12},{5,7},{6,14},{7,5},{8,0},{9,11},{1... | collective-permute-start | bytes 196616 | tf_op jit(solution)/shard_map/ppermute | solution.py:425
  59.0 1.3 %collective-permute-start.25 = (f32[128,128]{1,0:T(8,128)S(1)}, f32[128,128]{1,0:T(8,128)S(1)}, u32[]{:S(2)}, u32[]{:S(2)}) collective-permute-start(f32[128,128]{1,0:T(8,128)S(1)} %add.49), channel_id=1, source_target_pairs={{0,1},{1,0},{2,3},{3,2},{4,5},{5,4},{6,7},{7,6},{8,9},{9,8},{10,11... | collective-permute-start | bytes 196616 | tf_op jit(solution)/shard_map/ppermute | solution.py:415
  67.5 1.2 collective-permute-start.26
  70.3 6.2 %collective-permute-start.28 = (bf16[5,64,128]{2,1,0:T(8,128)(2,1)S(1)}, bf16[5,64,128]{2,1,0:T(8,128)(2,1)S(1)}, u32[]{:S(2)}, u32[]{:S(2)}) collective-permute-start(bf16[5,64,128]{2,1,0:T(8,128)(2,1)S(1)} %get-tuple-element.128.mine), channel_id=1, source_target_pairs={{0,1},{1,0},{2,3},{3,2},{4,5},{5,4},{6,7},{7,6},{8,9},{9,8},{10,11... | collective-permute-start | bytes 245768 | tf_op jit(solution)/shard_map/ppermute | solution.py:415
  77.5 0.9 collective-permute-start.29
  79.3 6.5 %collective-permute-start.30 = (bf16[5,64,128]{2,1,0:T(8,128)(2,1)S(1)}, bf16[5,64,128]{2,1,0:T(8,128)(2,1)S(1)}, u32[]{:S(2)}, u32[]{:S(2)}) collective-permute-start(bf16[5,64,128]{2,1,0:T(8,128)(2,1)S(1)} %get-tuple-element.130.mine), channel_id=1, source_target_pairs={{0,1},{1,0},{2,3},{3,2},{4,5},{5,4},{6,7},{7,6},{8,9},{9,8},{10,11... | collective-permute-start | bytes 245768 | tf_op jit(solution)/shard_map/ppermute | solution.py:415
  88.3 7.3 %collective-permute-start.32 = (bf16[5,64,128]{2,1,0:T(8,128)(2,1)S(1)}, bf16[5,64,128]{2,1,0:T(8,128)(2,1)S(1)}, u32[]{:S(2)}, u32[]{:S(2)}) collective-permute-start(bf16[5,64,128]{2,1,0:T(8,128)(2,1)S(1)} %get-tuple-element.132.mine), channel_id=1, source_target_pairs={{0,1},{1,0},{2,3},{3,2},{4,5},{5,4},{6,7},{7,6},{8,9},{9,8},{10,11... | collective-permute-start | bytes 245768 | tf_op jit(solution)/shard_map/ppermute | solution.py:415
  97.6 1.3 %collective-permute-start.33 = (f32[128,128]{1,0:T(8,128)S(1)}, f32[128,128]{1,0:T(8,128)S(1)}, u32[]{:S(2)}, u32[]{:S(2)}) collective-permute-start(f32[128,128]{1,0:T(8,128)S(1)} %broadcast_select_fusion.2), channel_id=1, source_target_pairs={{0,1},{1,0},{2,3},{3,2},{4,5},{5,4},{6,7},{7,6},{8,9},{9,8},{10,11... | collective-permute-start | bytes 196616 | tf_op jit(solution)/shard_map/ppermute | solution.py:415
  98.9 5.2 %collective-permute-start.34 = (f32[128,128]{1,0:T(8,128)S(1)}, f32[128,128]{1,0:T(8,128)S(1)}, u32[]{:S(2)}, u32[]{:S(2)}) collective-permute-start(f32[128,128]{1,0:T(8,128)S(1)} %select_add_fusion), channel_id=1, source_target_pairs={{0,2},{1,5},{2,0},{3,7},{4,6},{5,1},{6,4},{7,3},{8,10},{9,13},{10,... | collective-permute-start | bytes 196616 | tf_op jit(solution)/shard_map/ppermute | solution.py:425
  104.1 6.0 %collective-permute-start.35 = (f32[128,128]{1,0:T(8,128)S(1)}, f32[128,128]{1,0:T(8,128)S(1)}, u32[]{:S(2)}, u32[]{:S(2)}) collective-permute-start(f32[128,128]{1,0:T(8,128)S(1)} %add.51), channel_id=1, source_target_pairs={{0,4},{1,9},{2,6},{3,11},{4,0},{5,13},{6,2},{7,15},{8,12},{9,1},{1... | collective-permute-start | bytes 196616 | tf_op jit(solution)/shard_map/ppermute | solution.py:425
  110.1 5.2 %collective-permute-start.36 = (f32[128,128]{1,0:T(8,128)S(1)}, f32[128,128]{1,0:T(8,128)S(1)}, u32[]{:S(2)}, u32[]{:S(2)}) collective-permute-start(f32[128,128]{1,0:T(8,128)S(1)} %add.52), channel_id=1, source_target_pairs={{0,8},{1,3},{2,10},{3,1},{4,12},{5,7},{6,14},{7,5},{8,0},{9,11},{1... | collective-permute-start | bytes 196616 | tf_op jit(solution)/shard_map/ppermute | solution.py:425
  115.3 1.3 %collective-permute-start.37 = (f32[128,128]{1,0:T(8,128)S(1)}, f32[128,128]{1,0:T(8,128)S(1)}, u32[]{:S(2)}, u32[]{:S(2)}) collective-permute-start(f32[128,128]{1,0:T(8,128)S(1)} %add.53), channel_id=1, source_target_pairs={{0,1},{1,0},{2,3},{3,2},{4,5},{5,4},{6,7},{7,6},{8,9},{9,8},{10,11... | collective-permute-start | bytes 196616 | tf_op jit(solution)/shard_map/ppermute | solution.py:415
  (9 other events, 22.9 us)

commit v3 on v2

--- a/solution.py
+++ b/solution.py
@@ -119,7 +119,7 @@
             table[count + s : count + s + 1] = place(meta[s], reach, reach + count, near, 0)
 
 
-def residual_kernel(lists, positions, couple, from_chip, from_link, b, x, r, own, to_chip, ext):
+def residual_kernel(lists, positions, couple, from_chip, from_link, b, x, r, blocks, own, to_chip, ext):
     count = x.shape[0]
     ext[:count] = x[...].astype(BF16)
     unpack(ext, count, from_chip)
@@ -128,58 +128,86 @@
     for e in range(count):
         r[e] = b[e] - x[e] + coupled(positions, e, couple[e], ext)
     pack(own, [r[e] for e in range(count)])
-    ext[:count] = r[...].astype(BF16)
+    blocks[...] = r[...].astype(BF16)
+    ext[:count] = blocks[...]
     ext[count] = jnp.zeros(ext.shape[1:], BF16)
     pack(to_chip, listed(lists, 0, ext))
 
 
-def extend(ext, mine, theirs):
-    unpack(ext, 0, mine)
+def extend(ext, blocks, mine, theirs):
+    count = blocks.shape[0]
+    ext[:count] = blocks[...]
+    unpack(ext, count, mine.at[count // PACK :])
     unpack(ext, PACK * mine.shape[0], theirs)
     ext[ext.shape[0] - 1] = jnp.zeros(ext.shape[1:], BF16)
 
 
-def power_kernel(table, couple, extra, mine, theirs, power, message, ext):
+def power_kernel(table, couple, extra, blocks, mine, theirs, power, new_blocks, message, ext):
     count, slots = couple.shape[0], extra.shape[0]
-    extend(ext, mine, theirs)
+    extend(ext, blocks, mine, theirs)
     values = []
     for e in range(count + slots):
         rows = couple[e] if e < count else extra[e - count, :DOF]
         values.append(coupled(table, e, rows, ext) * (1.0 / GROWTH))
         if e < count:
             power[e] = values[e]
+            new_blocks[e] = values[e].astype(BF16)
     pack(message, values)
 
 
-def inner_products(columns):
-    stacked = jnp.concatenate(columns, axis=1)
-    high, low = split(stacked)
-    width = stacked.shape[1]
-    sums = lax.dot_general(
-        high, jnp.concatenate([high, low], axis=1), (((0,), (0,)), ((), ())), preferred_element_type=F32
-    )
+def inner_products(high, low):
+    width = high.shape[1]
+    sums = by_rows(high, jnp.concatenate([high, low], axis=1))
     cross = sums[:, width:]
     return sums[:, :width] + cross + cross.T
 
 
-def gram_kernel(table, couple, mine, theirs, *refs):
-    fields, (last, left, right, ext) = refs[:POWERS], refs[POWERS:]
+def squared_norms(fields):
+    rows = [jnp.sum(field * field, axis=0, keepdims=True) for field in fields]
+    return jnp.concatenate(rows + [jnp.zeros((8 - len(rows), RHS), F32)], axis=0)
+
+
+def early_gram_kernel(*refs):
+    fields, (high, low, gram, norms) = refs[:5], refs[5:]
+    fields = [field[...].reshape(-1, RHS) for field in fields]
+    columns = [fields[k] - GROWTH * fields[k + 1] for k in range(4)] + [fields[0]]
+    stacked = jnp.concatenate(columns + [jnp.zeros((columns[0].shape[0], 3 * RHS), F32)], axis=1)
+    high[...], low[...] = split(stacked)
+    gram[...] = inner_products(high[...], low[...])
+    norms[...] = squared_norms(fields)
+
+
+def by_rows(a, b):
+    return lax.dot_general(a, b, (((0,), (0,)), ((), ())), preferred_element_type=F32)
+
+
+def gram_kernel(table, couple, blocks, mine, theirs, b4, b5, high, low, early, norms, last, left, right, ext):
     count = couple.shape[0]
     rows = count * DOF
-    extend(ext, mine, theirs)
+    extend(ext, blocks, mine, theirs)
     for e in range(count):
         last[e] = coupled(table, e, couple[e], ext) * (1.0 / GROWTH)
-    fields = [field[...].reshape(rows, RHS) for field in (*fields, last)]
-    empty = jnp.zeros((rows, RHS), F32)
-    gram = inner_products([fields[k] - GROWTH * fields[k + 1] for k in range(POWERS)] + [fields[0], empty])
-    norms = jnp.concatenate(
-        [jnp.sum(field * field, axis=0, keepdims=True) for field in fields] + [jnp.zeros((1, RHS), F32)], axis=0
-    )
-    half = gram.shape[0] // 2
-    below = jnp.concatenate([jnp.zeros((RHS, half), F32), gram[half:, half:][: half - RHS]], axis=0)
-    left[...] = jnp.where(block_of(half, 0) > block_of(half, 1), below, gram[:half, :half])
-    right[...] = gram[:half, half:]
-    right[: POWERS + 2, half - RHS :] = norms
+    b4, b5, b6 = (field[...].reshape(rows, RHS) for field in (b4, b5, last))
+    late_high, late_low = split(jnp.concatenate([b4 - GROWTH * b5, b5 - GROWTH * b6], axis=1))
+    both = jnp.concatenate([late_high, late_low], axis=1)
+    width = late_high.shape[1]
+    cross = by_rows(both, high[...])
+    cross = cross[:width] + cross[width:] + by_rows(late_high, low[...])
+    own = by_rows(both, both)
+    own = own[:width, :width] + own[:width, width:] + own[width:, :width]
+    half = left.shape[0]
+    with_r = cross[:, half : half + RHS]
+    r_r = early[half : half + RHS, half : half + RHS]
+    corner = jnp.concatenate(
+        [jnp.concatenate([own, with_r], axis=1), jnp.concatenate([with_r.T, r_r], axis=1)], axis=0
+    )
+    corner = jnp.concatenate([corner, jnp.zeros((half - RHS, RHS), F32)], axis=1)
+    below_diagonal = jnp.concatenate([jnp.zeros((RHS, half), F32), corner], axis=0)
+    left[...] = jnp.where(block_of(half, 0) > block_of(half, 1), below_diagonal, early[:half, :half])
+    right[...] = jnp.concatenate(
+        [cross[:, :half].T, early[:half, half : half + RHS], jnp.zeros((half, RHS), F32)], axis=1
+    )
+    right[:8, half - RHS :] = jnp.concatenate([norms[:5], squared_norms([b5, b6])[:3]], axis=0)
 
 
 def block_of(size, dimension):
@@ -319,14 +347,15 @@
     return out[:, :RHS].reshape(shape), out[:, RHS:].reshape(shape)
 
 
-def update_kernel(lists, left, right, high, low, x, new_x, r, own, to_chip, doubt, ext):
+def update_kernel(lists, left, right, high, low, x, new_x, r, blocks, own, to_chip, doubt, ext):
     count = x.shape[0]
     mix, found = mixing(left, right)
     doubt[...] = jnp.broadcast_to(found, doubt.shape)
     step, r[...] = combined(mix, high, low, x.shape)
     new_x[...] = x[...] + step
     pack(own, [r[e] for e in range(count)])
-    ext[:count] = r[...].astype(BF16)
+    blocks[...] = r[...].astype(BF16)
+    ext[:count] = blocks[...]
     ext[count] = jnp.zeros(ext.shape[1:], BF16)
     pack(to_chip, listed(lists, 0, ext))
 
@@ -354,7 +383,8 @@
 def single_gram_kernel(*refs):
     fields, gram = refs[:-1], refs[-1]
     fields = [field[...].reshape(-1, RHS) for field in fields]
-    gram[...] = inner_products([fields[k] - fields[k + 1] for k in range(SSTEP)] + [fields[0]])
+    columns = [fields[k] - fields[k + 1] for k in range(SSTEP)] + [fields[0]]
+    gram[...] = inner_products(*split(jnp.concatenate(columns, axis=1)))
 
 
 def single_update_kernel(gram, high, low, x, new_x, r):
@@ -379,6 +409,7 @@
         return jax.ShapeDtypeStruct(sizes, dtype)
 
     field = shape(F32, count, DOF, RHS)
+    blocks_shape = shape(BF16, count, DOF, RHS)
     slot_message = shape(BF16, slots // PACK, DOF, PACK * RHS)
     own_message = shape(BF16, count // PACK, DOF, PACK * RHS)
     message = shape(BF16, (count + slots) // PACK, DOF, PACK * RHS)
@@ -443,16 +474,22 @@
     tables = call(tables_kernel, [table_shape] * 2, [VMEM] * 4, "tables")
     first = call(
         residual_kernel,
-        [field, own_message, slot_message],
+        [field, blocks_shape, own_message, slot_message],
         [VMEM] * 7,
         "first_residual",
         nowhere + 1,
     )
     reach = 2 * (count + slots) + 1
-    power = call(power_kernel, [field, message], [VMEM] * 5, "power", reach)
-    gram = call(
-        gram_kernel, [field, half_gram, half_gram], [VMEM] * (4 + POWERS), "power_and_gram", reach
-    )
+    power = call(power_kernel, [field, blocks_shape, message], [VMEM] * 6, "power", reach)
+    early_parts = [
+        shape(BF16, count * DOF, 2 * LANES),
+        shape(BF16, count * DOF, 2 * LANES),
+        shape(F32, 2 * LANES, 2 * LANES),
+        shape(F32, 8, RHS),
+    ]
+    early_gram = call(early_gram_kernel, early_parts, [VMEM] * 5, "early_gram")
+    gram = call(gram_kernel, [field, half_gram, half_gram], [VMEM] * 11, "power_and_gram", reach)
+
     def stacked(fields):
         width = -(-len(fields) * RHS // LANES) * LANES
         parts = [shape(BF16, count * DOF, width)] * 2
@@ -460,7 +497,7 @@
 
     update = call(
         update_kernel,
-        [field, field, own_message, slot_message, doubt_shape],
+        [field, field, blocks_shape, own_message, slot_message, doubt_shape],
         [VMEM] * 6,
         "solve_update",
         count + 1,
@@ -469,7 +506,7 @@
     finish = call(finish_kernel, [flat, flat, shape(jnp.int32, 1)], [VMEM] * 8, "solve_finish", last=SMEM)
 
     b = right_side.reshape(count, DOF, RHS)
-    assert CYCLES == 2 * MERGED
+    assert CYCLES == 2 * MERGED and POWERS == 6 and PACK * RHS == LANES
     first_x, kept, forward, backward = prepare(
         *(pltpu.with_memory_space_constraint(value, pltpu.HBM) for value in (send_lists, first_guess, couple))
     )
@@ -481,24 +518,26 @@
     chip_rows, link_rows = send_rows(lists, codes, kept)
     link_rows = link(link_rows)
     chip_rows = chip(chip_rows)
-    r, own, to_chip = first(lists, codes, kept, from_chip, from_link, b, x)
+    r, blocks, own, to_chip = first(lists, codes, kept, from_chip, from_link, b, x)
     chip_table, link_table = tables(lists, codes, chip_rows, link_rows)
     for group in range(CYCLES // MERGED):
         mine = jnp.concatenate([own, chip(to_chip)], axis=0)
         fields = [r]
         for k in range(POWERS - 1):
             if k % 2 == 0:
-                value, mine = power(link_table, kept, link_rows, mine, link(mine))
+                value, blocks, mine = power(link_table, kept, link_rows, blocks, mine, link(mine))
             else:
-                value, mine = power(chip_table, kept, chip_rows, mine, chip(mine))
+                value, blocks, mine = power(chip_table, kept, chip_rows, blocks, mine, chip(mine))
             fields.append(value)
-        value, left, right = gram(chip_table, kept, mine, chip(mine), *fields)
+            if k == 3:
+                early = early_gram(*fields)
+        value, left, right = gram(chip_table, kept, blocks, mine, chip(mine), *fields[4:], *early)
         fields.append(value)
         sums = total(left, right)
         if group == 0:
             first_r = r
         if group + 1 < CYCLES // MERGED:
-            x, r, own, to_chip, doubt = update(lists, *sums, *stacked(fields), x)
+            x, r, blocks, own, to_chip, doubt = update(lists, *sums, *stacked(fields), x)
         else:
             x, r, repeats = finish(*sums, *stacked(fields), x, doubt, first_r, first_x)
 

time: 127 us -> 125 us (0.984)
  starting transfers between devices: 66.2 us -> 64.5 us
    ppermute x14, waiting for transfers between devices: 9.95 us -> 8.57 us  [chip(): return lax.ppermute(value, AXES, chip_pairs)]
    pallas_call x14 -> x16, Pallas kernels: 20.8 us -> 20.9 us  [the longest x1 7.19 us: shards(): update(lists, *sums, *stacked(fields), x)]
  transfers between devices with their start and end apart: 28 -> 28, of which waited for: 18 -> 16; matrix products, arithmetic and copies ran while one was open for 0% -> 0% of each run, Pallas kernels for 2% -> 4%
where the time goes in v3:
time: 125 us
  starting transfers between devices  64.5 us (52%)
  Pallas kernels  32.5 us (26%)
  waiting for transfers between devices  24.4 us (20%)
    ppermute x14, starting transfers between devices, chip(): return lax.ppermute(value, AXES, chip_pairs)  42.6 us
    ppermute x6, starting transfers between devices, total(): value = value + lax.ppermute(value, AXES, pairs)  16.3 us
    ppermute x6, waiting for transfers between devices, total(): value = value + lax.ppermute(value, AXES, pairs)  15.8 us
    ppermute x14, waiting for transfers between devices, chip(): return lax.ppermute(value, AXES, chip_pairs)  8.57 us
    pallas_call x1, Pallas kernels, shards(): x, r, repeats = finish(*sums, *stacked(fields), x, doubt, first_r, first_x)  8.23 us
    pallas_call x1, Pallas kernels, shards(): update(lists, *sums, *stacked(fields), x)  7.19 us
    ppermute x8, starting transfers between devices, link(): return lax.ppermute(value, AXES, link_pairs)  5.67 us
    pallas_call x6, Pallas kernels, shards(): power(link_table, kept, link_rows, blocks, mine, link(mine))  4.76 us
  transfers between devices with their start and end apart: 28, of which 16 were waited for; matrix products, arithmetic and copies ran while one was open for 0% of the time, Pallas kernels for 4%

profile of v3, /device:TPU:0, one launch (start us, length us, event | category | flops | bytes accessed | tf_op | source)
XLA Modules:
  0.0 124.5 jit_solution(16274251107032074061)
XLA Ops:
  0.6 1.4 %prepare.1 = (f32[16,64,32]{2,1,0:T(8,128)S(1)}, bf16[16,64,384]{2,1,0:T(8,128)(2,1)S(1)}, bf16[1,64,128]{2,1,0:T(8,128)(2,1)S(1)}, bf16[1,64,128]{2,1,0:T(8,128)(2,1)S(1)}) custom-call(s32[1,2,4]{2,1,0:T(2,128)} %send_lists.1, f32[16,2048]{1,0:T(8,128)} %guess.1, bf16[16,64,384]{2,1,0:T(8,128)(2,1)} %couple.1), custom_call_target="tpu_custom_call" | custom-call | tf_op jit(solution)/shard_map/prepare/pallas_call | solution.py:510
  2.8 4.4 %collective-permute-start.12 = (bf16[1,64,128]{2,1,0:T(8,128)(2,1)S(1)}, bf16[1,64,128]{2,1,0:T(8,128)(2,1)S(1)}, u32[]{:S(2)}, u32[]{:S(2)}) collective-permute-start(bf16[1,64,128]{2,1,0:T(8,128)(2,1)S(1)} %get-tuple-element.210), channel_id=1, source_target_pairs={{0,1},{1,0},{2,3},{3,2},{4,5},{5,4},{6,7},{7,6},{8,9},{9,8},{10,11... | collective-permute-start | bytes 49160 | tf_op jit(solution)/shard_map/ppermute | solution.py:446
  9.3 2.9 %collective-permute-start.14 = (bf16[1,64,128]{2,1,0:T(8,128)(2,1)S(1)}, bf16[1,64,128]{2,1,0:T(8,128)(2,1)S(1)}, u32[]{:S(2)}, u32[]{:S(2)}) collective-permute-start(bf16[1,64,128]{2,1,0:T(8,128)(2,1)S(1)} %get-tuple-element.130), channel_id=1, source_target_pairs={{0,1},{1,0},{2,3},{3,2},{4,5},{5,4},{6,7},{7,6},{8,9},{9,8},{10,11... | collective-permute-start | bytes 49160 | tf_op jit(solution)/shard_map/ppermute | solution.py:446
  14.7 5.3 %collective-permute-start.16 = (bf16[5,64,128]{2,1,0:T(8,128)(2,1)S(1)}, bf16[5,64,128]{2,1,0:T(8,128)(2,1)S(1)}, u32[]{:S(2)}, u32[]{:S(2)}) collective-permute-start(bf16[5,64,128]{2,1,0:T(8,128)(2,1)S(1)} %get-tuple-element.132.mine), channel_id=1, source_target_pairs={{0,1},{1,0},{2,3},{3,2},{4,5},{5,4},{6,7},{7,6},{8,9},{9,8},{10,11... | collective-permute-start | bytes 245768 | tf_op jit(solution)/shard_map/ppermute | solution.py:446
  23.2 5.9 %collective-permute-start.18 = (bf16[5,64,128]{2,1,0:T(8,128)(2,1)S(1)}, bf16[5,64,128]{2,1,0:T(8,128)(2,1)S(1)}, u32[]{:S(2)}, u32[]{:S(2)}) collective-permute-start(bf16[5,64,128]{2,1,0:T(8,128)(2,1)S(1)} %get-tuple-element.136.mine), channel_id=1, source_target_pairs={{0,1},{1,0},{2,3},{3,2},{4,5},{5,4},{6,7},{7,6},{8,9},{9,8},{10,11... | collective-permute-start | bytes 245768 | tf_op jit(solution)/shard_map/ppermute | solution.py:446
  32.5 6.2 %collective-permute-start.20 = (bf16[5,64,128]{2,1,0:T(8,128)(2,1)S(1)}, bf16[5,64,128]{2,1,0:T(8,128)(2,1)S(1)}, u32[]{:S(2)}, u32[]{:S(2)}) collective-permute-start(bf16[5,64,128]{2,1,0:T(8,128)(2,1)S(1)} %get-tuple-element.140.mine), channel_id=1, source_target_pairs={{0,1},{1,0},{2,3},{3,2},{4,5},{5,4},{6,7},{7,6},{8,9},{9,8},{10,11... | collective-permute-start | bytes 245768 | tf_op jit(solution)/shard_map/ppermute | solution.py:446
  39.8 1.4 %power_and_gram.2 = (f32[16,64,32]{2,1,0:T(8,128)S(1)}, f32[128,128]{1,0:T(8,128)S(1)}, f32[128,128]{1,0:T(8,128)S(1)}) custom-call(s32[20,128]{1,0:T(8,128)S(1)} %get-tuple-element.123.table, bf16[16,64,384]{2,1,0:T(8,128)(2,1)S(1)} %get-tuple-element.120.couple, bf16[16,64,32]{2,1,0:T(8,128)(2,1)S(1)} %get-tuple-element.139.blocks, ...), custom_call_target="tpu_custom_call" | custom-call | tf_op jit(solution)/shard_map/power_and_gram/pallas_call | solution.py:534
  42.6 2.9 %collective-permute-start.22 = (f32[128,128]{1,0:T(8,128)S(1)}, f32[128,128]{1,0:T(8,128)S(1)}, u32[]{:S(2)}, u32[]{:S(2)}) collective-permute-start(f32[128,128]{1,0:T(8,128)S(1)} %select_add_fusion.1), channel_id=1, source_target_pairs={{0,2},{1,5},{2,0},{3,7},{4,6},{5,1},{6,4},{7,3},{8,10},{9,13},{10,... | collective-permute-start | bytes 196616 | tf_op jit(solution)/shard_map/ppermute | solution.py:456
  45.5 2.2 %collective-permute-done.22 = f32[128,128]{1,0:T(8,128)S(1)} collective-permute-done((f32[128,128]{1,0:T(8,128)S(1)}, f32[128,128]{1,0:T(8,128)S(1)}, u32[]{:S(2)}, u32[]{:S(2)}) %collective-permute-start.22) | collective-permute-done | bytes 65568 | tf_op jit(solution)/shard_map/ppermute | solution.py:456
  47.8 2.5 %collective-permute-start.23 = (f32[128,128]{1,0:T(8,128)S(1)}, f32[128,128]{1,0:T(8,128)S(1)}, u32[]{:S(2)}, u32[]{:S(2)}) collective-permute-start(f32[128,128]{1,0:T(8,128)S(1)} %add.47), channel_id=1, source_target_pairs={{0,4},{1,9},{2,6},{3,11},{4,0},{5,13},{6,2},{7,15},{8,12},{9,1},{1... | collective-permute-start | bytes 196616 | tf_op jit(solution)/shard_map/ppermute | solution.py:456
  50.2 2.8 %collective-permute-done.23 = f32[128,128]{1,0:T(8,128)S(1)} collective-permute-done((f32[128,128]{1,0:T(8,128)S(1)}, f32[128,128]{1,0:T(8,128)S(1)}, u32[]{:S(2)}, u32[]{:S(2)}) %collective-permute-start.23) | collective-permute-done | bytes 65568 | tf_op jit(solution)/shard_map/ppermute | solution.py:456
  53.0 2.6 %collective-permute-start.24 = (f32[128,128]{1,0:T(8,128)S(1)}, f32[128,128]{1,0:T(8,128)S(1)}, u32[]{:S(2)}, u32[]{:S(2)}) collective-permute-start(f32[128,128]{1,0:T(8,128)S(1)} %add.48), channel_id=1, source_target_pairs={{0,8},{1,3},{2,10},{3,1},{4,12},{5,7},{6,14},{7,5},{8,0},{9,11},{1... | collective-permute-start | bytes 196616 | tf_op jit(solution)/shard_map/ppermute | solution.py:456
  55.6 2.7 %collective-permute-done.24 = f32[128,128]{1,0:T(8,128)S(1)} collective-permute-done((f32[128,128]{1,0:T(8,128)S(1)}, f32[128,128]{1,0:T(8,128)S(1)}, u32[]{:S(2)}, u32[]{:S(2)}) %collective-permute-start.24) | collective-permute-done | bytes 65568 | tf_op jit(solution)/shard_map/ppermute | solution.py:456
  59.6 7.2 %solve_update.1 = (f32[16,64,32]{2,1,0:T(8,128)S(1)}, f32[16,64,32]{2,1,0:T(8,128)S(1)}, bf16[16,64,32]{2,1,0:T(8,128)(2,1)S(1)}, bf16[4,64,128]{2,1,0:T(8,128)(...) custom-call(s32[1,8]{1,0:T(1,128)S(1)} %reshape.22.lists, f32[128,128]{1,0:T(8,128)S(1)} %get-tuple-element.208.left, ...), custom_call_target="tpu_custom_call" | custom-call | tf_op jit(solution)/shard_map/solve_update/pallas_call | solution.py:540
  69.5 5.3 %collective-permute-start.28 = (bf16[5,64,128]{2,1,0:T(8,128)(2,1)S(1)}, bf16[5,64,128]{2,1,0:T(8,128)(2,1)S(1)}, u32[]{:S(2)}, u32[]{:S(2)}) collective-permute-start(bf16[5,64,128]{2,1,0:T(8,128)(2,1)S(1)} %get-tuple-element.160.mine), channel_id=1, source_target_pairs={{0,1},{1,0},{2,3},{3,2},{4,5},{5,4},{6,7},{7,6},{8,9},{9,8},{10,11... | collective-permute-start | bytes 245768 | tf_op jit(solution)/shard_map/ppermute | solution.py:446
  78.2 5.3 %collective-permute-start.30 = (bf16[5,64,128]{2,1,0:T(8,128)(2,1)S(1)}, bf16[5,64,128]{2,1,0:T(8,128)(2,1)S(1)}, u32[]{:S(2)}, u32[]{:S(2)}) collective-permute-start(bf16[5,64,128]{2,1,0:T(8,128)(2,1)S(1)} %get-tuple-element.164.mine), channel_id=1, source_target_pairs={{0,1},{1,0},{2,3},{3,2},{4,5},{5,4},{6,7},{7,6},{8,9},{9,8},{10,11... | collective-permute-start | bytes 245768 | tf_op jit(solution)/shard_map/ppermute | solution.py:446
  86.7 6.4 %collective-permute-start.32 = (bf16[5,64,128]{2,1,0:T(8,128)(2,1)S(1)}, bf16[5,64,128]{2,1,0:T(8,128)(2,1)S(1)}, u32[]{:S(2)}, u32[]{:S(2)}) collective-permute-start(bf16[5,64,128]{2,1,0:T(8,128)(2,1)S(1)} %get-tuple-element.168.mine), channel_id=1, source_target_pairs={{0,1},{1,0},{2,3},{3,2},{4,5},{5,4},{6,7},{7,6},{8,9},{9,8},{10,11... | collective-permute-start | bytes 245768 | tf_op jit(solution)/shard_map/ppermute | solution.py:446
  97.0 2.9 %collective-permute-start.34 = (f32[128,128]{1,0:T(8,128)S(1)}, f32[128,128]{1,0:T(8,128)S(1)}, u32[]{:S(2)}, u32[]{:S(2)}) collective-permute-start(f32[128,128]{1,0:T(8,128)S(1)} %select_add_fusion), channel_id=1, source_target_pairs={{0,2},{1,5},{2,0},{3,7},{4,6},{5,1},{6,4},{7,3},{8,10},{9,13},{10,... | collective-permute-start | bytes 196616 | tf_op jit(solution)/shard_map/ppermute | solution.py:456
  99.9 2.2 %collective-permute-done.34 = f32[128,128]{1,0:T(8,128)S(1)} collective-permute-done((f32[128,128]{1,0:T(8,128)S(1)}, f32[128,128]{1,0:T(8,128)S(1)}, u32[]{:S(2)}, u32[]{:S(2)}) %collective-permute-start.34) | collective-permute-done | bytes 65568 | tf_op jit(solution)/shard_map/ppermute | solution.py:456
  102.2 3.0 %collective-permute-start.35 = (f32[128,128]{1,0:T(8,128)S(1)}, f32[128,128]{1,0:T(8,128)S(1)}, u32[]{:S(2)}, u32[]{:S(2)}) collective-permute-start(f32[128,128]{1,0:T(8,128)S(1)} %add.51), channel_id=1, source_target_pairs={{0,4},{1,9},{2,6},{3,11},{4,0},{5,13},{6,2},{7,15},{8,12},{9,1},{1... | collective-permute-start | bytes 196616 | tf_op jit(solution)/shard_map/ppermute | solution.py:456
  105.2 2.9 %collective-permute-done.35 = f32[128,128]{1,0:T(8,128)S(1)} collective-permute-done((f32[128,128]{1,0:T(8,128)S(1)}, f32[128,128]{1,0:T(8,128)S(1)}, u32[]{:S(2)}, u32[]{:S(2)}) %collective-permute-start.35) | collective-permute-done | bytes 65568 | tf_op jit(solution)/shard_map/ppermute | solution.py:456
  108.2 2.3 %collective-permute-start.36 = (f32[128,128]{1,0:T(8,128)S(1)}, f32[128,128]{1,0:T(8,128)S(1)}, u32[]{:S(2)}, u32[]{:S(2)}) collective-permute-start(f32[128,128]{1,0:T(8,128)S(1)} %add.52), channel_id=1, source_target_pairs={{0,8},{1,3},{2,10},{3,1},{4,12},{5,7},{6,14},{7,5},{8,0},{9,11},{1... | collective-permute-start | bytes 196616 | tf_op jit(solution)/shard_map/ppermute | solution.py:456
  110.5 2.9 %collective-permute-done.36 = f32[128,128]{1,0:T(8,128)S(1)} collective-permute-done((f32[128,128]{1,0:T(8,128)S(1)}, f32[128,128]{1,0:T(8,128)S(1)}, u32[]{:S(2)}, u32[]{:S(2)}) %collective-permute-start.36) | collective-permute-done | bytes 65568 | tf_op jit(solution)/shard_map/ppermute | solution.py:456
  114.7 8.2 %solve_finish.1 = (f32[16,2048]{1,0:T(8,128)}, f32[16,2048]{1,0:T(8,128)S(1)}, s32[1]{0:T(128)}) custom-call(f32[128,128]{1,0:T(8,128)S(1)} %get-tuple-element.206.left, f32[128,128]{1,0:T(8,128)S(1)} %get-tuple-element.205.right, bf16[1024,256]{1,0:T(8,128)(2,1)S(1)} %get-tuple-element.182.high, bf16[1024,256]{1,0:T(8,128)(2,1)S(1)} %get-tuple-element.183.low, ...), custom_call_target="tpu_custom_call" | custom-call | tf_op jit(solution)/shard_map/solve_finish/pallas_call | solution.py:542
  (90 shorter events, 31.5 us)
Async XLA Ops:
  2.1 6.4 %collective-permute-start.13 = (bf16[1,64,128]{2,1,0:T(8,128)(2,1)S(1)}, bf16[1,64,128]{2,1,0:T(8,128)(2,1)S(1)}, u32[]{:S(2)}, u32[]{:S(2)}) collective-permute-start(bf16[1,64,128]{2,1,0:T(8,128)(2,1)S(1)} %get-tuple-element.209), channel_id=1, source_target_pairs={{1,2},{2,1},{3,4},{4,3},{5,6},{6,5},{7,8},{8,7},{9,10},{10,9},{11,... | collective-permute-start | bytes 49160 | tf_op jit(solution)/shard_map/ppermute | solution.py:449
  2.8 5.7 %collective-permute-start.12 = (bf16[1,64,128]{2,1,0:T(8,128)(2,1)S(1)}, bf16[1,64,128]{2,1,0:T(8,128)(2,1)S(1)}, u32[]{:S(2)}, u32[]{:S(2)}) collective-permute-start(bf16[1,64,128]{2,1,0:T(8,128)(2,1)S(1)} %get-tuple-element.210), channel_id=1, source_target_pairs={{0,1},{1,0},{2,3},{3,2},{4,5},{5,4},{6,7},{7,6},{8,9},{9,8},{10,11... | collective-permute-start | bytes 49160 | tf_op jit(solution)/shard_map/ppermute | solution.py:446
  7.5 6.2 %collective-permute-start.10 = (bf16[4,80,384]{2,1,0:T(8,128)(2,1)S(1)}, bf16[4,80,384]{2,1,0:T(8,128)(2,1)S(1)}, u32[]{:S(2)}, u32[]{:S(2)}) collective-permute-start(bf16[4,80,384]{2,1,0:T(8,128)(2,1)S(1)} %get-tuple-element.121), channel_id=1, source_target_pairs={{0,1},{1,0},{2,3},{3,2},{4,5},{5,4},{6,7},{7,6},{8,9},{9,8},{10,11... | collective-permute-start | bytes 737288 | tf_op jit(solution)/shard_map/ppermute | solution.py:446
  7.6 6.1 %collective-permute-start.11 = (bf16[4,80,384]{2,1,0:T(8,128)(2,1)S(1)}, bf16[4,80,384]{2,1,0:T(8,128)(2,1)S(1)}, u32[]{:S(2)}, u32[]{:S(2)}) collective-permute-start(bf16[4,80,384]{2,1,0:T(8,128)(2,1)S(1)} %get-tuple-element.122), channel_id=1, source_target_pairs={{1,2},{2,1},{3,4},{4,3},{5,6},{6,5},{7,8},{8,7},{9,10},{10,9},{11,... | collective-permute-start | bytes 737288 | tf_op jit(solution)/shard_map/ppermute | solution.py:449
  9.3 3.8 %collective-permute-start.14 = (bf16[1,64,128]{2,1,0:T(8,128)(2,1)S(1)}, bf16[1,64,128]{2,1,0:T(8,128)(2,1)S(1)}, u32[]{:S(2)}, u32[]{:S(2)}) collective-permute-start(bf16[1,64,128]{2,1,0:T(8,128)(2,1)S(1)} %get-tuple-element.130), channel_id=1, source_target_pairs={{0,1},{1,0},{2,3},{3,2},{4,5},{5,4},{6,7},{7,6},{8,9},{9,8},{10,11... | collective-permute-start | bytes 49160 | tf_op jit(solution)/shard_map/ppermute | solution.py:446
  14.7 6.3 %collective-permute-start.16 = (bf16[5,64,128]{2,1,0:T(8,128)(2,1)S(1)}, bf16[5,64,128]{2,1,0:T(8,128)(2,1)S(1)}, u32[]{:S(2)}, u32[]{:S(2)}) collective-permute-start(bf16[5,64,128]{2,1,0:T(8,128)(2,1)S(1)} %get-tuple-element.132.mine), channel_id=1, source_target_pairs={{0,1},{1,0},{2,3},{3,2},{4,5},{5,4},{6,7},{7,6},{8,9},{9,8},{10,11... | collective-permute-start | bytes 245768 | tf_op jit(solution)/shard_map/ppermute | solution.py:446
  23.2 6.9 %collective-permute-start.18 = (bf16[5,64,128]{2,1,0:T(8,128)(2,1)S(1)}, bf16[5,64,128]{2,1,0:T(8,128)(2,1)S(1)}, u32[]{:S(2)}, u32[]{:S(2)}) collective-permute-start(bf16[5,64,128]{2,1,0:T(8,128)(2,1)S(1)} %get-tuple-element.136.mine), channel_id=1, source_target_pairs={{0,1},{1,0},{2,3},{3,2},{4,5},{5,4},{6,7},{7,6},{8,9},{9,8},{10,11... | collective-permute-start | bytes 245768 | tf_op jit(solution)/shard_map/ppermute | solution.py:446
  30.8 0.8 collective-permute-start.19
  32.5 7.4 %collective-permute-start.20 = (bf16[5,64,128]{2,1,0:T(8,128)(2,1)S(1)}, bf16[5,64,128]{2,1,0:T(8,128)(2,1)S(1)}, u32[]{:S(2)}, u32[]{:S(2)}) collective-permute-start(bf16[5,64,128]{2,1,0:T(8,128)(2,1)S(1)} %get-tuple-element.140.mine), channel_id=1, source_target_pairs={{0,1},{1,0},{2,3},{3,2},{4,5},{5,4},{6,7},{7,6},{8,9},{9,8},{10,11... | collective-permute-start | bytes 245768 | tf_op jit(solution)/shard_map/ppermute | solution.py:446
  41.2 1.3 %collective-permute-start.21 = (f32[128,128]{1,0:T(8,128)S(1)}, f32[128,128]{1,0:T(8,128)S(1)}, u32[]{:S(2)}, u32[]{:S(2)}) collective-permute-start(f32[128,128]{1,0:T(8,128)S(1)} %broadcast_select_fusion.5), channel_id=1, source_target_pairs={{0,1},{1,0},{2,3},{3,2},{4,5},{5,4},{6,7},{7,6},{8,9},{9,8},{10,11... | collective-permute-start | bytes 196616 | tf_op jit(solution)/shard_map/ppermute | solution.py:446
  42.6 5.2 %collective-permute-start.22 = (f32[128,128]{1,0:T(8,128)S(1)}, f32[128,128]{1,0:T(8,128)S(1)}, u32[]{:S(2)}, u32[]{:S(2)}) collective-permute-start(f32[128,128]{1,0:T(8,128)S(1)} %select_add_fusion.1), channel_id=1, source_target_pairs={{0,2},{1,5},{2,0},{3,7},{4,6},{5,1},{6,4},{7,3},{8,10},{9,13},{10,... | collective-permute-start | bytes 196616 | tf_op jit(solution)/shard_map/ppermute | solution.py:456
  47.8 5.2 %collective-permute-start.23 = (f32[128,128]{1,0:T(8,128)S(1)}, f32[128,128]{1,0:T(8,128)S(1)}, u32[]{:S(2)}, u32[]{:S(2)}) collective-permute-start(f32[128,128]{1,0:T(8,128)S(1)} %add.47), channel_id=1, source_target_pairs={{0,4},{1,9},{2,6},{3,11},{4,0},{5,13},{6,2},{7,15},{8,12},{9,1},{1... | collective-permute-start | bytes 196616 | tf_op jit(solution)/shard_map/ppermute | solution.py:456
  53.0 5.2 %collective-permute-start.24 = (f32[128,128]{1,0:T(8,128)S(1)}, f32[128,128]{1,0:T(8,128)S(1)}, u32[]{:S(2)}, u32[]{:S(2)}) collective-permute-start(f32[128,128]{1,0:T(8,128)S(1)} %add.48), channel_id=1, source_target_pairs={{0,8},{1,3},{2,10},{3,1},{4,12},{5,7},{6,14},{7,5},{8,0},{9,11},{1... | collective-permute-start | bytes 196616 | tf_op jit(solution)/shard_map/ppermute | solution.py:456
  58.3 1.3 %collective-permute-start.25 = (f32[128,128]{1,0:T(8,128)S(1)}, f32[128,128]{1,0:T(8,128)S(1)}, u32[]{:S(2)}, u32[]{:S(2)}) collective-permute-start(f32[128,128]{1,0:T(8,128)S(1)} %add.49), channel_id=1, source_target_pairs={{0,1},{1,0},{2,3},{3,2},{4,5},{5,4},{6,7},{7,6},{8,9},{9,8},{10,11... | collective-permute-start | bytes 196616 | tf_op jit(solution)/shard_map/ppermute | solution.py:446
  66.8 1.2 collective-permute-start.26
  69.5 6.2 %collective-permute-start.28 = (bf16[5,64,128]{2,1,0:T(8,128)(2,1)S(1)}, bf16[5,64,128]{2,1,0:T(8,128)(2,1)S(1)}, u32[]{:S(2)}, u32[]{:S(2)}) collective-permute-start(bf16[5,64,128]{2,1,0:T(8,128)(2,1)S(1)} %get-tuple-element.160.mine), channel_id=1, source_target_pairs={{0,1},{1,0},{2,3},{3,2},{4,5},{5,4},{6,7},{7,6},{8,9},{9,8},{10,11... | collective-permute-start | bytes 245768 | tf_op jit(solution)/shard_map/ppermute | solution.py:446
  76.5 0.9 collective-permute-start.29
  78.2 6.2 %collective-permute-start.30 = (bf16[5,64,128]{2,1,0:T(8,128)(2,1)S(1)}, bf16[5,64,128]{2,1,0:T(8,128)(2,1)S(1)}, u32[]{:S(2)}, u32[]{:S(2)}) collective-permute-start(bf16[5,64,128]{2,1,0:T(8,128)(2,1)S(1)} %get-tuple-element.164.mine), channel_id=1, source_target_pairs={{0,1},{1,0},{2,3},{3,2},{4,5},{5,4},{6,7},{7,6},{8,9},{9,8},{10,11... | collective-permute-start | bytes 245768 | tf_op jit(solution)/shard_map/ppermute | solution.py:446
  86.7 7.5 %collective-permute-start.32 = (bf16[5,64,128]{2,1,0:T(8,128)(2,1)S(1)}, bf16[5,64,128]{2,1,0:T(8,128)(2,1)S(1)}, u32[]{:S(2)}, u32[]{:S(2)}) collective-permute-start(bf16[5,64,128]{2,1,0:T(8,128)(2,1)S(1)} %get-tuple-element.168.mine), channel_id=1, source_target_pairs={{0,1},{1,0},{2,3},{3,2},{4,5},{5,4},{6,7},{7,6},{8,9},{9,8},{10,11... | collective-permute-start | bytes 245768 | tf_op jit(solution)/shard_map/ppermute | solution.py:446
  95.6 1.3 %collective-permute-start.33 = (f32[128,128]{1,0:T(8,128)S(1)}, f32[128,128]{1,0:T(8,128)S(1)}, u32[]{:S(2)}, u32[]{:S(2)}) collective-permute-start(f32[128,128]{1,0:T(8,128)S(1)} %broadcast_select_fusion.2), channel_id=1, source_target_pairs={{0,1},{1,0},{2,3},{3,2},{4,5},{5,4},{6,7},{7,6},{8,9},{9,8},{10,11... | collective-permute-start | bytes 196616 | tf_op jit(solution)/shard_map/ppermute | solution.py:446
  97.0 5.2 %collective-permute-start.34 = (f32[128,128]{1,0:T(8,128)S(1)}, f32[128,128]{1,0:T(8,128)S(1)}, u32[]{:S(2)}, u32[]{:S(2)}) collective-permute-start(f32[128,128]{1,0:T(8,128)S(1)} %select_add_fusion), channel_id=1, source_target_pairs={{0,2},{1,5},{2,0},{3,7},{4,6},{5,1},{6,4},{7,3},{8,10},{9,13},{10,... | collective-permute-start | bytes 196616 | tf_op jit(solution)/shard_map/ppermute | solution.py:456
  102.2 6.0 %collective-permute-start.35 = (f32[128,128]{1,0:T(8,128)S(1)}, f32[128,128]{1,0:T(8,128)S(1)}, u32[]{:S(2)}, u32[]{:S(2)}) collective-permute-start(f32[128,128]{1,0:T(8,128)S(1)} %add.51), channel_id=1, source_target_pairs={{0,4},{1,9},{2,6},{3,11},{4,0},{5,13},{6,2},{7,15},{8,12},{9,1},{1... | collective-permute-start | bytes 196616 | tf_op jit(solution)/shard_map/ppermute | solution.py:456
  108.2 5.2 %collective-permute-start.36 = (f32[128,128]{1,0:T(8,128)S(1)}, f32[128,128]{1,0:T(8,128)S(1)}, u32[]{:S(2)}, u32[]{:S(2)}) collective-permute-start(f32[128,128]{1,0:T(8,128)S(1)} %add.52), channel_id=1, source_target_pairs={{0,8},{1,3},{2,10},{3,1},{4,12},{5,7},{6,14},{7,5},{8,0},{9,11},{1... | collective-permute-start | bytes 196616 | tf_op jit(solution)/shard_map/ppermute | solution.py:456
  113.4 1.3 %collective-permute-start.37 = (f32[128,128]{1,0:T(8,128)S(1)}, f32[128,128]{1,0:T(8,128)S(1)}, u32[]{:S(2)}, u32[]{:S(2)}) collective-permute-start(f32[128,128]{1,0:T(8,128)S(1)} %add.53), channel_id=1, source_target_pairs={{0,1},{1,0},{2,3},{3,2},{4,5},{5,4},{6,7},{7,6},{8,9},{9,8},{10,11... | collective-permute-start | bytes 196616 | tf_op jit(solution)/shard_map/ppermute | solution.py:446
  (9 other events, 22.9 us)

commit v4 on v3

--- a/solution.py
+++ b/solution.py
@@ -339,25 +339,36 @@
     high[...], low[...] = split(jnp.concatenate(columns, axis=1))
 
 
+def times(mix_high, mix_low, high, low):
+    width = mix_high.shape[1]
+    out = jnp.dot(high, jnp.concatenate([mix_high, mix_low], axis=1), preferred_element_type=F32)
+    return out[:, :width] + out[:, width:] + jnp.dot(low, mix_high, preferred_element_type=F32)
+
+
 def combined(mix, high, low, shape):
-    mix_high, mix_low = split(mix)
-    width = mix.shape[1]
-    out = jnp.dot(high[...], jnp.concatenate([mix_high, mix_low], axis=1), preferred_element_type=F32)
-    out = out[:, :width] + out[:, width:] + jnp.dot(low[...], mix_high, preferred_element_type=F32)
+    out = times(*split(mix), high[...], low[...])
     return out[:, :RHS].reshape(shape), out[:, RHS:].reshape(shape)
 
 
-def update_kernel(lists, left, right, high, low, x, new_x, r, blocks, own, to_chip, doubt, ext):
-    count = x.shape[0]
+def mix_kernel(lists, left, right, high, low, mix_high, mix_low, to_chip, doubt):
     mix, found = mixing(left, right)
     doubt[...] = jnp.broadcast_to(found, doubt.shape)
-    step, r[...] = combined(mix, high, low, x.shape)
-    new_x[...] = x[...] + step
-    pack(own, [r[e] for e in range(count)])
+    mix_high[...], mix_low[...] = split(mix)
+    count, slots = high.shape[0] // DOF, lists.shape[1] // 2
+    places = [lists[0, s] for s in range(slots)]
+    starts = [pl.multiple_of(jnp.minimum(place, count - 1) * DOF, DOF) for place in places]
+    rows = [jnp.concatenate([part[pl.ds(start, DOF), :] for start in starts], axis=0) for part in (high, low)]
+    out = times(mix_high[...], mix_low[...], *rows)[:, RHS:]
+    blocks = [out[DOF * s : DOF * s + DOF] for s in range(slots)]
+    pack(to_chip, [jnp.where(place < count, block, 0.0) for place, block in zip(places, blocks)])
+
+
+def update_kernel(mix_high, mix_low, high, low, x, new_x, r, blocks, own):
+    out = times(mix_high[...], mix_low[...], high[...], low[...])
+    new_x[...] = x[...] + out[:, :RHS].reshape(x.shape)
+    r[...] = out[:, RHS:].reshape(x.shape)
+    pack(own, [r[e] for e in range(x.shape[0])])
     blocks[...] = r[...].astype(BF16)
-    ext[:count] = blocks[...]
-    ext[count] = jnp.zeros(ext.shape[1:], BF16)
-    pack(to_chip, listed(lists, 0, ext))
 
 
 def finish_kernel(left, right, high, low, x, earlier, first_r, first_x, new_x, r, repeats):
@@ -495,13 +506,9 @@
         parts = [shape(BF16, count * DOF, width)] * 2
         return call(stack_kernel, parts, [VMEM] * len(fields), "stack")(*fields)
 
-    update = call(
-        update_kernel,
-        [field, field, blocks_shape, own_message, slot_message, doubt_shape],
-        [VMEM] * 6,
-        "solve_update",
-        count + 1,
-    )
+    mix_shape = shape(BF16, (POWERS + 2) * RHS, 2 * RHS)
+    mix = call(mix_kernel, [mix_shape, mix_shape, slot_message, doubt_shape], [VMEM] * 5, "solve")
+    update = call(update_kernel, [field, field, blocks_shape, own_message], [VMEM] * 5, "update")
     flat = shape(F32, *right_side.shape)
     finish = call(finish_kernel, [flat, flat, shape(jnp.int32, 1)], [VMEM] * 8, "solve_finish", last=SMEM)
 
@@ -537,7 +544,9 @@
         if group == 0:
             first_r = r
         if group + 1 < CYCLES // MERGED:
-            x, r, blocks, own, to_chip, doubt = update(lists, *sums, *stacked(fields), x)
+            parts = stacked(fields)
+            mix_high, mix_low, to_chip, doubt = mix(lists, *sums, *parts)
+            x, r, blocks, own = update(mix_high, mix_low, *parts, x)
         else:
             x, r, repeats = finish(*sums, *stacked(fields), x, doubt, first_r, first_x)
 

time: 125 us -> 124 us (level)
    pallas_call x1 -> x2, Pallas kernels: 7.19 us -> 7.38 us  [the longest x1 6.54 us: shards(): mix_high, mix_low, to_chip, doubt = mix(lists, *sums, *parts)]
  transfers between devices with their start and end apart: 28 -> 28, of which waited for: 16 -> 16; matrix products, arithmetic and copies ran while one was open for 0% -> 0% of each run, Pallas kernels for 4% -> 5%
where the time goes in v4:
time: 124 us
  starting transfers between devices  64.5 us (52%)
  Pallas kernels  32.7 us (26%)
  waiting for transfers between devices  23.5 us (19%)
    ppermute x14, starting transfers between devices, chip(): return lax.ppermute(value, AXES, chip_pairs)  42.6 us
    ppermute x6, starting transfers between devices, total(): value = value + lax.ppermute(value, AXES, pairs)  16.2 us
    ppermute x6, waiting for transfers between devices, total(): value = value + lax.ppermute(value, AXES, pairs)  15.8 us
    pallas_call x1, Pallas kernels, shards(): x, r, repeats = finish(*sums, *stacked(fields), x, doubt, first_r, first_x)  8.23 us
    ppermute x14, waiting for transfers between devices, chip(): return lax.ppermute(value, AXES, chip_pairs)  7.73 us
    pallas_call x1, Pallas kernels, shards(): mix_high, mix_low, to_chip, doubt = mix(lists, *sums, *parts)  6.54 us
    ppermute x8, starting transfers between devices, link(): return lax.ppermute(value, AXES, link_pairs)  5.67 us
    pallas_call x6, Pallas kernels, shards(): power(link_table, kept, link_rows, blocks, mine, link(mine))  4.76 us
  transfers between devices with their start and end apart: 28, of which 16 were waited for; matrix products, arithmetic and copies ran while one was open for 0% of the time, Pallas kernels for 5%

profile of v4, /device:TPU:0, one launch (start us, length us, event | category | flops | bytes accessed | tf_op | source)
XLA Modules:
  0.0 123.9 jit_solution(3735284644862064392)
XLA Ops:
  0.6 1.4 %prepare.1 = (f32[16,64,32]{2,1,0:T(8,128)S(1)}, bf16[16,64,384]{2,1,0:T(8,128)(2,1)S(1)}, bf16[1,64,128]{2,1,0:T(8,128)(2,1)S(1)}, bf16[1,64,128]{2,1,0:T(8,128)(2,1)S(1)}) custom-call(s32[1,2,4]{2,1,0:T(2,128)} %send_lists.1, f32[16,2048]{1,0:T(8,128)} %guess.1, bf16[16,64,384]{2,1,0:T(8,128)(2,1)} %couple.1), custom_call_target="tpu_custom_call" | custom-call | tf_op jit(solution)/shard_map/prepare/pallas_call | solution.py:517
  2.8 4.4 %collective-permute-start.12 = (bf16[1,64,128]{2,1,0:T(8,128)(2,1)S(1)}, bf16[1,64,128]{2,1,0:T(8,128)(2,1)S(1)}, u32[]{:S(2)}, u32[]{:S(2)}) collective-permute-start(bf16[1,64,128]{2,1,0:T(8,128)(2,1)S(1)} %get-tuple-element.214), channel_id=1, source_target_pairs={{0,1},{1,0},{2,3},{3,2},{4,5},{5,4},{6,7},{7,6},{8,9},{9,8},{10,11... | collective-permute-start | bytes 49160 | tf_op jit(solution)/shard_map/ppermute | solution.py:457
  9.3 2.9 %collective-permute-start.14 = (bf16[1,64,128]{2,1,0:T(8,128)(2,1)S(1)}, bf16[1,64,128]{2,1,0:T(8,128)(2,1)S(1)}, u32[]{:S(2)}, u32[]{:S(2)}) collective-permute-start(bf16[1,64,128]{2,1,0:T(8,128)(2,1)S(1)} %get-tuple-element.132), channel_id=1, source_target_pairs={{0,1},{1,0},{2,3},{3,2},{4,5},{5,4},{6,7},{7,6},{8,9},{9,8},{10,11... | collective-permute-start | bytes 49160 | tf_op jit(solution)/shard_map/ppermute | solution.py:457
  14.7 5.3 %collective-permute-start.16 = (bf16[5,64,128]{2,1,0:T(8,128)(2,1)S(1)}, bf16[5,64,128]{2,1,0:T(8,128)(2,1)S(1)}, u32[]{:S(2)}, u32[]{:S(2)}) collective-permute-start(bf16[5,64,128]{2,1,0:T(8,128)(2,1)S(1)} %get-tuple-element.134.mine), channel_id=1, source_target_pairs={{0,1},{1,0},{2,3},{3,2},{4,5},{5,4},{6,7},{7,6},{8,9},{9,8},{10,11... | collective-permute-start | bytes 245768 | tf_op jit(solution)/shard_map/ppermute | solution.py:457
  23.2 5.9 %collective-permute-start.18 = (bf16[5,64,128]{2,1,0:T(8,128)(2,1)S(1)}, bf16[5,64,128]{2,1,0:T(8,128)(2,1)S(1)}, u32[]{:S(2)}, u32[]{:S(2)}) collective-permute-start(bf16[5,64,128]{2,1,0:T(8,128)(2,1)S(1)} %get-tuple-element.138.mine), channel_id=1, source_target_pairs={{0,1},{1,0},{2,3},{3,2},{4,5},{5,4},{6,7},{7,6},{8,9},{9,8},{10,11... | collective-permute-start | bytes 245768 | tf_op jit(solution)/shard_map/ppermute | solution.py:457
  32.5 6.2 %collective-permute-start.20 = (bf16[5,64,128]{2,1,0:T(8,128)(2,1)S(1)}, bf16[5,64,128]{2,1,0:T(8,128)(2,1)S(1)}, u32[]{:S(2)}, u32[]{:S(2)}) collective-permute-start(bf16[5,64,128]{2,1,0:T(8,128)(2,1)S(1)} %get-tuple-element.142.mine), channel_id=1, source_target_pairs={{0,1},{1,0},{2,3},{3,2},{4,5},{5,4},{6,7},{7,6},{8,9},{9,8},{10,11... | collective-permute-start | bytes 245768 | tf_op jit(solution)/shard_map/ppermute | solution.py:457
  39.8 1.4 %power_and_gram.2 = (f32[16,64,32]{2,1,0:T(8,128)S(1)}, f32[128,128]{1,0:T(8,128)S(1)}, f32[128,128]{1,0:T(8,128)S(1)}) custom-call(s32[20,128]{1,0:T(8,128)S(1)} %get-tuple-element.125.table, bf16[16,64,384]{2,1,0:T(8,128)(2,1)S(1)} %get-tuple-element.122.couple, bf16[16,64,32]{2,1,0:T(8,128)(2,1)S(1)} %get-tuple-element.141.blocks, ...), custom_call_target="tpu_custom_call" | custom-call | tf_op jit(solution)/shard_map/power_and_gram/pallas_call | solution.py:541
  42.6 2.9 %collective-permute-start.22 = (f32[128,128]{1,0:T(8,128)S(1)}, f32[128,128]{1,0:T(8,128)S(1)}, u32[]{:S(2)}, u32[]{:S(2)}) collective-permute-start(f32[128,128]{1,0:T(8,128)S(1)} %select_add_fusion.1), channel_id=1, source_target_pairs={{0,2},{1,5},{2,0},{3,7},{4,6},{5,1},{6,4},{7,3},{8,10},{9,13},{10,... | collective-permute-start | bytes 196616 | tf_op jit(solution)/shard_map/ppermute | solution.py:467
  45.5 2.2 %collective-permute-done.22 = f32[128,128]{1,0:T(8,128)S(1)} collective-permute-done((f32[128,128]{1,0:T(8,128)S(1)}, f32[128,128]{1,0:T(8,128)S(1)}, u32[]{:S(2)}, u32[]{:S(2)}) %collective-permute-start.22) | collective-permute-done | bytes 65568 | tf_op jit(solution)/shard_map/ppermute | solution.py:467
  47.8 2.5 %collective-permute-start.23 = (f32[128,128]{1,0:T(8,128)S(1)}, f32[128,128]{1,0:T(8,128)S(1)}, u32[]{:S(2)}, u32[]{:S(2)}) collective-permute-start(f32[128,128]{1,0:T(8,128)S(1)} %add.47), channel_id=1, source_target_pairs={{0,4},{1,9},{2,6},{3,11},{4,0},{5,13},{6,2},{7,15},{8,12},{9,1},{1... | collective-permute-start | bytes 196616 | tf_op jit(solution)/shard_map/ppermute | solution.py:467
  50.3 2.8 %collective-permute-done.23 = f32[128,128]{1,0:T(8,128)S(1)} collective-permute-done((f32[128,128]{1,0:T(8,128)S(1)}, f32[128,128]{1,0:T(8,128)S(1)}, u32[]{:S(2)}, u32[]{:S(2)}) %collective-permute-start.23) | collective-permute-done | bytes 65568 | tf_op jit(solution)/shard_map/ppermute | solution.py:467
  53.0 2.6 %collective-permute-start.24 = (f32[128,128]{1,0:T(8,128)S(1)}, f32[128,128]{1,0:T(8,128)S(1)}, u32[]{:S(2)}, u32[]{:S(2)}) collective-permute-start(f32[128,128]{1,0:T(8,128)S(1)} %add.48), channel_id=1, source_target_pairs={{0,8},{1,3},{2,10},{3,1},{4,12},{5,7},{6,14},{7,5},{8,0},{9,11},{1... | collective-permute-start | bytes 196616 | tf_op jit(solution)/shard_map/ppermute | solution.py:467
  55.6 2.7 %collective-permute-done.24 = f32[128,128]{1,0:T(8,128)S(1)} collective-permute-done((f32[128,128]{1,0:T(8,128)S(1)}, f32[128,128]{1,0:T(8,128)S(1)}, u32[]{:S(2)}, u32[]{:S(2)}) %collective-permute-start.24) | collective-permute-done | bytes 65568 | tf_op jit(solution)/shard_map/ppermute | solution.py:467
  59.6 6.5 %solve.1 = (bf16[256,64]{1,0:T(8,128)(2,1)S(1)}, bf16[256,64]{1,0:T(8,128)(2,1)S(1)}, bf16[1,64,128]{2,1,0:T(8,128)(2,1)S(1)}, f32[8,128]{1,0:T(8,128)S(1)}) custom-call(s32[1,8]{1,0:T(1,128)S(1)} %reshape.22.lists, f32[128,128]{1,0:T(8,128)S(1)} %get-tuple-element.212.left, f32[128,128]{1,0:T(8,128)S(1)} %get-tuple-element.211.right, ...), custom_call_target="tpu_custom_call" | custom-call | tf_op jit(solution)/shard_map/solve/pallas_call | solution.py:548
  68.9 5.3 %collective-permute-start.28 = (bf16[5,64,128]{2,1,0:T(8,128)(2,1)S(1)}, bf16[5,64,128]{2,1,0:T(8,128)(2,1)S(1)}, u32[]{:S(2)}, u32[]{:S(2)}) collective-permute-start(bf16[5,64,128]{2,1,0:T(8,128)(2,1)S(1)} %get-tuple-element.164.mine), channel_id=1, source_target_pairs={{0,1},{1,0},{2,3},{3,2},{4,5},{5,4},{6,7},{7,6},{8,9},{9,8},{10,11... | collective-permute-start | bytes 245768 | tf_op jit(solution)/shard_map/ppermute | solution.py:457
  77.6 5.3 %collective-permute-start.30 = (bf16[5,64,128]{2,1,0:T(8,128)(2,1)S(1)}, bf16[5,64,128]{2,1,0:T(8,128)(2,1)S(1)}, u32[]{:S(2)}, u32[]{:S(2)}) collective-permute-start(bf16[5,64,128]{2,1,0:T(8,128)(2,1)S(1)} %get-tuple-element.168.mine), channel_id=1, source_target_pairs={{0,1},{1,0},{2,3},{3,2},{4,5},{5,4},{6,7},{7,6},{8,9},{9,8},{10,11... | collective-permute-start | bytes 245768 | tf_op jit(solution)/shard_map/ppermute | solution.py:457
  86.1 6.4 %collective-permute-start.32 = (bf16[5,64,128]{2,1,0:T(8,128)(2,1)S(1)}, bf16[5,64,128]{2,1,0:T(8,128)(2,1)S(1)}, u32[]{:S(2)}, u32[]{:S(2)}) collective-permute-start(bf16[5,64,128]{2,1,0:T(8,128)(2,1)S(1)} %get-tuple-element.172.mine), channel_id=1, source_target_pairs={{0,1},{1,0},{2,3},{3,2},{4,5},{5,4},{6,7},{7,6},{8,9},{9,8},{10,11... | collective-permute-start | bytes 245768 | tf_op jit(solution)/shard_map/ppermute | solution.py:457
  96.3 2.9 %collective-permute-start.34 = (f32[128,128]{1,0:T(8,128)S(1)}, f32[128,128]{1,0:T(8,128)S(1)}, u32[]{:S(2)}, u32[]{:S(2)}) collective-permute-start(f32[128,128]{1,0:T(8,128)S(1)} %select_add_fusion), channel_id=1, source_target_pairs={{0,2},{1,5},{2,0},{3,7},{4,6},{5,1},{6,4},{7,3},{8,10},{9,13},{10,... | collective-permute-start | bytes 196616 | tf_op jit(solution)/shard_map/ppermute | solution.py:467
  99.3 2.2 %collective-permute-done.34 = f32[128,128]{1,0:T(8,128)S(1)} collective-permute-done((f32[128,128]{1,0:T(8,128)S(1)}, f32[128,128]{1,0:T(8,128)S(1)}, u32[]{:S(2)}, u32[]{:S(2)}) %collective-permute-start.34) | collective-permute-done | bytes 65568 | tf_op jit(solution)/shard_map/ppermute | solution.py:467
  101.5 3.0 %collective-permute-start.35 = (f32[128,128]{1,0:T(8,128)S(1)}, f32[128,128]{1,0:T(8,128)S(1)}, u32[]{:S(2)}, u32[]{:S(2)}) collective-permute-start(f32[128,128]{1,0:T(8,128)S(1)} %add.51), channel_id=1, source_target_pairs={{0,4},{1,9},{2,6},{3,11},{4,0},{5,13},{6,2},{7,15},{8,12},{9,1},{1... | collective-permute-start | bytes 196616 | tf_op jit(solution)/shard_map/ppermute | solution.py:467
  104.5 2.9 %collective-permute-done.35 = f32[128,128]{1,0:T(8,128)S(1)} collective-permute-done((f32[128,128]{1,0:T(8,128)S(1)}, f32[128,128]{1,0:T(8,128)S(1)}, u32[]{:S(2)}, u32[]{:S(2)}) %collective-permute-start.35) | collective-permute-done | bytes 65568 | tf_op jit(solution)/shard_map/ppermute | solution.py:467
  107.5 2.3 %collective-permute-start.36 = (f32[128,128]{1,0:T(8,128)S(1)}, f32[128,128]{1,0:T(8,128)S(1)}, u32[]{:S(2)}, u32[]{:S(2)}) collective-permute-start(f32[128,128]{1,0:T(8,128)S(1)} %add.52), channel_id=1, source_target_pairs={{0,8},{1,3},{2,10},{3,1},{4,12},{5,7},{6,14},{7,5},{8,0},{9,11},{1... | collective-permute-start | bytes 196616 | tf_op jit(solution)/shard_map/ppermute | solution.py:467
  109.8 2.9 %collective-permute-done.36 = f32[128,128]{1,0:T(8,128)S(1)} collective-permute-done((f32[128,128]{1,0:T(8,128)S(1)}, f32[128,128]{1,0:T(8,128)S(1)}, u32[]{:S(2)}, u32[]{:S(2)}) %collective-permute-start.36) | collective-permute-done | bytes 65568 | tf_op jit(solution)/shard_map/ppermute | solution.py:467
  114.1 8.2 %solve_finish.1 = (f32[16,2048]{1,0:T(8,128)}, f32[16,2048]{1,0:T(8,128)S(1)}, s32[1]{0:T(128)}) custom-call(f32[128,128]{1,0:T(8,128)S(1)} %get-tuple-element.210.left, f32[128,128]{1,0:T(8,128)S(1)} %get-tuple-element.209.right, bf16[1024,256]{1,0:T(8,128)(2,1)S(1)} %get-tuple-element.186.high, bf16[1024,256]{1,0:T(8,128)(2,1)S(1)} %get-tuple-element.187.low, ...), custom_call_target="tpu_custom_call" | custom-call | tf_op jit(solution)/shard_map/solve_finish/pallas_call | solution.py:551
  (91 shorter events, 31.5 us)
Async XLA Ops:
  2.1 6.4 %collective-permute-start.13 = (bf16[1,64,128]{2,1,0:T(8,128)(2,1)S(1)}, bf16[1,64,128]{2,1,0:T(8,128)(2,1)S(1)}, u32[]{:S(2)}, u32[]{:S(2)}) collective-permute-start(bf16[1,64,128]{2,1,0:T(8,128)(2,1)S(1)} %get-tuple-element.213), channel_id=1, source_target_pairs={{1,2},{2,1},{3,4},{4,3},{5,6},{6,5},{7,8},{8,7},{9,10},{10,9},{11,... | collective-permute-start | bytes 49160 | tf_op jit(solution)/shard_map/ppermute | solution.py:460
  2.8 5.7 %collective-permute-start.12 = (bf16[1,64,128]{2,1,0:T(8,128)(2,1)S(1)}, bf16[1,64,128]{2,1,0:T(8,128)(2,1)S(1)}, u32[]{:S(2)}, u32[]{:S(2)}) collective-permute-start(bf16[1,64,128]{2,1,0:T(8,128)(2,1)S(1)} %get-tuple-element.214), channel_id=1, source_target_pairs={{0,1},{1,0},{2,3},{3,2},{4,5},{5,4},{6,7},{7,6},{8,9},{9,8},{10,11... | collective-permute-start | bytes 49160 | tf_op jit(solution)/shard_map/ppermute | solution.py:457
  7.5 6.2 %collective-permute-start.10 = (bf16[4,80,384]{2,1,0:T(8,128)(2,1)S(1)}, bf16[4,80,384]{2,1,0:T(8,128)(2,1)S(1)}, u32[]{:S(2)}, u32[]{:S(2)}) collective-permute-start(bf16[4,80,384]{2,1,0:T(8,128)(2,1)S(1)} %get-tuple-element.123), channel_id=1, source_target_pairs={{0,1},{1,0},{2,3},{3,2},{4,5},{5,4},{6,7},{7,6},{8,9},{9,8},{10,11... | collective-permute-start | bytes 737288 | tf_op jit(solution)/shard_map/ppermute | solution.py:457
  7.6 6.1 %collective-permute-start.11 = (bf16[4,80,384]{2,1,0:T(8,128)(2,1)S(1)}, bf16[4,80,384]{2,1,0:T(8,128)(2,1)S(1)}, u32[]{:S(2)}, u32[]{:S(2)}) collective-permute-start(bf16[4,80,384]{2,1,0:T(8,128)(2,1)S(1)} %get-tuple-element.124), channel_id=1, source_target_pairs={{1,2},{2,1},{3,4},{4,3},{5,6},{6,5},{7,8},{8,7},{9,10},{10,9},{11,... | collective-permute-start | bytes 737288 | tf_op jit(solution)/shard_map/ppermute | solution.py:460
  9.3 3.8 %collective-permute-start.14 = (bf16[1,64,128]{2,1,0:T(8,128)(2,1)S(1)}, bf16[1,64,128]{2,1,0:T(8,128)(2,1)S(1)}, u32[]{:S(2)}, u32[]{:S(2)}) collective-permute-start(bf16[1,64,128]{2,1,0:T(8,128)(2,1)S(1)} %get-tuple-element.132), channel_id=1, source_target_pairs={{0,1},{1,0},{2,3},{3,2},{4,5},{5,4},{6,7},{7,6},{8,9},{9,8},{10,11... | collective-permute-start | bytes 49160 | tf_op jit(solution)/shard_map/ppermute | solution.py:457
  14.7 6.3 %collective-permute-start.16 = (bf16[5,64,128]{2,1,0:T(8,128)(2,1)S(1)}, bf16[5,64,128]{2,1,0:T(8,128)(2,1)S(1)}, u32[]{:S(2)}, u32[]{:S(2)}) collective-permute-start(bf16[5,64,128]{2,1,0:T(8,128)(2,1)S(1)} %get-tuple-element.134.mine), channel_id=1, source_target_pairs={{0,1},{1,0},{2,3},{3,2},{4,5},{5,4},{6,7},{7,6},{8,9},{9,8},{10,11... | collective-permute-start | bytes 245768 | tf_op jit(solution)/shard_map/ppermute | solution.py:457
  23.2 6.9 %collective-permute-start.18 = (bf16[5,64,128]{2,1,0:T(8,128)(2,1)S(1)}, bf16[5,64,128]{2,1,0:T(8,128)(2,1)S(1)}, u32[]{:S(2)}, u32[]{:S(2)}) collective-permute-start(bf16[5,64,128]{2,1,0:T(8,128)(2,1)S(1)} %get-tuple-element.138.mine), channel_id=1, source_target_pairs={{0,1},{1,0},{2,3},{3,2},{4,5},{5,4},{6,7},{7,6},{8,9},{9,8},{10,11... | collective-permute-start | bytes 245768 | tf_op jit(solution)/shard_map/ppermute | solution.py:457
  30.8 0.8 collective-permute-start.19
  32.5 7.4 %collective-permute-start.20 = (bf16[5,64,128]{2,1,0:T(8,128)(2,1)S(1)}, bf16[5,64,128]{2,1,0:T(8,128)(2,1)S(1)}, u32[]{:S(2)}, u32[]{:S(2)}) collective-permute-start(bf16[5,64,128]{2,1,0:T(8,128)(2,1)S(1)} %get-tuple-element.142.mine), channel_id=1, source_target_pairs={{0,1},{1,0},{2,3},{3,2},{4,5},{5,4},{6,7},{7,6},{8,9},{9,8},{10,11... | collective-permute-start | bytes 245768 | tf_op jit(solution)/shard_map/ppermute | solution.py:457
  41.2 1.3 %collective-permute-start.21 = (f32[128,128]{1,0:T(8,128)S(1)}, f32[128,128]{1,0:T(8,128)S(1)}, u32[]{:S(2)}, u32[]{:S(2)}) collective-permute-start(f32[128,128]{1,0:T(8,128)S(1)} %broadcast_select_fusion.5), channel_id=1, source_target_pairs={{0,1},{1,0},{2,3},{3,2},{4,5},{5,4},{6,7},{7,6},{8,9},{9,8},{10,11... | collective-permute-start | bytes 196616 | tf_op jit(solution)/shard_map/ppermute | solution.py:457
  42.6 5.2 %collective-permute-start.22 = (f32[128,128]{1,0:T(8,128)S(1)}, f32[128,128]{1,0:T(8,128)S(1)}, u32[]{:S(2)}, u32[]{:S(2)}) collective-permute-start(f32[128,128]{1,0:T(8,128)S(1)} %select_add_fusion.1), channel_id=1, source_target_pairs={{0,2},{1,5},{2,0},{3,7},{4,6},{5,1},{6,4},{7,3},{8,10},{9,13},{10,... | collective-permute-start | bytes 196616 | tf_op jit(solution)/shard_map/ppermute | solution.py:467
  47.8 5.3 %collective-permute-start.23 = (f32[128,128]{1,0:T(8,128)S(1)}, f32[128,128]{1,0:T(8,128)S(1)}, u32[]{:S(2)}, u32[]{:S(2)}) collective-permute-start(f32[128,128]{1,0:T(8,128)S(1)} %add.47), channel_id=1, source_target_pairs={{0,4},{1,9},{2,6},{3,11},{4,0},{5,13},{6,2},{7,15},{8,12},{9,1},{1... | collective-permute-start | bytes 196616 | tf_op jit(solution)/shard_map/ppermute | solution.py:467
  53.0 5.2 %collective-permute-start.24 = (f32[128,128]{1,0:T(8,128)S(1)}, f32[128,128]{1,0:T(8,128)S(1)}, u32[]{:S(2)}, u32[]{:S(2)}) collective-permute-start(f32[128,128]{1,0:T(8,128)S(1)} %add.48), channel_id=1, source_target_pairs={{0,8},{1,3},{2,10},{3,1},{4,12},{5,7},{6,14},{7,5},{8,0},{9,11},{1... | collective-permute-start | bytes 196616 | tf_op jit(solution)/shard_map/ppermute | solution.py:467
  58.3 1.3 %collective-permute-start.25 = (f32[128,128]{1,0:T(8,128)S(1)}, f32[128,128]{1,0:T(8,128)S(1)}, u32[]{:S(2)}, u32[]{:S(2)}) collective-permute-start(f32[128,128]{1,0:T(8,128)S(1)} %add.49), channel_id=1, source_target_pairs={{0,1},{1,0},{2,3},{3,2},{4,5},{5,4},{6,7},{7,6},{8,9},{9,8},{10,11... | collective-permute-start | bytes 196616 | tf_op jit(solution)/shard_map/ppermute | solution.py:457
  66.2 1.2 %collective-permute-start.26 = (bf16[1,64,128]{2,1,0:T(8,128)(2,1)S(1)}, bf16[1,64,128]{2,1,0:T(8,128)(2,1)S(1)}, u32[]{:S(2)}, u32[]{:S(2)}) collective-permute-start(bf16[1,64,128]{2,1,0:T(8,128)(2,1)S(1)} %get-tuple-element.162), channel_id=1, source_target_pairs={{0,1},{1,0},{2,3},{3,2},{4,5},{5,4},{6,7},{7,6},{8,9},{9,8},{10,11... | collective-permute-start | bytes 49160 | tf_op jit(solution)/shard_map/ppermute | solution.py:457
  68.9 6.3 %collective-permute-start.28 = (bf16[5,64,128]{2,1,0:T(8,128)(2,1)S(1)}, bf16[5,64,128]{2,1,0:T(8,128)(2,1)S(1)}, u32[]{:S(2)}, u32[]{:S(2)}) collective-permute-start(bf16[5,64,128]{2,1,0:T(8,128)(2,1)S(1)} %get-tuple-element.164.mine), channel_id=1, source_target_pairs={{0,1},{1,0},{2,3},{3,2},{4,5},{5,4},{6,7},{7,6},{8,9},{9,8},{10,11... | collective-permute-start | bytes 245768 | tf_op jit(solution)/shard_map/ppermute | solution.py:457
  75.9 0.9 collective-permute-start.29
  77.6 6.2 %collective-permute-start.30 = (bf16[5,64,128]{2,1,0:T(8,128)(2,1)S(1)}, bf16[5,64,128]{2,1,0:T(8,128)(2,1)S(1)}, u32[]{:S(2)}, u32[]{:S(2)}) collective-permute-start(bf16[5,64,128]{2,1,0:T(8,128)(2,1)S(1)} %get-tuple-element.168.mine), channel_id=1, source_target_pairs={{0,1},{1,0},{2,3},{3,2},{4,5},{5,4},{6,7},{7,6},{8,9},{9,8},{10,11... | collective-permute-start | bytes 245768 | tf_op jit(solution)/shard_map/ppermute | solution.py:457
  86.1 7.5 %collective-permute-start.32 = (bf16[5,64,128]{2,1,0:T(8,128)(2,1)S(1)}, bf16[5,64,128]{2,1,0:T(8,128)(2,1)S(1)}, u32[]{:S(2)}, u32[]{:S(2)}) collective-permute-start(bf16[5,64,128]{2,1,0:T(8,128)(2,1)S(1)} %get-tuple-element.172.mine), channel_id=1, source_target_pairs={{0,1},{1,0},{2,3},{3,2},{4,5},{5,4},{6,7},{7,6},{8,9},{9,8},{10,11... | collective-permute-start | bytes 245768 | tf_op jit(solution)/shard_map/ppermute | solution.py:457
  95.0 1.3 %collective-permute-start.33 = (f32[128,128]{1,0:T(8,128)S(1)}, f32[128,128]{1,0:T(8,128)S(1)}, u32[]{:S(2)}, u32[]{:S(2)}) collective-permute-start(f32[128,128]{1,0:T(8,128)S(1)} %broadcast_select_fusion.2), channel_id=1, source_target_pairs={{0,1},{1,0},{2,3},{3,2},{4,5},{5,4},{6,7},{7,6},{8,9},{9,8},{10,11... | collective-permute-start | bytes 196616 | tf_op jit(solution)/shard_map/ppermute | solution.py:457
  96.3 5.2 %collective-permute-start.34 = (f32[128,128]{1,0:T(8,128)S(1)}, f32[128,128]{1,0:T(8,128)S(1)}, u32[]{:S(2)}, u32[]{:S(2)}) collective-permute-start(f32[128,128]{1,0:T(8,128)S(1)} %select_add_fusion), channel_id=1, source_target_pairs={{0,2},{1,5},{2,0},{3,7},{4,6},{5,1},{6,4},{7,3},{8,10},{9,13},{10,... | collective-permute-start | bytes 196616 | tf_op jit(solution)/shard_map/ppermute | solution.py:467
  101.5 6.0 %collective-permute-start.35 = (f32[128,128]{1,0:T(8,128)S(1)}, f32[128,128]{1,0:T(8,128)S(1)}, u32[]{:S(2)}, u32[]{:S(2)}) collective-permute-start(f32[128,128]{1,0:T(8,128)S(1)} %add.51), channel_id=1, source_target_pairs={{0,4},{1,9},{2,6},{3,11},{4,0},{5,13},{6,2},{7,15},{8,12},{9,1},{1... | collective-permute-start | bytes 196616 | tf_op jit(solution)/shard_map/ppermute | solution.py:467
  107.5 5.2 %collective-permute-start.36 = (f32[128,128]{1,0:T(8,128)S(1)}, f32[128,128]{1,0:T(8,128)S(1)}, u32[]{:S(2)}, u32[]{:S(2)}) collective-permute-start(f32[128,128]{1,0:T(8,128)S(1)} %add.52), channel_id=1, source_target_pairs={{0,8},{1,3},{2,10},{3,1},{4,12},{5,7},{6,14},{7,5},{8,0},{9,11},{1... | collective-permute-start | bytes 196616 | tf_op jit(solution)/shard_map/ppermute | solution.py:467
  112.8 1.3 %collective-permute-start.37 = (f32[128,128]{1,0:T(8,128)S(1)}, f32[128,128]{1,0:T(8,128)S(1)}, u32[]{:S(2)}, u32[]{:S(2)}) collective-permute-start(f32[128,128]{1,0:T(8,128)S(1)} %add.53), channel_id=1, source_target_pairs={{0,1},{1,0},{2,3},{3,2},{4,5},{5,4},{6,7},{7,6},{8,9},{9,8},{10,11... | collective-permute-start | bytes 196616 | tf_op jit(solution)/shard_map/ppermute | solution.py:457
  (9 other events, 22.9 us)

commit v5 on v4

--- a/solution.py
+++ b/solution.py
@@ -1,3 +1,5 @@
+import functools
+
 import jax
 import jax.numpy as jnp
 from jax import lax
@@ -83,40 +85,38 @@
     pack(to_link, listed(lists, 1, ext))
 
 
-def rows_kernel(lists, codes, couple, to_chip, to_link):
-    count, slots = couple.shape[0], to_chip.shape[0]
+def rows_kernel(side, lists, codes, couple, after, message):
+    count, slots = couple.shape[0], message.shape[0]
     lanes = lax.broadcasted_iota(jnp.int32, (1, LANES), 1)
-    for side, message in ((0, to_chip), (1, to_link)):
-        for s in range(slots):
-            place = lists[0, side * slots + s]
-            e = jnp.minimum(place, count - 1)
-            message[s, :DOF] = couple[e]
-            meta = jnp.where(place < count, codes[pl.ds(e, 1), :], count + 2 * slots)
-            meta = jnp.where(lanes == FACES, place, meta).astype(F32)
-            message[s, DOF:] = jnp.zeros((META, couple.shape[2]), BF16)
-            message[s, DOF:, :LANES] = jnp.broadcast_to(meta, (META, LANES)).astype(BF16)
-
-
-def tables_kernel(lists, codes, chip_rows, link_rows, chip_table, link_table):
-    count, slots = codes.shape[0], chip_rows.shape[0]
+    for s in range(slots):
+        place = lists[0, side * slots + s]
+        e = jnp.minimum(place, count - 1)
+        message[s, :DOF] = couple[e]
+        meta = jnp.where(place < count, codes[pl.ds(e, 1), :], count + 2 * slots)
+        meta = jnp.where(lanes == FACES, place, meta).astype(F32)
+        message[s, DOF:] = jnp.zeros((META, couple.shape[2]), BF16)
+        message[s, DOF:, :LANES] = jnp.broadcast_to(meta, (META, LANES)).astype(BF16)
+
+
+def table_kernel(side, lists, codes, rows, table):
+    count, slots = codes.shape[0], rows.shape[0]
     reach = count + slots
     chip_base, link_base, empty = count, count + slots, 2 * reach
-    sides = ((0, chip_table, chip_rows, link_base, chip_base), (1, link_table, link_rows, chip_base, link_base))
-    for side, table, rows, known_base, far_base in sides:
-        meta = [rows[s, DOF:, :LANES].astype(F32)[:1].astype(jnp.int32) for s in range(slots)]
-        far = [value[:, FACES : FACES + 1] for value in meta]
-        near = [lists[:, side * slots + s : side * slots + s + 1] for s in range(slots)]
-
-        def place(at, own, known, listed_at, listed_own):
-            found = jnp.where((at >= known_base) & (at < known_base + slots), at - known_base + known, empty)
-            for s in range(slots):
-                target = jnp.where(listed_at[s] < count, listed_at[s] + listed_own, empty)
-                found = jnp.where(at == far_base + s, target, found)
-            return jnp.where(at < count, at + own, found)
-
-        table[:count] = place(codes[...], 0, count, far, reach)
+    known_base, far_base = (chip_base, link_base) if side else (link_base, chip_base)
+    meta = [rows[s, DOF:, :LANES].astype(F32)[:1].astype(jnp.int32) for s in range(slots)]
+    far = [value[:, FACES : FACES + 1] for value in meta]
+    near = [lists[:, side * slots + s : side * slots + s + 1] for s in range(slots)]
+
+    def place(at, own, known, listed_at, listed_own):
+        found = jnp.where((at >= known_base) & (at < known_base + slots), at - known_base + known, empty)
         for s in range(slots):
-            table[count + s : count + s + 1] = place(meta[s], reach, reach + count, near, 0)
+            target = jnp.where(listed_at[s] < count, listed_at[s] + listed_own, empty)
+            found = jnp.where(at == far_base + s, target, found)
+        return jnp.where(at < count, at + own, found)
+
+    table[:count] = place(codes[...], 0, count, far, reach)
+    for s in range(slots):
+        table[count + s : count + s + 1] = place(meta[s], reach, reach + count, near, 0)
 
 
 def residual_kernel(lists, positions, couple, from_chip, from_link, b, x, r, blocks, own, to_chip, ext):
@@ -481,8 +481,10 @@
             pltpu.SemaphoreType.DMA((3,)),
         ],
     )
-    send_rows = call(rows_kernel, [row_message] * 2, [VMEM] * 3, "rows")
-    tables = call(tables_kernel, [table_shape] * 2, [VMEM] * 4, "tables")
+    send_rows = [
+        call(functools.partial(rows_kernel, side), [row_message], [VMEM, VMEM, VMEM, ANY], "rows") for side in (0, 1)
+    ]
+    tables = [call(functools.partial(table_kernel, side), [table_shape], [VMEM] * 3, "table") for side in (0, 1)]
     first = call(
         residual_kernel,
         [field, blocks_shape, own_message, slot_message],
@@ -522,11 +524,11 @@
     x = first_x
     from_link = link(to_link)
     from_chip = chip(to_chip)
-    chip_rows, link_rows = send_rows(lists, codes, kept)
-    link_rows = link(link_rows)
-    chip_rows = chip(chip_rows)
+    link_rows = link(send_rows[1](lists, codes, kept, to_link)[0])
     r, blocks, own, to_chip = first(lists, codes, kept, from_chip, from_link, b, x)
-    chip_table, link_table = tables(lists, codes, chip_rows, link_rows)
+    chip_rows = chip(send_rows[0](lists, codes, kept, own)[0])
+    (link_table,) = tables[1](lists, codes, link_rows)
+    (chip_table,) = tables[0](lists, codes, chip_rows)
     for group in range(CYCLES // MERGED):
         mine = jnp.concatenate([own, chip(to_chip)], axis=0)
         fields = [r]

time: 124 us -> 124 us (level)
  transfers between devices with their start and end apart: 28 -> 28, of which waited for: 16 -> 16; matrix products, arithmetic and copies ran while one was open for 0% -> 0% of each run, Pallas kernels for 5% -> 6%
where the time goes in v5:
time: 124 us; the launch traced here: 123 us
  starting transfers between devices  64 us (52%)
  Pallas kernels  32.9 us (27%)
  waiting for transfers between devices  23.2 us (19%)
    ppermute x14, starting transfers between devices, chip(): return lax.ppermute(value, AXES, chip_pairs)  42.8 us
    ppermute x6, waiting for transfers between devices, total(): value = value + lax.ppermute(value, AXES, pairs)  15.8 us
    ppermute x6, starting transfers between devices, total(): value = value + lax.ppermute(value, AXES, pairs)  15.6 us
    pallas_call x1, Pallas kernels, shards(): x, r, repeats = finish(*sums, *stacked(fields), x, doubt, first_r, first_x)  8.25 us
    ppermute x14, waiting for transfers between devices, chip(): return lax.ppermute(value, AXES, chip_pairs)  7.42 us
    pallas_call x1, Pallas kernels, shards(): mix_high, mix_low, to_chip, doubt = mix(lists, *sums, *parts)  6.54 us
    ppermute x8, starting transfers between devices, link(): return lax.ppermute(value, AXES, link_pairs)  5.67 us
    pallas_call x6, Pallas kernels, shards(): power(link_table, kept, link_rows, blocks, mine, link(mine))  4.76 us
  transfers between devices with their start and end apart: 28, of which 16 were waited for; matrix products, arithmetic and copies ran while one was open for 0% of the time, Pallas kernels for 6%

profile of v5, /device:TPU:0, one launch (start us, length us, event | category | flops | bytes accessed | tf_op | source)
XLA Modules:
  0.0 123.4 jit_solution(117573932782027965)
XLA Ops:
  0.6 1.4 %prepare.1 = (f32[16,64,32]{2,1,0:T(8,128)S(1)}, bf16[16,64,384]{2,1,0:T(8,128)(2,1)S(1)}, bf16[1,64,128]{2,1,0:T(8,128)(2,1)S(1)}, bf16[1,64,128]{2,1,0:T(8,128)(2,1)S(1)}) custom-call(s32[1,2,4]{2,1,0:T(2,128)} %send_lists.1, f32[16,2048]{1,0:T(8,128)} %guess.1, bf16[16,64,384]{2,1,0:T(8,128)(2,1)} %couple.1), custom_call_target="tpu_custom_call" | custom-call | tf_op jit(solution)/shard_map/prepare/pallas_call | solution.py:519
  5.4 5.1 %collective-permute-start.14 = (bf16[1,64,128]{2,1,0:T(8,128)(2,1)S(1)}, bf16[1,64,128]{2,1,0:T(8,128)(2,1)S(1)}, u32[]{:S(2)}, u32[]{:S(2)}) collective-permute-start(bf16[1,64,128]{2,1,0:T(8,128)(2,1)S(1)} %get-tuple-element.124), channel_id=1, source_target_pairs={{0,1},{1,0},{2,3},{3,2},{4,5},{5,4},{6,7},{7,6},{8,9},{9,8},{10,11... | collective-permute-start | bytes 49160 | tf_op jit(solution)/shard_map/ppermute | solution.py:457
  13.0 6.4 %collective-permute-start.16 = (bf16[5,64,128]{2,1,0:T(8,128)(2,1)S(1)}, bf16[5,64,128]{2,1,0:T(8,128)(2,1)S(1)}, u32[]{:S(2)}, u32[]{:S(2)}) collective-permute-start(bf16[5,64,128]{2,1,0:T(8,128)(2,1)S(1)} %get-tuple-element.126.mine), channel_id=1, source_target_pairs={{0,1},{1,0},{2,3},{3,2},{4,5},{5,4},{6,7},{7,6},{8,9},{9,8},{10,11... | collective-permute-start | bytes 245768 | tf_op jit(solution)/shard_map/ppermute | solution.py:457
  22.5 6.4 %collective-permute-start.18 = (bf16[5,64,128]{2,1,0:T(8,128)(2,1)S(1)}, bf16[5,64,128]{2,1,0:T(8,128)(2,1)S(1)}, u32[]{:S(2)}, u32[]{:S(2)}) collective-permute-start(bf16[5,64,128]{2,1,0:T(8,128)(2,1)S(1)} %get-tuple-element.130.mine), channel_id=1, source_target_pairs={{0,1},{1,0},{2,3},{3,2},{4,5},{5,4},{6,7},{7,6},{8,9},{9,8},{10,11... | collective-permute-start | bytes 245768 | tf_op jit(solution)/shard_map/ppermute | solution.py:457
  32.3 6.2 %collective-permute-start.20 = (bf16[5,64,128]{2,1,0:T(8,128)(2,1)S(1)}, bf16[5,64,128]{2,1,0:T(8,128)(2,1)S(1)}, u32[]{:S(2)}, u32[]{:S(2)}) collective-permute-start(bf16[5,64,128]{2,1,0:T(8,128)(2,1)S(1)} %get-tuple-element.134.mine), channel_id=1, source_target_pairs={{0,1},{1,0},{2,3},{3,2},{4,5},{5,4},{6,7},{7,6},{8,9},{9,8},{10,11... | collective-permute-start | bytes 245768 | tf_op jit(solution)/shard_map/ppermute | solution.py:457
  39.6 1.4 %power_and_gram.2 = (f32[16,64,32]{2,1,0:T(8,128)S(1)}, f32[128,128]{1,0:T(8,128)S(1)}, f32[128,128]{1,0:T(8,128)S(1)}) custom-call(s32[20,128]{1,0:T(8,128)S(1)} %table.2, bf16[16,64,384]{2,1,0:T(8,128)(2,1)S(1)} %get-tuple-element.118.couple, bf16[16,64,32]{2,1,0:T(8,128)(2,1)S(1)} %get-tuple-element.133.blocks, ...), custom_call_target="tpu_custom_call" | custom-call | tf_op jit(solution)/shard_map/power_and_gram/pallas_call | solution.py:543
  42.4 2.9 %collective-permute-start.22 = (f32[128,128]{1,0:T(8,128)S(1)}, f32[128,128]{1,0:T(8,128)S(1)}, u32[]{:S(2)}, u32[]{:S(2)}) collective-permute-start(f32[128,128]{1,0:T(8,128)S(1)} %select_add_fusion.1), channel_id=1, source_target_pairs={{0,2},{1,5},{2,0},{3,7},{4,6},{5,1},{6,4},{7,3},{8,10},{9,13},{10,... | collective-permute-start | bytes 196616 | tf_op jit(solution)/shard_map/ppermute | solution.py:467
  45.3 2.2 %collective-permute-done.22 = f32[128,128]{1,0:T(8,128)S(1)} collective-permute-done((f32[128,128]{1,0:T(8,128)S(1)}, f32[128,128]{1,0:T(8,128)S(1)}, u32[]{:S(2)}, u32[]{:S(2)}) %collective-permute-start.22) | collective-permute-done | bytes 65568 | tf_op jit(solution)/shard_map/ppermute | solution.py:467
  47.6 2.1 %collective-permute-start.23 = (f32[128,128]{1,0:T(8,128)S(1)}, f32[128,128]{1,0:T(8,128)S(1)}, u32[]{:S(2)}, u32[]{:S(2)}) collective-permute-start(f32[128,128]{1,0:T(8,128)S(1)} %add.47), channel_id=1, source_target_pairs={{0,4},{1,9},{2,6},{3,11},{4,0},{5,13},{6,2},{7,15},{8,12},{9,1},{1... | collective-permute-start | bytes 196616 | tf_op jit(solution)/shard_map/ppermute | solution.py:467
  49.7 2.8 %collective-permute-done.23 = f32[128,128]{1,0:T(8,128)S(1)} collective-permute-done((f32[128,128]{1,0:T(8,128)S(1)}, f32[128,128]{1,0:T(8,128)S(1)}, u32[]{:S(2)}, u32[]{:S(2)}) %collective-permute-start.23) | collective-permute-done | bytes 65568 | tf_op jit(solution)/shard_map/ppermute | solution.py:467
  52.5 2.6 %collective-permute-start.24 = (f32[128,128]{1,0:T(8,128)S(1)}, f32[128,128]{1,0:T(8,128)S(1)}, u32[]{:S(2)}, u32[]{:S(2)}) collective-permute-start(f32[128,128]{1,0:T(8,128)S(1)} %add.48), channel_id=1, source_target_pairs={{0,8},{1,3},{2,10},{3,1},{4,12},{5,7},{6,14},{7,5},{8,0},{9,11},{1... | collective-permute-start | bytes 196616 | tf_op jit(solution)/shard_map/ppermute | solution.py:467
  55.1 2.7 %collective-permute-done.24 = f32[128,128]{1,0:T(8,128)S(1)} collective-permute-done((f32[128,128]{1,0:T(8,128)S(1)}, f32[128,128]{1,0:T(8,128)S(1)}, u32[]{:S(2)}, u32[]{:S(2)}) %collective-permute-start.24) | collective-permute-done | bytes 65568 | tf_op jit(solution)/shard_map/ppermute | solution.py:467
  59.1 6.5 %solve.1 = (bf16[256,64]{1,0:T(8,128)(2,1)S(1)}, bf16[256,64]{1,0:T(8,128)(2,1)S(1)}, bf16[1,64,128]{2,1,0:T(8,128)(2,1)S(1)}, f32[8,128]{1,0:T(8,128)S(1)}) custom-call(s32[1,8]{1,0:T(1,128)S(1)} %reshape.22.lists, f32[128,128]{1,0:T(8,128)S(1)} %get-tuple-element.204.left, f32[128,128]{1,0:T(8,128)S(1)} %get-tuple-element.203.right, ...), custom_call_target="tpu_custom_call" | custom-call | tf_op jit(solution)/shard_map/solve/pallas_call | solution.py:550
  68.3 5.3 %collective-permute-start.28 = (bf16[5,64,128]{2,1,0:T(8,128)(2,1)S(1)}, bf16[5,64,128]{2,1,0:T(8,128)(2,1)S(1)}, u32[]{:S(2)}, u32[]{:S(2)}) collective-permute-start(bf16[5,64,128]{2,1,0:T(8,128)(2,1)S(1)} %get-tuple-element.156.mine), channel_id=1, source_target_pairs={{0,1},{1,0},{2,3},{3,2},{4,5},{5,4},{6,7},{7,6},{8,9},{9,8},{10,11... | collective-permute-start | bytes 245768 | tf_op jit(solution)/shard_map/ppermute | solution.py:457
  77.1 5.6 %collective-permute-start.30 = (bf16[5,64,128]{2,1,0:T(8,128)(2,1)S(1)}, bf16[5,64,128]{2,1,0:T(8,128)(2,1)S(1)}, u32[]{:S(2)}, u32[]{:S(2)}) collective-permute-start(bf16[5,64,128]{2,1,0:T(8,128)(2,1)S(1)} %get-tuple-element.160.mine), channel_id=1, source_target_pairs={{0,1},{1,0},{2,3},{3,2},{4,5},{5,4},{6,7},{7,6},{8,9},{9,8},{10,11... | collective-permute-start | bytes 245768 | tf_op jit(solution)/shard_map/ppermute | solution.py:457
  85.9 6.4 %collective-permute-start.32 = (bf16[5,64,128]{2,1,0:T(8,128)(2,1)S(1)}, bf16[5,64,128]{2,1,0:T(8,128)(2,1)S(1)}, u32[]{:S(2)}, u32[]{:S(2)}) collective-permute-start(bf16[5,64,128]{2,1,0:T(8,128)(2,1)S(1)} %get-tuple-element.164.mine), channel_id=1, source_target_pairs={{0,1},{1,0},{2,3},{3,2},{4,5},{5,4},{6,7},{7,6},{8,9},{9,8},{10,11... | collective-permute-start | bytes 245768 | tf_op jit(solution)/shard_map/ppermute | solution.py:457
  93.4 1.4 %power_and_gram.3 = (f32[16,64,32]{2,1,0:T(8,128)S(1)}, f32[128,128]{1,0:T(8,128)S(1)}, f32[128,128]{1,0:T(8,128)S(1)}) custom-call(s32[20,128]{1,0:T(8,128)S(1)} %table.2, bf16[16,64,384]{2,1,0:T(8,128)(2,1)S(1)} %get-tuple-element.118.couple, bf16[16,64,32]{2,1,0:T(8,128)(2,1)S(1)} %get-tuple-element.163.blocks, ...), custom_call_target="tpu_custom_call" | custom-call | tf_op jit(solution)/shard_map/power_and_gram/pallas_call | solution.py:543
  96.2 2.9 %collective-permute-start.34 = (f32[128,128]{1,0:T(8,128)S(1)}, f32[128,128]{1,0:T(8,128)S(1)}, u32[]{:S(2)}, u32[]{:S(2)}) collective-permute-start(f32[128,128]{1,0:T(8,128)S(1)} %select_add_fusion), channel_id=1, source_target_pairs={{0,2},{1,5},{2,0},{3,7},{4,6},{5,1},{6,4},{7,3},{8,10},{9,13},{10,... | collective-permute-start | bytes 196616 | tf_op jit(solution)/shard_map/ppermute | solution.py:467
  99.1 2.2 %collective-permute-done.34 = f32[128,128]{1,0:T(8,128)S(1)} collective-permute-done((f32[128,128]{1,0:T(8,128)S(1)}, f32[128,128]{1,0:T(8,128)S(1)}, u32[]{:S(2)}, u32[]{:S(2)}) %collective-permute-start.34) | collective-permute-done | bytes 65568 | tf_op jit(solution)/shard_map/ppermute | solution.py:467
  101.4 2.7 %collective-permute-start.35 = (f32[128,128]{1,0:T(8,128)S(1)}, f32[128,128]{1,0:T(8,128)S(1)}, u32[]{:S(2)}, u32[]{:S(2)}) collective-permute-start(f32[128,128]{1,0:T(8,128)S(1)} %add.51), channel_id=1, source_target_pairs={{0,4},{1,9},{2,6},{3,11},{4,0},{5,13},{6,2},{7,15},{8,12},{9,1},{1... | collective-permute-start | bytes 196616 | tf_op jit(solution)/shard_map/ppermute | solution.py:467
  104.0 2.9 %collective-permute-done.35 = f32[128,128]{1,0:T(8,128)S(1)} collective-permute-done((f32[128,128]{1,0:T(8,128)S(1)}, f32[128,128]{1,0:T(8,128)S(1)}, u32[]{:S(2)}, u32[]{:S(2)}) %collective-permute-start.35) | collective-permute-done | bytes 65568 | tf_op jit(solution)/shard_map/ppermute | solution.py:467
  107.0 2.3 %collective-permute-start.36 = (f32[128,128]{1,0:T(8,128)S(1)}, f32[128,128]{1,0:T(8,128)S(1)}, u32[]{:S(2)}, u32[]{:S(2)}) collective-permute-start(f32[128,128]{1,0:T(8,128)S(1)} %add.52), channel_id=1, source_target_pairs={{0,8},{1,3},{2,10},{3,1},{4,12},{5,7},{6,14},{7,5},{8,0},{9,11},{1... | collective-permute-start | bytes 196616 | tf_op jit(solution)/shard_map/ppermute | solution.py:467
  109.3 2.9 %collective-permute-done.36 = f32[128,128]{1,0:T(8,128)S(1)} collective-permute-done((f32[128,128]{1,0:T(8,128)S(1)}, f32[128,128]{1,0:T(8,128)S(1)}, u32[]{:S(2)}, u32[]{:S(2)}) %collective-permute-start.36) | collective-permute-done | bytes 65568 | tf_op jit(solution)/shard_map/ppermute | solution.py:467
  113.6 8.2 %solve_finish.1 = (f32[16,2048]{1,0:T(8,128)}, f32[16,2048]{1,0:T(8,128)S(1)}, s32[1]{0:T(128)}) custom-call(f32[128,128]{1,0:T(8,128)S(1)} %get-tuple-element.202.left, f32[128,128]{1,0:T(8,128)S(1)} %get-tuple-element.201.right, bf16[1024,256]{1,0:T(8,128)(2,1)S(1)} %get-tuple-element.178.high, bf16[1024,256]{1,0:T(8,128)(2,1)S(1)} %get-tuple-element.179.low, ...), custom_call_target="tpu_custom_call" | custom-call | tf_op jit(solution)/shard_map/solve_finish/pallas_call | solution.py:553
  (93 shorter events, 30.6 us)
Async XLA Ops:
  2.1 2.5 %collective-permute-start.10 = (bf16[1,64,128]{2,1,0:T(8,128)(2,1)S(1)}, bf16[1,64,128]{2,1,0:T(8,128)(2,1)S(1)}, u32[]{:S(2)}, u32[]{:S(2)}) collective-permute-start(bf16[1,64,128]{2,1,0:T(8,128)(2,1)S(1)} %get-tuple-element.206), channel_id=1, source_target_pairs={{0,1},{1,0},{2,3},{3,2},{4,5},{5,4},{6,7},{7,6},{8,9},{9,8},{10,11... | collective-permute-start | bytes 49160 | tf_op jit(solution)/shard_map/ppermute | solution.py:457
  2.6 2.0 %collective-permute-start.11 = (bf16[1,64,128]{2,1,0:T(8,128)(2,1)S(1)}, bf16[1,64,128]{2,1,0:T(8,128)(2,1)S(1)}, u32[]{:S(2)}, u32[]{:S(2)}) collective-permute-start(bf16[1,64,128]{2,1,0:T(8,128)(2,1)S(1)} %get-tuple-element.205.after), channel_id=1, source_target_pairs={{1,2},{2,1},{3,4},{4,3},{5,6},{6,5},{7,8},{8,7},{9,10},{10,9},{11,... | collective-permute-start | bytes 49160 | tf_op jit(solution)/shard_map/ppermute | solution.py:460
  3.7 8.4 %collective-permute-start.13 = (bf16[4,80,384]{2,1,0:T(8,128)(2,1)S(1)}, bf16[4,80,384]{2,1,0:T(8,128)(2,1)S(1)}, u32[]{:S(2)}, u32[]{:S(2)}) collective-permute-start(bf16[4,80,384]{2,1,0:T(8,128)(2,1)S(1)} %rows.3), channel_id=1, source_target_pairs={{1,2},{2,1},{3,4},{4,3},{5,6},{6,5},{7,8},{8,7},{9,10},{10,9},{11,... | collective-permute-start | bytes 737288 | tf_op jit(solution)/shard_map/ppermute | solution.py:460
  5.4 6.0 %collective-permute-start.14 = (bf16[1,64,128]{2,1,0:T(8,128)(2,1)S(1)}, bf16[1,64,128]{2,1,0:T(8,128)(2,1)S(1)}, u32[]{:S(2)}, u32[]{:S(2)}) collective-permute-start(bf16[1,64,128]{2,1,0:T(8,128)(2,1)S(1)} %get-tuple-element.124), channel_id=1, source_target_pairs={{0,1},{1,0},{2,3},{3,2},{4,5},{5,4},{6,7},{7,6},{8,9},{9,8},{10,11... | collective-permute-start | bytes 49160 | tf_op jit(solution)/shard_map/ppermute | solution.py:457
  10.7 8.7 %collective-permute-start.12 = (bf16[4,80,384]{2,1,0:T(8,128)(2,1)S(1)}, bf16[4,80,384]{2,1,0:T(8,128)(2,1)S(1)}, u32[]{:S(2)}, u32[]{:S(2)}) collective-permute-start(bf16[4,80,384]{2,1,0:T(8,128)(2,1)S(1)} %rows.2), channel_id=1, source_target_pairs={{0,1},{1,0},{2,3},{3,2},{4,5},{5,4},{6,7},{7,6},{8,9},{9,8},{10,11... | collective-permute-start | bytes 737288 | tf_op jit(solution)/shard_map/ppermute | solution.py:457
  13.0 7.3 %collective-permute-start.16 = (bf16[5,64,128]{2,1,0:T(8,128)(2,1)S(1)}, bf16[5,64,128]{2,1,0:T(8,128)(2,1)S(1)}, u32[]{:S(2)}, u32[]{:S(2)}) collective-permute-start(bf16[5,64,128]{2,1,0:T(8,128)(2,1)S(1)} %get-tuple-element.126.mine), channel_id=1, source_target_pairs={{0,1},{1,0},{2,3},{3,2},{4,5},{5,4},{6,7},{7,6},{8,9},{9,8},{10,11... | collective-permute-start | bytes 245768 | tf_op jit(solution)/shard_map/ppermute | solution.py:457
  22.5 7.3 %collective-permute-start.18 = (bf16[5,64,128]{2,1,0:T(8,128)(2,1)S(1)}, bf16[5,64,128]{2,1,0:T(8,128)(2,1)S(1)}, u32[]{:S(2)}, u32[]{:S(2)}) collective-permute-start(bf16[5,64,128]{2,1,0:T(8,128)(2,1)S(1)} %get-tuple-element.130.mine), channel_id=1, source_target_pairs={{0,1},{1,0},{2,3},{3,2},{4,5},{5,4},{6,7},{7,6},{8,9},{9,8},{10,11... | collective-permute-start | bytes 245768 | tf_op jit(solution)/shard_map/ppermute | solution.py:457
  30.6 0.8 collective-permute-start.19
  32.3 7.4 %collective-permute-start.20 = (bf16[5,64,128]{2,1,0:T(8,128)(2,1)S(1)}, bf16[5,64,128]{2,1,0:T(8,128)(2,1)S(1)}, u32[]{:S(2)}, u32[]{:S(2)}) collective-permute-start(bf16[5,64,128]{2,1,0:T(8,128)(2,1)S(1)} %get-tuple-element.134.mine), channel_id=1, source_target_pairs={{0,1},{1,0},{2,3},{3,2},{4,5},{5,4},{6,7},{7,6},{8,9},{9,8},{10,11... | collective-permute-start | bytes 245768 | tf_op jit(solution)/shard_map/ppermute | solution.py:457
  41.0 1.3 %collective-permute-start.21 = (f32[128,128]{1,0:T(8,128)S(1)}, f32[128,128]{1,0:T(8,128)S(1)}, u32[]{:S(2)}, u32[]{:S(2)}) collective-permute-start(f32[128,128]{1,0:T(8,128)S(1)} %broadcast_select_fusion.5), channel_id=1, source_target_pairs={{0,1},{1,0},{2,3},{3,2},{4,5},{5,4},{6,7},{7,6},{8,9},{9,8},{10,11... | collective-permute-start | bytes 196616 | tf_op jit(solution)/shard_map/ppermute | solution.py:457
  42.4 5.2 %collective-permute-start.22 = (f32[128,128]{1,0:T(8,128)S(1)}, f32[128,128]{1,0:T(8,128)S(1)}, u32[]{:S(2)}, u32[]{:S(2)}) collective-permute-start(f32[128,128]{1,0:T(8,128)S(1)} %select_add_fusion.1), channel_id=1, source_target_pairs={{0,2},{1,5},{2,0},{3,7},{4,6},{5,1},{6,4},{7,3},{8,10},{9,13},{10,... | collective-permute-start | bytes 196616 | tf_op jit(solution)/shard_map/ppermute | solution.py:467
  47.6 4.9 %collective-permute-start.23 = (f32[128,128]{1,0:T(8,128)S(1)}, f32[128,128]{1,0:T(8,128)S(1)}, u32[]{:S(2)}, u32[]{:S(2)}) collective-permute-start(f32[128,128]{1,0:T(8,128)S(1)} %add.47), channel_id=1, source_target_pairs={{0,4},{1,9},{2,6},{3,11},{4,0},{5,13},{6,2},{7,15},{8,12},{9,1},{1... | collective-permute-start | bytes 196616 | tf_op jit(solution)/shard_map/ppermute | solution.py:467
  52.5 5.2 %collective-permute-start.24 = (f32[128,128]{1,0:T(8,128)S(1)}, f32[128,128]{1,0:T(8,128)S(1)}, u32[]{:S(2)}, u32[]{:S(2)}) collective-permute-start(f32[128,128]{1,0:T(8,128)S(1)} %add.48), channel_id=1, source_target_pairs={{0,8},{1,3},{2,10},{3,1},{4,12},{5,7},{6,14},{7,5},{8,0},{9,11},{1... | collective-permute-start | bytes 196616 | tf_op jit(solution)/shard_map/ppermute | solution.py:467
  57.7 1.3 %collective-permute-start.25 = (f32[128,128]{1,0:T(8,128)S(1)}, f32[128,128]{1,0:T(8,128)S(1)}, u32[]{:S(2)}, u32[]{:S(2)}) collective-permute-start(f32[128,128]{1,0:T(8,128)S(1)} %add.49), channel_id=1, source_target_pairs={{0,1},{1,0},{2,3},{3,2},{4,5},{5,4},{6,7},{7,6},{8,9},{9,8},{10,11... | collective-permute-start | bytes 196616 | tf_op jit(solution)/shard_map/ppermute | solution.py:457
  65.6 1.2 %collective-permute-start.26 = (bf16[1,64,128]{2,1,0:T(8,128)(2,1)S(1)}, bf16[1,64,128]{2,1,0:T(8,128)(2,1)S(1)}, u32[]{:S(2)}, u32[]{:S(2)}) collective-permute-start(bf16[1,64,128]{2,1,0:T(8,128)(2,1)S(1)} %get-tuple-element.154), channel_id=1, source_target_pairs={{0,1},{1,0},{2,3},{3,2},{4,5},{5,4},{6,7},{7,6},{8,9},{9,8},{10,11... | collective-permute-start | bytes 49160 | tf_op jit(solution)/shard_map/ppermute | solution.py:457
  68.3 6.3 %collective-permute-start.28 = (bf16[5,64,128]{2,1,0:T(8,128)(2,1)S(1)}, bf16[5,64,128]{2,1,0:T(8,128)(2,1)S(1)}, u32[]{:S(2)}, u32[]{:S(2)}) collective-permute-start(bf16[5,64,128]{2,1,0:T(8,128)(2,1)S(1)} %get-tuple-element.156.mine), channel_id=1, source_target_pairs={{0,1},{1,0},{2,3},{3,2},{4,5},{5,4},{6,7},{7,6},{8,9},{9,8},{10,11... | collective-permute-start | bytes 245768 | tf_op jit(solution)/shard_map/ppermute | solution.py:457
  75.4 0.9 collective-permute-start.29
  77.1 6.6 %collective-permute-start.30 = (bf16[5,64,128]{2,1,0:T(8,128)(2,1)S(1)}, bf16[5,64,128]{2,1,0:T(8,128)(2,1)S(1)}, u32[]{:S(2)}, u32[]{:S(2)}) collective-permute-start(bf16[5,64,128]{2,1,0:T(8,128)(2,1)S(1)} %get-tuple-element.160.mine), channel_id=1, source_target_pairs={{0,1},{1,0},{2,3},{3,2},{4,5},{5,4},{6,7},{7,6},{8,9},{9,8},{10,11... | collective-permute-start | bytes 245768 | tf_op jit(solution)/shard_map/ppermute | solution.py:457
  85.9 7.5 %collective-permute-start.32 = (bf16[5,64,128]{2,1,0:T(8,128)(2,1)S(1)}, bf16[5,64,128]{2,1,0:T(8,128)(2,1)S(1)}, u32[]{:S(2)}, u32[]{:S(2)}) collective-permute-start(bf16[5,64,128]{2,1,0:T(8,128)(2,1)S(1)} %get-tuple-element.164.mine), channel_id=1, source_target_pairs={{0,1},{1,0},{2,3},{3,2},{4,5},{5,4},{6,7},{7,6},{8,9},{9,8},{10,11... | collective-permute-start | bytes 245768 | tf_op jit(solution)/shard_map/ppermute | solution.py:457
  94.8 1.3 %collective-permute-start.33 = (f32[128,128]{1,0:T(8,128)S(1)}, f32[128,128]{1,0:T(8,128)S(1)}, u32[]{:S(2)}, u32[]{:S(2)}) collective-permute-start(f32[128,128]{1,0:T(8,128)S(1)} %broadcast_select_fusion.2), channel_id=1, source_target_pairs={{0,1},{1,0},{2,3},{3,2},{4,5},{5,4},{6,7},{7,6},{8,9},{9,8},{10,11... | collective-permute-start | bytes 196616 | tf_op jit(solution)/shard_map/ppermute | solution.py:457
  96.2 5.2 %collective-permute-start.34 = (f32[128,128]{1,0:T(8,128)S(1)}, f32[128,128]{1,0:T(8,128)S(1)}, u32[]{:S(2)}, u32[]{:S(2)}) collective-permute-start(f32[128,128]{1,0:T(8,128)S(1)} %select_add_fusion), channel_id=1, source_target_pairs={{0,2},{1,5},{2,0},{3,7},{4,6},{5,1},{6,4},{7,3},{8,10},{9,13},{10,... | collective-permute-start | bytes 196616 | tf_op jit(solution)/shard_map/ppermute | solution.py:467
  101.4 5.6 %collective-permute-start.35 = (f32[128,128]{1,0:T(8,128)S(1)}, f32[128,128]{1,0:T(8,128)S(1)}, u32[]{:S(2)}, u32[]{:S(2)}) collective-permute-start(f32[128,128]{1,0:T(8,128)S(1)} %add.51), channel_id=1, source_target_pairs={{0,4},{1,9},{2,6},{3,11},{4,0},{5,13},{6,2},{7,15},{8,12},{9,1},{1... | collective-permute-start | bytes 196616 | tf_op jit(solution)/shard_map/ppermute | solution.py:467
  107.0 5.2 %collective-permute-start.36 = (f32[128,128]{1,0:T(8,128)S(1)}, f32[128,128]{1,0:T(8,128)S(1)}, u32[]{:S(2)}, u32[]{:S(2)}) collective-permute-start(f32[128,128]{1,0:T(8,128)S(1)} %add.52), channel_id=1, source_target_pairs={{0,8},{1,3},{2,10},{3,1},{4,12},{5,7},{6,14},{7,5},{8,0},{9,11},{1... | collective-permute-start | bytes 196616 | tf_op jit(solution)/shard_map/ppermute | solution.py:467
  112.2 1.3 %collective-permute-start.37 = (f32[128,128]{1,0:T(8,128)S(1)}, f32[128,128]{1,0:T(8,128)S(1)}, u32[]{:S(2)}, u32[]{:S(2)}) collective-permute-start(f32[128,128]{1,0:T(8,128)S(1)} %add.53), channel_id=1, source_target_pairs={{0,1},{1,0},{2,3},{3,2},{4,5},{5,4},{6,7},{7,6},{8,9},{9,8},{10,11... | collective-permute-start | bytes 196616 | tf_op jit(solution)/shard_map/ppermute | solution.py:457
  (9 other events, 15.1 us)

commit v6 on v5

--- a/solution.py
+++ b/solution.py
@@ -257,8 +257,10 @@
             if g == home:
                 groups[g] = panel
                 continue
-            for m in range(8):
-                groups[g] = groups[g] - columns[g][m] * panel[m : m + 1, :]
+            terms = [columns[g][m] * panel[m : m + 1, :] for m in range(8)]
+            while len(terms) > 1:
+                terms = [x + y for x, y in zip(terms[::2], terms[1::2])]
+            groups[g] = groups[g] - terms[0]
     return jnp.concatenate(groups, axis=0)[:, SSTEP * RHS :], pivots
 
 

time: 124 us -> 124 us (level)
  no operation moved by 1% of the time
where the time goes in v6:
time: 124 us
  starting transfers between devices  64 us (52%)
  Pallas kernels  33.1 us (27%)
  waiting for transfers between devices  23.2 us (19%)
    ppermute x14, starting transfers between devices, chip(): return lax.ppermute(value, AXES, chip_pairs)  42.8 us
    ppermute x6, waiting for transfers between devices, total(): value = value + lax.ppermute(value, AXES, pairs)  15.8 us
    ppermute x6, starting transfers between devices, total(): value = value + lax.ppermute(value, AXES, pairs)  15.6 us
    pallas_call x1, Pallas kernels, shards(): x, r, repeats = finish(*sums, *stacked(fields), x, doubt, first_r, first_x)  8.31 us
    ppermute x14, waiting for transfers between devices, chip(): return lax.ppermute(value, AXES, chip_pairs)  7.42 us
    pallas_call x1, Pallas kernels, shards(): mix_high, mix_low, to_chip, doubt = mix(lists, *sums, *parts)  6.65 us
    ppermute x8, starting transfers between devices, link(): return lax.ppermute(value, AXES, link_pairs)  5.67 us
    pallas_call x6, Pallas kernels, shards(): power(link_table, kept, link_rows, blocks, mine, link(mine))  4.76 us
  transfers between devices with their start and end apart: 28, of which 16 were waited for; matrix products, arithmetic and copies ran while one was open for 0% of the time, Pallas kernels for 6%

profile of v6, /device:TPU:0, one launch (start us, length us, event | category | flops | bytes accessed | tf_op | source)
XLA Modules:
  0.0 123.6 jit_solution(4739534046448234552)
XLA Ops:
  0.6 1.4 %prepare.1 = (f32[16,64,32]{2,1,0:T(8,128)S(1)}, bf16[16,64,384]{2,1,0:T(8,128)(2,1)S(1)}, bf16[1,64,128]{2,1,0:T(8,128)(2,1)S(1)}, bf16[1,64,128]{2,1,0:T(8,128)(2,1)S(1)}) custom-call(s32[1,2,4]{2,1,0:T(2,128)} %send_lists.1, f32[16,2048]{1,0:T(8,128)} %guess.1, bf16[16,64,384]{2,1,0:T(8,128)(2,1)} %couple.1), custom_call_target="tpu_custom_call" | custom-call | tf_op jit(solution)/shard_map/prepare/pallas_call | solution.py:521
  5.4 5.1 %collective-permute-start.14 = (bf16[1,64,128]{2,1,0:T(8,128)(2,1)S(1)}, bf16[1,64,128]{2,1,0:T(8,128)(2,1)S(1)}, u32[]{:S(2)}, u32[]{:S(2)}) collective-permute-start(bf16[1,64,128]{2,1,0:T(8,128)(2,1)S(1)} %get-tuple-element.124), channel_id=1, source_target_pairs={{0,1},{1,0},{2,3},{3,2},{4,5},{5,4},{6,7},{7,6},{8,9},{9,8},{10,11... | collective-permute-start | bytes 49160 | tf_op jit(solution)/shard_map/ppermute | solution.py:459
  13.0 6.4 %collective-permute-start.16 = (bf16[5,64,128]{2,1,0:T(8,128)(2,1)S(1)}, bf16[5,64,128]{2,1,0:T(8,128)(2,1)S(1)}, u32[]{:S(2)}, u32[]{:S(2)}) collective-permute-start(bf16[5,64,128]{2,1,0:T(8,128)(2,1)S(1)} %get-tuple-element.126.mine), channel_id=1, source_target_pairs={{0,1},{1,0},{2,3},{3,2},{4,5},{5,4},{6,7},{7,6},{8,9},{9,8},{10,11... | collective-permute-start | bytes 245768 | tf_op jit(solution)/shard_map/ppermute | solution.py:459
  22.5 6.4 %collective-permute-start.18 = (bf16[5,64,128]{2,1,0:T(8,128)(2,1)S(1)}, bf16[5,64,128]{2,1,0:T(8,128)(2,1)S(1)}, u32[]{:S(2)}, u32[]{:S(2)}) collective-permute-start(bf16[5,64,128]{2,1,0:T(8,128)(2,1)S(1)} %get-tuple-element.130.mine), channel_id=1, source_target_pairs={{0,1},{1,0},{2,3},{3,2},{4,5},{5,4},{6,7},{7,6},{8,9},{9,8},{10,11... | collective-permute-start | bytes 245768 | tf_op jit(solution)/shard_map/ppermute | solution.py:459
  32.3 6.2 %collective-permute-start.20 = (bf16[5,64,128]{2,1,0:T(8,128)(2,1)S(1)}, bf16[5,64,128]{2,1,0:T(8,128)(2,1)S(1)}, u32[]{:S(2)}, u32[]{:S(2)}) collective-permute-start(bf16[5,64,128]{2,1,0:T(8,128)(2,1)S(1)} %get-tuple-element.134.mine), channel_id=1, source_target_pairs={{0,1},{1,0},{2,3},{3,2},{4,5},{5,4},{6,7},{7,6},{8,9},{9,8},{10,11... | collective-permute-start | bytes 245768 | tf_op jit(solution)/shard_map/ppermute | solution.py:459
  39.6 1.4 %power_and_gram.2 = (f32[16,64,32]{2,1,0:T(8,128)S(1)}, f32[128,128]{1,0:T(8,128)S(1)}, f32[128,128]{1,0:T(8,128)S(1)}) custom-call(s32[20,128]{1,0:T(8,128)S(1)} %table.2, bf16[16,64,384]{2,1,0:T(8,128)(2,1)S(1)} %get-tuple-element.118.couple, bf16[16,64,32]{2,1,0:T(8,128)(2,1)S(1)} %get-tuple-element.133.blocks, ...), custom_call_target="tpu_custom_call" | custom-call | tf_op jit(solution)/shard_map/power_and_gram/pallas_call | solution.py:545
  42.4 2.9 %collective-permute-start.22 = (f32[128,128]{1,0:T(8,128)S(1)}, f32[128,128]{1,0:T(8,128)S(1)}, u32[]{:S(2)}, u32[]{:S(2)}) collective-permute-start(f32[128,128]{1,0:T(8,128)S(1)} %select_add_fusion.1), channel_id=1, source_target_pairs={{0,2},{1,5},{2,0},{3,7},{4,6},{5,1},{6,4},{7,3},{8,10},{9,13},{10,... | collective-permute-start | bytes 196616 | tf_op jit(solution)/shard_map/ppermute | solution.py:469
  45.3 2.2 %collective-permute-done.22 = f32[128,128]{1,0:T(8,128)S(1)} collective-permute-done((f32[128,128]{1,0:T(8,128)S(1)}, f32[128,128]{1,0:T(8,128)S(1)}, u32[]{:S(2)}, u32[]{:S(2)}) %collective-permute-start.22) | collective-permute-done | bytes 65568 | tf_op jit(solution)/shard_map/ppermute | solution.py:469
  47.6 2.1 %collective-permute-start.23 = (f32[128,128]{1,0:T(8,128)S(1)}, f32[128,128]{1,0:T(8,128)S(1)}, u32[]{:S(2)}, u32[]{:S(2)}) collective-permute-start(f32[128,128]{1,0:T(8,128)S(1)} %add.47), channel_id=1, source_target_pairs={{0,4},{1,9},{2,6},{3,11},{4,0},{5,13},{6,2},{7,15},{8,12},{9,1},{1... | collective-permute-start | bytes 196616 | tf_op jit(solution)/shard_map/ppermute | solution.py:469
  49.7 2.8 %collective-permute-done.23 = f32[128,128]{1,0:T(8,128)S(1)} collective-permute-done((f32[128,128]{1,0:T(8,128)S(1)}, f32[128,128]{1,0:T(8,128)S(1)}, u32[]{:S(2)}, u32[]{:S(2)}) %collective-permute-start.23) | collective-permute-done | bytes 65568 | tf_op jit(solution)/shard_map/ppermute | solution.py:469
  52.5 2.6 %collective-permute-start.24 = (f32[128,128]{1,0:T(8,128)S(1)}, f32[128,128]{1,0:T(8,128)S(1)}, u32[]{:S(2)}, u32[]{:S(2)}) collective-permute-start(f32[128,128]{1,0:T(8,128)S(1)} %add.48), channel_id=1, source_target_pairs={{0,8},{1,3},{2,10},{3,1},{4,12},{5,7},{6,14},{7,5},{8,0},{9,11},{1... | collective-permute-start | bytes 196616 | tf_op jit(solution)/shard_map/ppermute | solution.py:469
  55.1 2.7 %collective-permute-done.24 = f32[128,128]{1,0:T(8,128)S(1)} collective-permute-done((f32[128,128]{1,0:T(8,128)S(1)}, f32[128,128]{1,0:T(8,128)S(1)}, u32[]{:S(2)}, u32[]{:S(2)}) %collective-permute-start.24) | collective-permute-done | bytes 65568 | tf_op jit(solution)/shard_map/ppermute | solution.py:469
  59.1 6.6 %solve.1 = (bf16[256,64]{1,0:T(8,128)(2,1)S(1)}, bf16[256,64]{1,0:T(8,128)(2,1)S(1)}, bf16[1,64,128]{2,1,0:T(8,128)(2,1)S(1)}, f32[8,128]{1,0:T(8,128)S(1)}) custom-call(s32[1,8]{1,0:T(1,128)S(1)} %reshape.22.lists, f32[128,128]{1,0:T(8,128)S(1)} %get-tuple-element.204.left, f32[128,128]{1,0:T(8,128)S(1)} %get-tuple-element.203.right, ...), custom_call_target="tpu_custom_call" | custom-call | tf_op jit(solution)/shard_map/solve/pallas_call | solution.py:552
  68.4 5.3 %collective-permute-start.28 = (bf16[5,64,128]{2,1,0:T(8,128)(2,1)S(1)}, bf16[5,64,128]{2,1,0:T(8,128)(2,1)S(1)}, u32[]{:S(2)}, u32[]{:S(2)}) collective-permute-start(bf16[5,64,128]{2,1,0:T(8,128)(2,1)S(1)} %get-tuple-element.156.mine), channel_id=1, source_target_pairs={{0,1},{1,0},{2,3},{3,2},{4,5},{5,4},{6,7},{7,6},{8,9},{9,8},{10,11... | collective-permute-start | bytes 245768 | tf_op jit(solution)/shard_map/ppermute | solution.py:459
  77.2 5.6 %collective-permute-start.30 = (bf16[5,64,128]{2,1,0:T(8,128)(2,1)S(1)}, bf16[5,64,128]{2,1,0:T(8,128)(2,1)S(1)}, u32[]{:S(2)}, u32[]{:S(2)}) collective-permute-start(bf16[5,64,128]{2,1,0:T(8,128)(2,1)S(1)} %get-tuple-element.160.mine), channel_id=1, source_target_pairs={{0,1},{1,0},{2,3},{3,2},{4,5},{5,4},{6,7},{7,6},{8,9},{9,8},{10,11... | collective-permute-start | bytes 245768 | tf_op jit(solution)/shard_map/ppermute | solution.py:459
  86.0 6.4 %collective-permute-start.32 = (bf16[5,64,128]{2,1,0:T(8,128)(2,1)S(1)}, bf16[5,64,128]{2,1,0:T(8,128)(2,1)S(1)}, u32[]{:S(2)}, u32[]{:S(2)}) collective-permute-start(bf16[5,64,128]{2,1,0:T(8,128)(2,1)S(1)} %get-tuple-element.164.mine), channel_id=1, source_target_pairs={{0,1},{1,0},{2,3},{3,2},{4,5},{5,4},{6,7},{7,6},{8,9},{9,8},{10,11... | collective-permute-start | bytes 245768 | tf_op jit(solution)/shard_map/ppermute | solution.py:459
  93.5 1.4 %power_and_gram.3 = (f32[16,64,32]{2,1,0:T(8,128)S(1)}, f32[128,128]{1,0:T(8,128)S(1)}, f32[128,128]{1,0:T(8,128)S(1)}) custom-call(s32[20,128]{1,0:T(8,128)S(1)} %table.2, bf16[16,64,384]{2,1,0:T(8,128)(2,1)S(1)} %get-tuple-element.118.couple, bf16[16,64,32]{2,1,0:T(8,128)(2,1)S(1)} %get-tuple-element.163.blocks, ...), custom_call_target="tpu_custom_call" | custom-call | tf_op jit(solution)/shard_map/power_and_gram/pallas_call | solution.py:545
  96.3 2.9 %collective-permute-start.34 = (f32[128,128]{1,0:T(8,128)S(1)}, f32[128,128]{1,0:T(8,128)S(1)}, u32[]{:S(2)}, u32[]{:S(2)}) collective-permute-start(f32[128,128]{1,0:T(8,128)S(1)} %select_add_fusion), channel_id=1, source_target_pairs={{0,2},{1,5},{2,0},{3,7},{4,6},{5,1},{6,4},{7,3},{8,10},{9,13},{10,... | collective-permute-start | bytes 196616 | tf_op jit(solution)/shard_map/ppermute | solution.py:469
  99.2 2.2 %collective-permute-done.34 = f32[128,128]{1,0:T(8,128)S(1)} collective-permute-done((f32[128,128]{1,0:T(8,128)S(1)}, f32[128,128]{1,0:T(8,128)S(1)}, u32[]{:S(2)}, u32[]{:S(2)}) %collective-permute-start.34) | collective-permute-done | bytes 65568 | tf_op jit(solution)/shard_map/ppermute | solution.py:469
  101.5 2.7 %collective-permute-start.35 = (f32[128,128]{1,0:T(8,128)S(1)}, f32[128,128]{1,0:T(8,128)S(1)}, u32[]{:S(2)}, u32[]{:S(2)}) collective-permute-start(f32[128,128]{1,0:T(8,128)S(1)} %add.51), channel_id=1, source_target_pairs={{0,4},{1,9},{2,6},{3,11},{4,0},{5,13},{6,2},{7,15},{8,12},{9,1},{1... | collective-permute-start | bytes 196616 | tf_op jit(solution)/shard_map/ppermute | solution.py:469
  104.1 2.9 %collective-permute-done.35 = f32[128,128]{1,0:T(8,128)S(1)} collective-permute-done((f32[128,128]{1,0:T(8,128)S(1)}, f32[128,128]{1,0:T(8,128)S(1)}, u32[]{:S(2)}, u32[]{:S(2)}) %collective-permute-start.35) | collective-permute-done | bytes 65568 | tf_op jit(solution)/shard_map/ppermute | solution.py:469
  107.1 2.3 %collective-permute-start.36 = (f32[128,128]{1,0:T(8,128)S(1)}, f32[128,128]{1,0:T(8,128)S(1)}, u32[]{:S(2)}, u32[]{:S(2)}) collective-permute-start(f32[128,128]{1,0:T(8,128)S(1)} %add.52), channel_id=1, source_target_pairs={{0,8},{1,3},{2,10},{3,1},{4,12},{5,7},{6,14},{7,5},{8,0},{9,11},{1... | collective-permute-start | bytes 196616 | tf_op jit(solution)/shard_map/ppermute | solution.py:469
  109.4 2.9 %collective-permute-done.36 = f32[128,128]{1,0:T(8,128)S(1)} collective-permute-done((f32[128,128]{1,0:T(8,128)S(1)}, f32[128,128]{1,0:T(8,128)S(1)}, u32[]{:S(2)}, u32[]{:S(2)}) %collective-permute-start.36) | collective-permute-done | bytes 65568 | tf_op jit(solution)/shard_map/ppermute | solution.py:469
  113.7 8.3 %solve_finish.1 = (f32[16,2048]{1,0:T(8,128)}, f32[16,2048]{1,0:T(8,128)S(1)}, s32[1]{0:T(128)}) custom-call(f32[128,128]{1,0:T(8,128)S(1)} %get-tuple-element.202.left, f32[128,128]{1,0:T(8,128)S(1)} %get-tuple-element.201.right, bf16[1024,256]{1,0:T(8,128)(2,1)S(1)} %get-tuple-element.178.high, bf16[1024,256]{1,0:T(8,128)(2,1)S(1)} %get-tuple-element.179.low, ...), custom_call_target="tpu_custom_call" | custom-call | tf_op jit(solution)/shard_map/solve_finish/pallas_call | solution.py:555
  (93 shorter events, 30.6 us)
Async XLA Ops:
  2.1 2.5 %collective-permute-start.10 = (bf16[1,64,128]{2,1,0:T(8,128)(2,1)S(1)}, bf16[1,64,128]{2,1,0:T(8,128)(2,1)S(1)}, u32[]{:S(2)}, u32[]{:S(2)}) collective-permute-start(bf16[1,64,128]{2,1,0:T(8,128)(2,1)S(1)} %get-tuple-element.206), channel_id=1, source_target_pairs={{0,1},{1,0},{2,3},{3,2},{4,5},{5,4},{6,7},{7,6},{8,9},{9,8},{10,11... | collective-permute-start | bytes 49160 | tf_op jit(solution)/shard_map/ppermute | solution.py:459
  2.6 2.0 %collective-permute-start.11 = (bf16[1,64,128]{2,1,0:T(8,128)(2,1)S(1)}, bf16[1,64,128]{2,1,0:T(8,128)(2,1)S(1)}, u32[]{:S(2)}, u32[]{:S(2)}) collective-permute-start(bf16[1,64,128]{2,1,0:T(8,128)(2,1)S(1)} %get-tuple-element.205.after), channel_id=1, source_target_pairs={{1,2},{2,1},{3,4},{4,3},{5,6},{6,5},{7,8},{8,7},{9,10},{10,9},{11,... | collective-permute-start | bytes 49160 | tf_op jit(solution)/shard_map/ppermute | solution.py:462
  3.7 8.4 %collective-permute-start.13 = (bf16[4,80,384]{2,1,0:T(8,128)(2,1)S(1)}, bf16[4,80,384]{2,1,0:T(8,128)(2,1)S(1)}, u32[]{:S(2)}, u32[]{:S(2)}) collective-permute-start(bf16[4,80,384]{2,1,0:T(8,128)(2,1)S(1)} %rows.3), channel_id=1, source_target_pairs={{1,2},{2,1},{3,4},{4,3},{5,6},{6,5},{7,8},{8,7},{9,10},{10,9},{11,... | collective-permute-start | bytes 737288 | tf_op jit(solution)/shard_map/ppermute | solution.py:462
  5.4 6.0 %collective-permute-start.14 = (bf16[1,64,128]{2,1,0:T(8,128)(2,1)S(1)}, bf16[1,64,128]{2,1,0:T(8,128)(2,1)S(1)}, u32[]{:S(2)}, u32[]{:S(2)}) collective-permute-start(bf16[1,64,128]{2,1,0:T(8,128)(2,1)S(1)} %get-tuple-element.124), channel_id=1, source_target_pairs={{0,1},{1,0},{2,3},{3,2},{4,5},{5,4},{6,7},{7,6},{8,9},{9,8},{10,11... | collective-permute-start | bytes 49160 | tf_op jit(solution)/shard_map/ppermute | solution.py:459
  10.6 8.7 %collective-permute-start.12 = (bf16[4,80,384]{2,1,0:T(8,128)(2,1)S(1)}, bf16[4,80,384]{2,1,0:T(8,128)(2,1)S(1)}, u32[]{:S(2)}, u32[]{:S(2)}) collective-permute-start(bf16[4,80,384]{2,1,0:T(8,128)(2,1)S(1)} %rows.2), channel_id=1, source_target_pairs={{0,1},{1,0},{2,3},{3,2},{4,5},{5,4},{6,7},{7,6},{8,9},{9,8},{10,11... | collective-permute-start | bytes 737288 | tf_op jit(solution)/shard_map/ppermute | solution.py:459
  13.0 7.3 %collective-permute-start.16 = (bf16[5,64,128]{2,1,0:T(8,128)(2,1)S(1)}, bf16[5,64,128]{2,1,0:T(8,128)(2,1)S(1)}, u32[]{:S(2)}, u32[]{:S(2)}) collective-permute-start(bf16[5,64,128]{2,1,0:T(8,128)(2,1)S(1)} %get-tuple-element.126.mine), channel_id=1, source_target_pairs={{0,1},{1,0},{2,3},{3,2},{4,5},{5,4},{6,7},{7,6},{8,9},{9,8},{10,11... | collective-permute-start | bytes 245768 | tf_op jit(solution)/shard_map/ppermute | solution.py:459
  22.5 7.3 %collective-permute-start.18 = (bf16[5,64,128]{2,1,0:T(8,128)(2,1)S(1)}, bf16[5,64,128]{2,1,0:T(8,128)(2,1)S(1)}, u32[]{:S(2)}, u32[]{:S(2)}) collective-permute-start(bf16[5,64,128]{2,1,0:T(8,128)(2,1)S(1)} %get-tuple-element.130.mine), channel_id=1, source_target_pairs={{0,1},{1,0},{2,3},{3,2},{4,5},{5,4},{6,7},{7,6},{8,9},{9,8},{10,11... | collective-permute-start | bytes 245768 | tf_op jit(solution)/shard_map/ppermute | solution.py:459
  30.6 0.8 collective-permute-start.19
  32.3 7.4 %collective-permute-start.20 = (bf16[5,64,128]{2,1,0:T(8,128)(2,1)S(1)}, bf16[5,64,128]{2,1,0:T(8,128)(2,1)S(1)}, u32[]{:S(2)}, u32[]{:S(2)}) collective-permute-start(bf16[5,64,128]{2,1,0:T(8,128)(2,1)S(1)} %get-tuple-element.134.mine), channel_id=1, source_target_pairs={{0,1},{1,0},{2,3},{3,2},{4,5},{5,4},{6,7},{7,6},{8,9},{9,8},{10,11... | collective-permute-start | bytes 245768 | tf_op jit(solution)/shard_map/ppermute | solution.py:459
  41.0 1.3 %collective-permute-start.21 = (f32[128,128]{1,0:T(8,128)S(1)}, f32[128,128]{1,0:T(8,128)S(1)}, u32[]{:S(2)}, u32[]{:S(2)}) collective-permute-start(f32[128,128]{1,0:T(8,128)S(1)} %broadcast_select_fusion.5), channel_id=1, source_target_pairs={{0,1},{1,0},{2,3},{3,2},{4,5},{5,4},{6,7},{7,6},{8,9},{9,8},{10,11... | collective-permute-start | bytes 196616 | tf_op jit(solution)/shard_map/ppermute | solution.py:459
  42.4 5.2 %collective-permute-start.22 = (f32[128,128]{1,0:T(8,128)S(1)}, f32[128,128]{1,0:T(8,128)S(1)}, u32[]{:S(2)}, u32[]{:S(2)}) collective-permute-start(f32[128,128]{1,0:T(8,128)S(1)} %select_add_fusion.1), channel_id=1, source_target_pairs={{0,2},{1,5},{2,0},{3,7},{4,6},{5,1},{6,4},{7,3},{8,10},{9,13},{10,... | collective-permute-start | bytes 196616 | tf_op jit(solution)/shard_map/ppermute | solution.py:469
  47.6 4.9 %collective-permute-start.23 = (f32[128,128]{1,0:T(8,128)S(1)}, f32[128,128]{1,0:T(8,128)S(1)}, u32[]{:S(2)}, u32[]{:S(2)}) collective-permute-start(f32[128,128]{1,0:T(8,128)S(1)} %add.47), channel_id=1, source_target_pairs={{0,4},{1,9},{2,6},{3,11},{4,0},{5,13},{6,2},{7,15},{8,12},{9,1},{1... | collective-permute-start | bytes 196616 | tf_op jit(solution)/shard_map/ppermute | solution.py:469
  52.5 5.2 %collective-permute-start.24 = (f32[128,128]{1,0:T(8,128)S(1)}, f32[128,128]{1,0:T(8,128)S(1)}, u32[]{:S(2)}, u32[]{:S(2)}) collective-permute-start(f32[128,128]{1,0:T(8,128)S(1)} %add.48), channel_id=1, source_target_pairs={{0,8},{1,3},{2,10},{3,1},{4,12},{5,7},{6,14},{7,5},{8,0},{9,11},{1... | collective-permute-start | bytes 196616 | tf_op jit(solution)/shard_map/ppermute | solution.py:469
  57.7 1.3 %collective-permute-start.25 = (f32[128,128]{1,0:T(8,128)S(1)}, f32[128,128]{1,0:T(8,128)S(1)}, u32[]{:S(2)}, u32[]{:S(2)}) collective-permute-start(f32[128,128]{1,0:T(8,128)S(1)} %add.49), channel_id=1, source_target_pairs={{0,1},{1,0},{2,3},{3,2},{4,5},{5,4},{6,7},{7,6},{8,9},{9,8},{10,11... | collective-permute-start | bytes 196616 | tf_op jit(solution)/shard_map/ppermute | solution.py:459
  65.7 1.2 %collective-permute-start.26 = (bf16[1,64,128]{2,1,0:T(8,128)(2,1)S(1)}, bf16[1,64,128]{2,1,0:T(8,128)(2,1)S(1)}, u32[]{:S(2)}, u32[]{:S(2)}) collective-permute-start(bf16[1,64,128]{2,1,0:T(8,128)(2,1)S(1)} %get-tuple-element.154), channel_id=1, source_target_pairs={{0,1},{1,0},{2,3},{3,2},{4,5},{5,4},{6,7},{7,6},{8,9},{9,8},{10,11... | collective-permute-start | bytes 49160 | tf_op jit(solution)/shard_map/ppermute | solution.py:459
  68.4 6.3 %collective-permute-start.28 = (bf16[5,64,128]{2,1,0:T(8,128)(2,1)S(1)}, bf16[5,64,128]{2,1,0:T(8,128)(2,1)S(1)}, u32[]{:S(2)}, u32[]{:S(2)}) collective-permute-start(bf16[5,64,128]{2,1,0:T(8,128)(2,1)S(1)} %get-tuple-element.156.mine), channel_id=1, source_target_pairs={{0,1},{1,0},{2,3},{3,2},{4,5},{5,4},{6,7},{7,6},{8,9},{9,8},{10,11... | collective-permute-start | bytes 245768 | tf_op jit(solution)/shard_map/ppermute | solution.py:459
  75.5 0.9 collective-permute-start.29
  77.2 6.6 %collective-permute-start.30 = (bf16[5,64,128]{2,1,0:T(8,128)(2,1)S(1)}, bf16[5,64,128]{2,1,0:T(8,128)(2,1)S(1)}, u32[]{:S(2)}, u32[]{:S(2)}) collective-permute-start(bf16[5,64,128]{2,1,0:T(8,128)(2,1)S(1)} %get-tuple-element.160.mine), channel_id=1, source_target_pairs={{0,1},{1,0},{2,3},{3,2},{4,5},{5,4},{6,7},{7,6},{8,9},{9,8},{10,11... | collective-permute-start | bytes 245768 | tf_op jit(solution)/shard_map/ppermute | solution.py:459
  86.0 7.5 %collective-permute-start.32 = (bf16[5,64,128]{2,1,0:T(8,128)(2,1)S(1)}, bf16[5,64,128]{2,1,0:T(8,128)(2,1)S(1)}, u32[]{:S(2)}, u32[]{:S(2)}) collective-permute-start(bf16[5,64,128]{2,1,0:T(8,128)(2,1)S(1)} %get-tuple-element.164.mine), channel_id=1, source_target_pairs={{0,1},{1,0},{2,3},{3,2},{4,5},{5,4},{6,7},{7,6},{8,9},{9,8},{10,11... | collective-permute-start | bytes 245768 | tf_op jit(solution)/shard_map/ppermute | solution.py:459
  94.9 1.3 %collective-permute-start.33 = (f32[128,128]{1,0:T(8,128)S(1)}, f32[128,128]{1,0:T(8,128)S(1)}, u32[]{:S(2)}, u32[]{:S(2)}) collective-permute-start(f32[128,128]{1,0:T(8,128)S(1)} %broadcast_select_fusion.2), channel_id=1, source_target_pairs={{0,1},{1,0},{2,3},{3,2},{4,5},{5,4},{6,7},{7,6},{8,9},{9,8},{10,11... | collective-permute-start | bytes 196616 | tf_op jit(solution)/shard_map/ppermute | solution.py:459
  96.3 5.2 %collective-permute-start.34 = (f32[128,128]{1,0:T(8,128)S(1)}, f32[128,128]{1,0:T(8,128)S(1)}, u32[]{:S(2)}, u32[]{:S(2)}) collective-permute-start(f32[128,128]{1,0:T(8,128)S(1)} %select_add_fusion), channel_id=1, source_target_pairs={{0,2},{1,5},{2,0},{3,7},{4,6},{5,1},{6,4},{7,3},{8,10},{9,13},{10,... | collective-permute-start | bytes 196616 | tf_op jit(solution)/shard_map/ppermute | solution.py:469
  101.5 5.6 %collective-permute-start.35 = (f32[128,128]{1,0:T(8,128)S(1)}, f32[128,128]{1,0:T(8,128)S(1)}, u32[]{:S(2)}, u32[]{:S(2)}) collective-permute-start(f32[128,128]{1,0:T(8,128)S(1)} %add.51), channel_id=1, source_target_pairs={{0,4},{1,9},{2,6},{3,11},{4,0},{5,13},{6,2},{7,15},{8,12},{9,1},{1... | collective-permute-start | bytes 196616 | tf_op jit(solution)/shard_map/ppermute | solution.py:469
  107.1 5.2 %collective-permute-start.36 = (f32[128,128]{1,0:T(8,128)S(1)}, f32[128,128]{1,0:T(8,128)S(1)}, u32[]{:S(2)}, u32[]{:S(2)}) collective-permute-start(f32[128,128]{1,0:T(8,128)S(1)} %add.52), channel_id=1, source_target_pairs={{0,8},{1,3},{2,10},{3,1},{4,12},{5,7},{6,14},{7,5},{8,0},{9,11},{1... | collective-permute-start | bytes 196616 | tf_op jit(solution)/shard_map/ppermute | solution.py:469
  112.3 1.3 %collective-permute-start.37 = (f32[128,128]{1,0:T(8,128)S(1)}, f32[128,128]{1,0:T(8,128)S(1)}, u32[]{:S(2)}, u32[]{:S(2)}) collective-permute-start(f32[128,128]{1,0:T(8,128)S(1)} %add.53), channel_id=1, source_target_pairs={{0,1},{1,0},{2,3},{3,2},{4,5},{5,4},{6,7},{7,6},{8,9},{9,8},{10,11... | collective-permute-start | bytes 196616 | tf_op jit(solution)/shard_map/ppermute | solution.py:459
  (9 other events, 15.1 us)
